TPU v7x, 512 devices: a whole 4x4x16 slice. The times are simulated.
512 devices in a mesh: row: 32 (over x, y, core), col: 16 (over z).
Axes of the slice: x: 4, y: 4, z: 16, core: 2. Of those that a mesh axis runs over, the one named last changes fastest.
Arguments:
- inputs: bfloat16 [2048, 8192], P('row', 'col'), may hold values from -6 to 6
- gate_pre: bfloat16 [2048, 16384], P('col', 'row'), may hold values from -8 to 8
- up_pre: bfloat16 [2048, 16384], P('col', 'row'), may hold values from -6 to 6
- w_gate: bfloat16 [8192, 16384], P('col', 'row'), may hold values from -0.0625 to 0.0625
- w_up: bfloat16 [8192, 16384], P('col', 'row'), may hold values from -0.0625 to 0.0625
- w_down: bfloat16 [16384, 8192], P('row', 'col'), may hold values from -0.046875 to 0.046875
- grad_out: bfloat16 [2048, 8192], P('row', 'col'), may hold values from -2 to 2
Outputs:
- input_grad: bfloat16 [2048, 8192], P('row', 'col')
- w_gate_grad: bfloat16 [8192, 16384], P('col', 'row')
- w_up_grad: bfloat16 [8192, 16384], P('col', 'row')
- w_down_grad: bfloat16 [16384, 8192], P('row', 'col')
All inputs are finite; a program needn't handle non-finite values.
Results may differ from a plain program's by a relative error of at most 0.03.
Values may be sent and summed in bfloat16 or wider, within the bound.
No kernel may reach another device: no remote copies, remote signals or barrier semaphores. Data moves between devices by JAX's collectives and lax.ppermute only.
A program may use at most 64 MiB of HBM per device.

v0:
```python
import jax
import jax.numpy as jnp
from jax import lax
from jax.sharding import PartitionSpec as P


def local_step(down_grad, gate_pre, up_pre):
    gate_val = gate_pre.astype(jnp.float32)
    up_val = up_pre.astype(jnp.float32)
    sigma = jax.nn.sigmoid(gate_val)
    active = gate_val * sigma
    hidden = (active * up_val).astype(jnp.bfloat16)
    gate_grad = (down_grad * up_val * sigma * (1.0 + gate_val * (1.0 - sigma))).astype(jnp.bfloat16)
    up_grad = (down_grad * active).astype(jnp.bfloat16)
    return (hidden, gate_grad, up_grad)


def local(inputs, gate_pre, up_pre, w_gate, w_up, w_down, grad_out):
    ndims = (((1,), (1,)), ((), ()))
    tdims = (((0,), (0,)), ((), ()))
    cot_rows = lax.all_gather(grad_out, "row", axis=0, tiled=True)
    down_grad = lax.psum_scatter(
        lax.dot_general(cot_rows, w_down, ndims, preferred_element_type=jnp.float32).astype(
            jnp.bfloat16
        ),
        "col",
        scatter_dimension=0,
        tiled=True,
    ).astype(jnp.float32)
    hidden, gate_grad, up_grad = local_step(down_grad, gate_pre, up_pre)
    hidden_all, gate_all, up_all = (
        lax.all_gather(hidden, "col", axis=0, tiled=True),
        lax.all_gather(gate_grad, "col", axis=0, tiled=True),
        lax.all_gather(up_grad, "col", axis=0, tiled=True),
    )
    input_rows = lax.all_gather(inputs, "row", axis=0, tiled=True)
    w_down_grad = lax.dot_general(
        hidden_all, cot_rows, tdims, preferred_element_type=jnp.float32
    ).astype(jnp.bfloat16)
    w_gate_grad = lax.dot_general(
        input_rows, gate_all, tdims, preferred_element_type=jnp.float32
    ).astype(jnp.bfloat16)
    w_up_grad = lax.dot_general(
        input_rows, up_all, tdims, preferred_element_type=jnp.float32
    ).astype(jnp.bfloat16)
    total = lax.dot_general(gate_all, w_gate, ndims, preferred_element_type=jnp.float32)
    input_grad = lax.psum_scatter(
        (total + lax.dot_general(up_all, w_up, ndims, preferred_element_type=jnp.float32)).astype(
            jnp.bfloat16
        ),
        "row",
        scatter_dimension=0,
        tiled=True,
    )
    return (input_grad, w_gate_grad, w_up_grad, w_down_grad)


def solution(mesh):
    return jax.shard_map(
        local,
        mesh=mesh,
        in_specs=(
            P("row", "col"),
            P("col", "row"),
            P("col", "row"),
            P("col", "row"),
            P("col", "row"),
            P("row", "col"),
            P("row", "col"),
        ),
        out_specs=(P("row", "col"), P("col", "row"), P("col", "row"), P("row", "col")),
        check_vma=False,
    )
```

profile of v0, /device:TPU:1, one launch (start us, length us, event | category | flops | bytes accessed | tf_op | source)
XLA Modules:
  0.0 542.1 jit_solution(2371667237916201741)
XLA Ops:
  7.2 0.7 all-gather.6.cloned.1.call-update
  7.9 0.0 reduce-scatter.3.cloned.1.call-start
  8.0 68.1 %all-gather.6.cloned.1.call-done = bf16[2048,512]{1,0:T(8,128)(2,1)} async-done(((bf16[64,512]{1,0:T(8,128)(2,1)}), bf16[2048,512]{1,0:T(8,128)(2,1)}) %all-gather.6.cloned.1.call-update) | async-done | bytes 2097168 | tf_op jit(solution)/shard_map/all_gather | solution.py:21
  76.1 4.2 convolution_convert_fusion
  80.3 0.0 all-gather.8.cloned.1.call-start
  80.3 62.2 %reduce-scatter.3.cloned.1.call-done = bf16[128,512]{1,0:T(8,128)(2,1)} async-done(((bf16[2048,512]{1,0:T(8,128)(2,1)}), bf16[128,512]{1,0:T(8,128)(2,1)}) %reduce-scatter.3.cloned.1.call-update) | async-done | bytes 131088 | tf_op jit(solution)/shard_map/reduce_scatter | solution.py:22
  142.5 1.8 fusion.6
  144.3 0.0 all-gather.10.cloned.1.call-start
  144.4 0.5 all-gather.10.cloned.1.call-update
  145.0 0.5 all-gather.12.cloned.1.call-update
  145.5 0.5 all-gather.14.cloned.1.call-update
  146.1 0.0 reduce-scatter.5.cloned.1.call-start
  146.1 71.1 %all-gather.8.cloned.1.call-done = bf16[2048,512]{1,0:T(8,128)(2,1)} async-done(((bf16[128,512]{1,0:T(8,128)(2,1)}), bf16[2048,512]{1,0:T(8,128)(2,1)}) %all-gather.8.cloned.1.call-update) | async-done | bytes 2097168 | tf_op jit(solution)/shard_map/all_gather | solution.py:33
  217.2 4.8 fusion.11
  222.0 67.8 %all-gather.10.cloned.1.call-done = bf16[2048,512]{1,0:T(8,128)(2,1)} async-done(((bf16[128,512]{1,0:T(8,128)(2,1)}), bf16[2048,512]{1,0:T(8,128)(2,1)}) %all-gather.10.cloned.1.call-update) | async-done | bytes 2097168 | tf_op jit(solution)/shard_map/all_gather | solution.py:34
  289.8 5.4 %add_convert_fusion = bf16[2048,512]{1,0:T(8,128)(2,1)} fusion(f32[2048,512]{1,0:T(8,128)} %fusion.11, bf16[2048,512]{1,0:T(8,128)(2,1)} %all-gather.10.cloned.1.call-done, bf16[512,512]{1,0:T(8,128)(2,1)S(1)} %copy-done.4), kind=kOutput, calls=%fused_computation | convolution fusion | flops 1075838976 | bytes 8912896 | tf_op jit(solution)/shard_map/dot_general | solution.py:48
  295.3 63.1 %all-gather.12.cloned.1.call-done = bf16[2048,512]{1,0:T(8,128)(2,1)} async-done(((bf16[64,512]{1,0:T(8,128)(2,1)}), bf16[2048,512]{1,0:T(8,128)(2,1)}) %all-gather.12.cloned.1.call-update) | async-done | bytes 2097168 | tf_op jit(solution)/shard_map/all_gather | solution.py:36
  358.4 2.9 fusion
  361.3 1.0 copy.11
  362.3 3.6 fusion.1
  365.9 1.0 copy.12
  366.9 57.0 %all-gather.14.cloned.1.call-done = bf16[2048,512]{1,0:T(8,128)(2,1)} async-done(((bf16[128,512]{1,0:T(8,128)(2,1)}), bf16[2048,512]{1,0:T(8,128)(2,1)}) %all-gather.14.cloned.1.call-update) | async-done | bytes 2097168 | tf_op jit(solution)/shard_map/all_gather | solution.py:32
  423.9 3.7 convolution_convert_fusion.1
  427.6 107.7 %reduce-scatter.5.cloned.1.call-done = bf16[64,512]{1,0:T(8,128)(2,1)} async-done(((bf16[2048,512]{1,0:T(8,128)(2,1)}), bf16[64,512]{1,0:T(8,128)(2,1)}) %reduce-scatter.5.cloned.1.call-update) | async-done | bytes 65552 | tf_op jit(solution)/shard_map/reduce_scatter | solution.py:47
  (20 shorter events, 0.2 us)
Async XLA Ops:
  7.2 68.9 %copy-start = (bf16[512,512]{1,0:T(8,128)(2,1)S(1)}, bf16[512,512]{1,0:T(8,128)(2,1)}, u32[]{:S(2)}) copy-start(bf16[512,512]{1,0:T(8,128)(2,1)} %param.12) | copy-start | bytes 1572868
  7.2 68.9 %all-gather.6.cloned.1.call-start = ((), (), s32[]{:S(2)}) async-start(), calls=%async_computation.2 | async-start | bytes 2162688 | tf_op jit(solution)/shard_map/all_gather | solution.py:21
  7.9 134.6 %reduce-scatter.3.cloned.1.call-start = ((), (), s32[]{:S(2)}) async-start(), calls=%async_computation.3 | async-start | bytes 2228224 | tf_op jit(solution)/shard_map/reduce_scatter | solution.py:22
  80.3 62.3 %copy-start.5 = (bf16[128,512]{1,0:T(8,128)(2,1)S(1)}, bf16[128,512]{1,0:T(8,128)(2,1)}, u32[]{:S(2)}) copy-start(bf16[128,512]{1,0:T(8,128)(2,1)} %param.9) | copy-start | bytes 393220
  80.3 62.3 %copy-start.6 = (bf16[128,512]{1,0:T(8,128)(2,1)S(1)}, bf16[128,512]{1,0:T(8,128)(2,1)}, u32[]{:S(2)}) copy-start(bf16[128,512]{1,0:T(8,128)(2,1)} %param.8) | copy-start | bytes 393220
  80.3 136.9 %copy-start.3 = (bf16[512,512]{1,0:T(8,128)(2,1)S(1)}, bf16[512,512]{1,0:T(8,128)(2,1)}, u32[]{:S(2)}) copy-start(bf16[512,512]{1,0:T(8,128)(2,1)} %param.10) | copy-start | bytes 1572868
  80.3 136.9 %all-gather.8.cloned.1.call-start = ((), (), s32[]{:S(2)}) async-start(), calls=%async_computation.4 | async-start | bytes 2228224 | tf_op jit(solution)/shard_map/all_gather | solution.py:33
  144.3 145.5 %all-gather.10.cloned.1.call-start = ((), (), s32[]{:S(2)}) async-start(), calls=%async_computation.5 | async-start | bytes 2228224 | tf_op jit(solution)/shard_map/all_gather | solution.py:34
  144.9 213.5 %all-gather.12.cloned.1.call-start = ((), (), s32[]{:S(2)}) async-start(), calls=%async_computation.7 | async-start | bytes 2162688 | tf_op jit(solution)/shard_map/all_gather | solution.py:36
  145.5 278.4 %all-gather.14.cloned.1.call-start = ((), (), s32[]{:S(2)}) async-start(), calls=%async_computation.8 | async-start | bytes 2228224 | tf_op jit(solution)/shard_map/all_gather | solution.py:32
  146.1 143.7 %copy-start.4 = (bf16[512,512]{1,0:T(8,128)(2,1)S(1)}, bf16[512,512]{1,0:T(8,128)(2,1)}, u32[]{:S(2)}) copy-start(bf16[512,512]{1,0:T(8,128)(2,1)} %param.11) | copy-start | bytes 1572868
  146.1 389.2 %reduce-scatter.5.cloned.1.call-start = ((), (), s32[]{:S(2)}) async-start(), calls=%async_computation.6 | async-start | bytes 2162688 | tf_op jit(solution)/shard_map/reduce_scatter | solution.py:47
  295.2 63.2 %copy-start.1 = (bf16[2048,512]{1,0:T(8,128)(2,1)S(1)}, bf16[2048,512]{1,0:T(8,128)(2,1)}, u32[]{:S(2)}) copy-start(bf16[2048,512]{1,0:T(8,128)(2,1)} %all-gather.8.cloned.1.call-done) | copy-start | bytes 6291460
  362.3 61.6 %copy-start.2 = (bf16[2048,512]{1,0:T(8,128)(2,1)S(1)}, bf16[2048,512]{1,0:T(8,128)(2,1)}, u32[]{:S(2)}) copy-start(bf16[2048,512]{1,0:T(8,128)(2,1)} %all-gather.6.cloned.1.call-done) | copy-start | bytes 6291460
Sparse Core Ops, SparseCore 0:
  11.1 64.8 all-gather.5
  80.4 62.0 reduce-scatter.2
  145.2 71.9 all-gather.7
  219.7 70.0 all-gather.9
  292.8 65.5 all-gather.11
  360.9 62.9 all-gather.13
  428.9 106.3 reduce-scatter.4
where the time goes:
time: 543 us; the launch traced here: 542 us
  waiting for transfers between devices  499 us (92%)
  matrix products  24.6 us (5%)
  between operations  14.2 us (3%)
    reduce_scatter x1, waiting for transfers between devices, local(): lax.psum_scatter((total + lax.dot_general(up_all, w_up, ndims, preferred_...  108 us
    all_gather x1, waiting for transfers between devices, local(): lax.all_gather(gate_grad, 'col', axis=0, tiled=True)  71.1 us
    all_gather x1, waiting for transfers between devices, local(): cot_rows = lax.all_gather(grad_out, 'row', axis=0, tiled=True)  68.1 us
    all_gather x1, waiting for transfers between devices, local(): lax.all_gather(up_grad, 'col', axis=0, tiled=True)  67.8 us
    all_gather x1, waiting for transfers between devices, local(): input_rows = lax.all_gather(inputs, 'row', axis=0, tiled=True)  63.1 us
    reduce_scatter x1, waiting for transfers between devices, local(): lax.psum_scatter(lax.dot_general(cot_rows, w_down, ndims, preferred_eleme...  62.2 us
    all_gather x1, waiting for transfers between devices, local(): lax.all_gather(hidden, 'col', axis=0, tiled=True)  57 us
  transfers between devices with their start and end apart: 7, of which 7 were waited for; matrix products, arithmetic and copies ran while one was open for 4% of the time, Pallas kernels for 0%

commit v1 on v0

v1 whole, which is shorter than its diff:
```python
import jax
import jax.numpy as jnp
from jax import lax
from jax.sharding import PartitionSpec as P

F32 = jnp.float32
BF16 = jnp.bfloat16
NDIMS = (((1,), (1,)), ((), ()))
TDIMS = (((0,), (0,)), ((), ()))


def local(n_row, n_col, inputs, gate_pre, up_pre, w_gate, w_up, w_down, grad_out):
    chips = n_row // 2
    half = n_col // 2
    core = lax.axis_index("row") % 2
    col = lax.axis_index("col")
    siblings = [(i, i ^ 1) for i in range(n_row)]
    groups = [[2 * i + c for i in range(chips)] for c in range(2)]
    tokens = inputs.shape[0]
    units = w_gate.shape[1]

    def swap(array):
        return lax.ppermute(array, "row", siblings)

    def hop(array, step):
        return lax.ppermute(array, "col", [(i, (i + step) % n_col) for i in range(n_col)])

    def exchange(array):
        return lax.all_to_all(array, "row", 0, 0, axis_index_groups=groups, tiled=True)

    def chunk(array, index):
        return lax.dynamic_slice_in_dim(array, (index % n_col) * tokens, tokens, 0)

    acts = jnp.concatenate((gate_pre, up_pre), axis=1)
    keep = lax.dynamic_slice_in_dim(acts, core * tokens, tokens, 0)
    give = lax.dynamic_slice_in_dim(acts, (1 - core) * tokens, tokens, 0)
    acts = jnp.concatenate((keep, swap(give)), axis=1)
    acts_all = lax.all_gather(acts, "col", axis=0, tiled=True)
    w_down2 = jnp.concatenate((w_down, swap(w_down)), axis=0)

    cot = exchange(jnp.tile(grad_out, (chips, 1)))
    partial = lax.dot_general(cot, w_down2, NDIMS, preferred_element_type=F32).astype(BF16)

    up_sum = chunk(partial, col + half)
    down_sum = chunk(partial, col - half + 1)
    for step in range(1, half + 1):
        up_in = hop(up_sum, 1)
        if step < half:
            down_in = hop(down_sum, -1)
            up_sum = (up_in.astype(F32) + chunk(partial, col + half - step).astype(F32)).astype(BF16)
            if step < half - 1:
                own = chunk(partial, col - half + 1 + step).astype(F32)
                down_sum = (down_in.astype(F32) + own).astype(BF16)
            else:
                down_sum = down_in
    mine = up_in.astype(F32) + down_sum.astype(F32) + chunk(partial, col).astype(F32)
    mine = mine.astype(BF16)

    down_grad = jnp.zeros((n_col * tokens, 2 * units), BF16)

    def put(whole, piece, index):
        return lax.dynamic_update_slice_in_dim(whole, piece, (index % n_col) * tokens, 0)

    down_grad = put(down_grad, mine, col)
    above = below = mine
    for step in range(1, half + 1):
        above = hop(above, 1)
        if step < half:
            below = hop(below, -1)
        down_grad = put(down_grad, above, col - step)
        if step < half:
            down_grad = put(down_grad, below, col + step)

    w_gate2 = jnp.concatenate((w_gate, swap(w_gate)), axis=1)
    w_up2 = jnp.concatenate((w_up, swap(w_up)), axis=1)
    input_rows = lax.all_gather(inputs, "row", axis=0, tiled=True, axis_index_groups=groups)

    parts = [acts_all[:, i * units : (i + 1) * units].astype(F32) for i in range(4)]
    gate_val = jnp.concatenate((parts[0], parts[2]), axis=1)
    up_val = jnp.concatenate((parts[1], parts[3]), axis=1)
    sigma = jax.nn.sigmoid(gate_val)
    active = gate_val * sigma
    hidden = (active * up_val).astype(BF16)
    grads = down_grad.astype(F32)
    gate_grad = (grads * up_val * sigma * (1.0 + gate_val * (1.0 - sigma))).astype(BF16)
    up_grad = (grads * active).astype(BF16)

    wd = lax.dot_general(hidden, cot, TDIMS, preferred_element_type=F32)
    w_down_grad = (wd[:units] + swap(wd[units:].astype(BF16)).astype(F32)).astype(BF16)
    total = lax.dot_general(gate_grad, w_gate2, NDIMS, preferred_element_type=F32)
    total = total + lax.dot_general(up_grad, w_up2, NDIMS, preferred_element_type=F32)
    sums = exchange(total.astype(BF16)).reshape(chips, tokens, -1)
    input_grad = jnp.sum(sums.astype(F32), axis=0).astype(BF16)
    wg = lax.dot_general(input_rows, gate_grad, TDIMS, preferred_element_type=F32)
    wu = lax.dot_general(input_rows, up_grad, TDIMS, preferred_element_type=F32)
    other = swap(jnp.concatenate((wg[:, units:], wu[:, units:]), axis=0).astype(BF16)).astype(F32)
    rows = wg.shape[0]
    w_gate_grad = (wg[:, :units] + other[:rows]).astype(BF16)
    w_up_grad = (wu[:, :units] + other[rows:]).astype(BF16)
    return (input_grad, w_gate_grad, w_up_grad, w_down_grad)


def solution(mesh):
    n_row, n_col = mesh.shape["row"], mesh.shape["col"]

    def step(*arrays):
        return local(n_row, n_col, *arrays)

    return jax.shard_map(
        step,
        mesh=mesh,
        in_specs=(
            P("row", "col"),
            P("col", "row"),
            P("col", "row"),
            P("col", "row"),
            P("col", "row"),
            P("row", "col"),
            P("row", "col"),
        ),
        out_specs=(P("row", "col"), P("col", "row"), P("col", "row"), P("row", "col")),
        check_vma=False,
    )
```

time: 543 us -> 254 us (0.47)
  waiting for transfers between devices: 499 us -> 57 us
  starting transfers between devices: 0.27 us -> 147 us
  matrix products: 24.6 us -> 15.6 us
  other arithmetic: 1.79 us -> 10.2 us
  local copies, waits for them, and re-layouts: 2.04 us -> 7.51 us
    all_gather x5 -> x2, waiting for transfers between devices: 327 us -> 0.04 us  [the longest x1 0.02 us: local(): acts_all = lax.all_gather(acts, 'col', axis=0, tiled=True)]
    reduce_scatter x2 -> x0, waiting for transfers between devices: 170 us -> none  [the longest x1 108 us: local(): lax.psum_scatter((total + lax.dot_general(up_all, w_up, ndims, preferred_...]
    ppermute x0 -> x36, starting transfers between devices: none -> 139 us  [the longest x30 99.8 us: hop(): lax.ppermute(array, 'col', [(i, (i + step) % n_col) for i in range(n_col)])]
    ppermute x0 -> x36, waiting for transfers between devices: none -> 44.2 us  [the longest x30 39.8 us: hop(): lax.ppermute(array, 'col', [(i, (i + step) % n_col) for i in range(n_col)])]
    all_to_all x0 -> x2, waiting for transfers between devices: none -> 12.7 us  [exchange(): lax.all_to_all(array, 'row', 0, 0, axis_index_groups=groups, tiled=True)]
    dot_general x6, matrix products: 24.6 us -> 15.6 us  [the longest x1 3.51 us: local(): lax.dot_general(gate_grad, w_gate2, NDIMS, preferred_element_type=F32)]
    all_to_all x0 -> x2, starting transfers between devices: none -> 8.39 us  [exchange(): lax.all_to_all(array, 'row', 0, 0, axis_index_groups=groups, tiled=True)]
  transfers between devices with their start and end apart: 7 -> 40, of which waited for: 7 -> 24; matrix products, arithmetic and copies ran while one was open for 4% -> 11% of each run, Pallas kernels for 0% -> 0%
where the time goes in v1:
time: 254 us; the launch traced here: 253 us
  starting transfers between devices  147 us (58%)
  waiting for transfers between devices  57 us (22%)
  matrix products  15.6 us (6%)
  between operations  15.3 us (6%)
  other arithmetic  10.2 us (4%)
  local copies, waits for them, and re-layouts  7.51 us (3%)
    ppermute x30, starting transfers between devices, hop(): lax.ppermute(array, 'col', [(i, (i + step) % n_col) for i in range(n_col)])  99.8 us
    ppermute x30, waiting for transfers between devices, hop(): lax.ppermute(array, 'col', [(i, (i + step) % n_col) for i in range(n_col)])  39.8 us
    ppermute x6, starting transfers between devices, swap(): return lax.ppermute(array, 'row', siblings)  38.7 us
    all_to_all x2, waiting for transfers between devices, exchange(): lax.all_to_all(array, 'row', 0, 0, axis_index_groups=groups, tiled=True)  12.7 us
    all_to_all x2, starting transfers between devices, exchange(): lax.all_to_all(array, 'row', 0, 0, axis_index_groups=groups, tiled=True)  8.39 us
  transfers between devices with their start and end apart: 40, of which 24 were waited for; matrix products, arithmetic and copies ran while one was open for 11% of the time, Pallas kernels for 0%

profile of v1, /device:TPU:1, one launch (start us, length us, event | category | flops | bytes accessed | tf_op | source)
XLA Modules:
  0.0 252.5 jit_solution(4084060272961408514)
XLA Ops:
  9.1 8.9 %collective-permute-start.31 = (bf16[64,1024]{1,0:T(8,128)(2,1)S(1)}, bf16[64,1024]{1,0:T(8,128)(2,1)S(1)}, u32[]{:S(2)}, u32[]{:S(2)}) collective-permute-start(bf16[64,1024]{1,0:T(8,128)(2,1)S(1)} %get-tuple-element.29), channel_id=1, source_target_pairs={{0,16},{16,0},{32,48},{48,32},{64,80},{80,64},{96,112},{112,96},{1... | collective-permute-start | bytes 393224 | tf_op jit(solution)/shard_map/ppermute | solution.py:23
  21.7 3.7 %all-to-all-start = ((bf16[16,64,512]{2,1,0:T(8,128)(2,1)}), bf16[16,64,512]{2,1,0:T(8,128)(2,1)S(1)}, u32[]{:S(2)}, u32[]{:S(2)}) async-start(bf16[16,64,512]{2,1,0:T(8,128)(2,1)} %tile.2), calls=%async_computation | async-start | bytes 2097152 | tf_op jit(solution)/shard_map/all_to_all | solution.py:29
  29.2 12.7 %all-to-all-done = bf16[16,64,512]{2,1,0:T(8,128)(2,1)S(1)} async-done(((bf16[16,64,512]{2,1,0:T(8,128)(2,1)}), bf16[16,64,512]{2,1,0:T(8,128)(2,1)S(1)}, u32[]{:S(2)}, u32[]{:S(2)}) %all-to-all-start) | async-done | bytes 1048608 | tf_op jit(solution)/shard_map/all_to_all | solution.py:29
  46.8 7.9 %collective-permute-start.9 = (bf16[64,1024]{1,0:T(8,128)(2,1)S(1)}, bf16[64,1024]{1,0:T(8,128)(2,1)S(1)}, u32[]{:S(2)}, u32[]{:S(2)}) collective-permute-start(bf16[64,1024]{1,0:T(8,128)(2,1)S(1)} %get-tuple-element.27), channel_id=1, source_target_pairs={{0,15},{1,0},{2,1},{3,2},{4,3},{5,4},{6,5},{7,6},{8,7},{9,8},{10,9... | collective-permute-start | bytes 393224 | tf_op jit(solution)/shard_map/ppermute | solution.py:26
  58.3 8.0 %collective-permute-done.2 = bf16[64,1024]{1,0:T(8,128)(2,1)S(1)} collective-permute-done((bf16[64,1024]{1,0:T(8,128)(2,1)S(1)}, bf16[64,1024]{1,0:T(8,128)(2,1)S(1)}, u32[]{:S(2)}, u32[]{:S(2)}) %collective-permute-start.2) | collective-permute-done | bytes 131104 | tf_op jit(solution)/shard_map/ppermute | solution.py:26
  68.3 4.6 %collective-permute-start.10 = (bf16[64,1024]{1,0:T(8,128)(2,1)S(1)}, bf16[64,1024]{1,0:T(8,128)(2,1)S(1)}, u32[]{:S(2)}, u32[]{:S(2)}) collective-permute-start(bf16[64,1024]{1,0:T(8,128)(2,1)S(1)} %get-tuple-element.25), channel_id=1, source_target_pairs={{0,15},{1,0},{2,1},{3,2},{4,3},{5,4},{6,5},{7,6},{8,7},{9,8},{10,9... | collective-permute-start | bytes 393224 | tf_op jit(solution)/shard_map/ppermute | solution.py:26
  78.9 4.6 %collective-permute-start.11 = (bf16[64,1024]{1,0:T(8,128)(2,1)S(1)}, bf16[64,1024]{1,0:T(8,128)(2,1)S(1)}, u32[]{:S(2)}, u32[]{:S(2)}) collective-permute-start(bf16[64,1024]{1,0:T(8,128)(2,1)S(1)} %get-tuple-element.23), channel_id=1, source_target_pairs={{0,15},{1,0},{2,1},{3,2},{4,3},{5,4},{6,5},{7,6},{8,7},{9,8},{10,9... | collective-permute-start | bytes 393224 | tf_op jit(solution)/shard_map/ppermute | solution.py:26
  89.7 5.2 %collective-permute-start.12 = (bf16[64,1024]{1,0:T(8,128)(2,1)S(1)}, bf16[64,1024]{1,0:T(8,128)(2,1)S(1)}, u32[]{:S(2)}, u32[]{:S(2)}) collective-permute-start(bf16[64,1024]{1,0:T(8,128)(2,1)S(1)} %get-tuple-element.21), channel_id=1, source_target_pairs={{0,15},{1,0},{2,1},{3,2},{4,3},{5,4},{6,5},{7,6},{8,7},{9,8},{10,9... | collective-permute-start | bytes 393224 | tf_op jit(solution)/shard_map/ppermute | solution.py:26
  100.7 4.2 %collective-permute-start.13 = (bf16[64,1024]{1,0:T(8,128)(2,1)S(1)}, bf16[64,1024]{1,0:T(8,128)(2,1)S(1)}, u32[]{:S(2)}, u32[]{:S(2)}) collective-permute-start(bf16[64,1024]{1,0:T(8,128)(2,1)S(1)} %get-tuple-element.19), channel_id=1, source_target_pairs={{0,15},{1,0},{2,1},{3,2},{4,3},{5,4},{6,5},{7,6},{8,7},{9,8},{10,9... | collective-permute-start | bytes 393224 | tf_op jit(solution)/shard_map/ppermute | solution.py:26
  108.9 3.6 %collective-permute-start.7 = (bf16[64,1024]{1,0:T(8,128)(2,1)S(1)}, bf16[64,1024]{1,0:T(8,128)(2,1)S(1)}, u32[]{:S(2)}, u32[]{:S(2)}) collective-permute-start(bf16[64,1024]{1,0:T(8,128)(2,1)S(1)} %get-tuple-element.16), channel_id=1, source_target_pairs={{0,1},{1,2},{2,3},{3,4},{4,5},{5,6},{6,7},{7,8},{8,9},{9,10},{10,1... | collective-permute-start | bytes 393224 | tf_op jit(solution)/shard_map/ppermute | solution.py:26
  118.3 4.1 %collective-permute-start.15 = (bf16[64,1024]{1,0:T(8,128)(2,1)S(1)}, bf16[64,1024]{1,0:T(8,128)(2,1)S(1)}, u32[]{:S(2)}, u32[]{:S(2)}) collective-permute-start(bf16[64,1024]{1,0:T(8,128)(2,1)S(1)} %get-tuple-element.15), channel_id=1, source_target_pairs={{0,15},{1,0},{2,1},{3,2},{4,3},{5,4},{6,5},{7,6},{8,7},{9,8},{10,9... | collective-permute-start | bytes 393224 | tf_op jit(solution)/shard_map/ppermute | solution.py:26
  125.3 4.0 %collective-permute-done.8 = bf16[64,1024]{1,0:T(8,128)(2,1)S(1)} collective-permute-done((bf16[64,1024]{1,0:T(8,128)(2,1)S(1)}, bf16[64,1024]{1,0:T(8,128)(2,1)S(1)}, u32[]{:S(2)}, u32[]{:S(2)}) %collective-permute-start.8) | collective-permute-done | bytes 131104 | tf_op jit(solution)/shard_map/ppermute | solution.py:26
  132.5 4.6 %collective-permute-start.17 = (bf16[64,1024]{1,0:T(8,128)(2,1)S(1)}, bf16[64,1024]{1,0:T(8,128)(2,1)S(1)}, u32[]{:S(2)}, u32[]{:S(2)}) collective-permute-start(bf16[64,1024]{1,0:T(8,128)(2,1)S(1)} %get-tuple-element.5), channel_id=1, source_target_pairs={{0,15},{1,0},{2,1},{3,2},{4,3},{5,4},{6,5},{7,6},{8,7},{9,8},{10,9... | collective-permute-start | bytes 393224 | tf_op jit(solution)/shard_map/ppermute | solution.py:26
  137.0 13.0 %collective-permute-start.33 = (bf16[512,512]{1,0:T(8,128)(2,1)}, bf16[512,512]{1,0:T(8,128)(2,1)}, u32[]{:S(2)}, u32[]{:S(2)}) collective-permute-start(bf16[512,512]{1,0:T(8,128)(2,1)} %param.11), channel_id=1, source_target_pairs={{0,16},{16,0},{32,48},{48,32},{64,80},{80,64},{96,112},{112,96},{1... | collective-permute-start | bytes 1572872 | tf_op jit(solution)/shard_map/ppermute | solution.py:23
  154.0 4.6 %collective-permute-start.19 = (bf16[64,1024]{1,0:T(8,128)(2,1)S(1)}, bf16[64,1024]{1,0:T(8,128)(2,1)S(1)}, u32[]{:S(2)}, u32[]{:S(2)}) collective-permute-start(bf16[64,1024]{1,0:T(8,128)(2,1)S(1)} %collective-permute-done.17), channel_id=1, source_target_pairs={{0,15},{1,0},{2,1},{3,2},{4,3},{5,4},{6,5},{7,6},{8,7},{9,8},{10,9... | collective-permute-start | bytes 393224 | tf_op jit(solution)/shard_map/ppermute | solution.py:26
  161.7 4.6 %collective-permute-start.21 = (bf16[64,1024]{1,0:T(8,128)(2,1)S(1)}, bf16[64,1024]{1,0:T(8,128)(2,1)S(1)}, u32[]{:S(2)}, u32[]{:S(2)}) collective-permute-start(bf16[64,1024]{1,0:T(8,128)(2,1)S(1)} %collective-permute-done.19), channel_id=1, source_target_pairs={{0,15},{1,0},{2,1},{3,2},{4,3},{5,4},{6,5},{7,6},{8,7},{9,8},{10,9... | collective-permute-start | bytes 393224 | tf_op jit(solution)/shard_map/ppermute | solution.py:26
  168.6 4.6 %collective-permute-start.23 = (bf16[64,1024]{1,0:T(8,128)(2,1)S(1)}, bf16[64,1024]{1,0:T(8,128)(2,1)S(1)}, u32[]{:S(2)}, u32[]{:S(2)}) collective-permute-start(bf16[64,1024]{1,0:T(8,128)(2,1)S(1)} %collective-permute-done.21), channel_id=1, source_target_pairs={{0,15},{1,0},{2,1},{3,2},{4,3},{5,4},{6,5},{7,6},{8,7},{9,8},{10,9... | collective-permute-start | bytes 393224 | tf_op jit(solution)/shard_map/ppermute | solution.py:26
  175.5 4.9 %collective-permute-start.25 = (bf16[64,1024]{1,0:T(8,128)(2,1)S(1)}, bf16[64,1024]{1,0:T(8,128)(2,1)S(1)}, u32[]{:S(2)}, u32[]{:S(2)}) collective-permute-start(bf16[64,1024]{1,0:T(8,128)(2,1)S(1)} %collective-permute-done.23), channel_id=1, source_target_pairs={{0,15},{1,0},{2,1},{3,2},{4,3},{5,4},{6,5},{7,6},{8,7},{9,8},{10,9... | collective-permute-start | bytes 393224 | tf_op jit(solution)/shard_map/ppermute | solution.py:26
  182.7 4.6 %collective-permute-start.27 = (bf16[64,1024]{1,0:T(8,128)(2,1)S(1)}, bf16[64,1024]{1,0:T(8,128)(2,1)S(1)}, u32[]{:S(2)}, u32[]{:S(2)}) collective-permute-start(bf16[64,1024]{1,0:T(8,128)(2,1)S(1)} %collective-permute-done.25), channel_id=1, source_target_pairs={{0,15},{1,0},{2,1},{3,2},{4,3},{5,4},{6,5},{7,6},{8,7},{9,8},{10,9... | collective-permute-start | bytes 393224 | tf_op jit(solution)/shard_map/ppermute | solution.py:26
  189.3 4.9 %collective-permute-start.29 = (bf16[64,1024]{1,0:T(8,128)(2,1)S(1)}, bf16[64,1024]{1,0:T(8,128)(2,1)S(1)}, u32[]{:S(2)}, u32[]{:S(2)}) collective-permute-start(bf16[64,1024]{1,0:T(8,128)(2,1)S(1)} %collective-permute-done.27), channel_id=1, source_target_pairs={{0,15},{1,0},{2,1},{3,2},{4,3},{5,4},{6,5},{7,6},{8,7},{9,8},{10,9... | collective-permute-start | bytes 393224 | tf_op jit(solution)/shard_map/ppermute | solution.py:26
  196.3 5.7 %collective-permute-done.30 = bf16[64,1024]{1,0:T(8,128)(2,1)S(1)} collective-permute-done((bf16[64,1024]{1,0:T(8,128)(2,1)S(1)}, bf16[64,1024]{1,0:T(8,128)(2,1)S(1)}, u32[]{:S(2)}, u32[]{:S(2)}) %collective-permute-start.30) | collective-permute-done | bytes 131104 | tf_op jit(solution)/shard_map/ppermute | solution.py:26
  210.3 3.5 %add_convert_fusion = bf16[1024,512]{1,0:T(8,128)(2,1)} fusion(f32[1024,512]{1,0:T(8,128)S(1)} %fusion.20, bf16[1024,1024]{1,0:T(8,128)(2,1)S(1)} %get-tuple-element.6, bf16[512,512]{1,0:T(8,128)(2,1)} %collective-permute-done.32, bf16[512,512]{1,0:T(8,128)(2,1)} %param.10), kind=kOutput, calls=%fused_computation.18 | convolution fusion | flops 1076887552 | bytes 6291456 | tf_op jit(solution)/shard_map/dot_general | solution.py:90
  213.8 4.7 %all-to-all-start.1 = ((bf16[16,64,512]{2,1,0:T(8,128)(2,1)}), bf16[16,64,512]{2,1,0:T(8,128)(2,1)S(1)}, u32[]{:S(2)}, u32[]{:S(2)}) async-start(bf16[16,64,512]{2,1,0:T(8,128)(2,1)} %bitcast.17), calls=%async_computation.1 | async-start | bytes 2097152 | tf_op jit(solution)/shard_map/all_to_all | solution.py:29
  224.5 10.7 %collective-permute-start.34 = (bf16[1024,512]{1,0:T(8,128)(2,1)}, bf16[1024,512]{1,0:T(8,128)(2,1)}, u32[]{:S(2)}, u32[]{:S(2)}) collective-permute-start(bf16[1024,512]{1,0:T(8,128)(2,1)} %pad_maximum_fusion.3), channel_id=1, source_target_pairs={{0,16},{16,0},{32,48},{48,32},{64,80},{80,64},{96,112},{112,96},{1... | collective-permute-start | bytes 3145736 | tf_op jit(solution)/shard_map/ppermute | solution.py:23
  (142 shorter events, 95.3 us)
Async XLA Ops:
  7.2 194.9 %all-gather.3.cloned.1.call-start = ((), (), s32[]{:S(2)}) async-start(), calls=%async_computation.2 | async-start | bytes 4456448 | tf_op jit(solution)/shard_map/all_gather | solution.py:38
  9.1 9.9 %collective-permute-start.31 = (bf16[64,1024]{1,0:T(8,128)(2,1)S(1)}, bf16[64,1024]{1,0:T(8,128)(2,1)S(1)}, u32[]{:S(2)}, u32[]{:S(2)}) collective-permute-start(bf16[64,1024]{1,0:T(8,128)(2,1)S(1)} %get-tuple-element.29), channel_id=1, source_target_pairs={{0,16},{16,0},{32,48},{48,32},{64,80},{80,64},{96,112},{112,96},{1... | collective-permute-start | bytes 393224 | tf_op jit(solution)/shard_map/ppermute | solution.py:23
  21.7 20.3 %all-to-all-start = ((bf16[16,64,512]{2,1,0:T(8,128)(2,1)}), bf16[16,64,512]{2,1,0:T(8,128)(2,1)S(1)}, u32[]{:S(2)}, u32[]{:S(2)}) async-start(bf16[16,64,512]{2,1,0:T(8,128)(2,1)} %tile.2), calls=%async_computation | async-start | bytes 2097152 | tf_op jit(solution)/shard_map/all_to_all | solution.py:29
  25.4 193.2 %all-gather.5.cloned.1.call-start = ((), (), s32[]{:S(2)}) async-start(), calls=%async_computation.3 | async-start | bytes 1114112 | tf_op jit(solution)/shard_map/all_gather | solution.py:76
  44.9 10.9 %collective-permute-start.1 = (bf16[64,1024]{1,0:T(8,128)(2,1)S(1)}, bf16[64,1024]{1,0:T(8,128)(2,1)S(1)}, u32[]{:S(2)}, u32[]{:S(2)}) collective-permute-start(bf16[64,1024]{1,0:T(8,128)(2,1)S(1)} %get-tuple-element.26), channel_id=1, source_target_pairs={{0,1},{1,2},{2,3},{3,4},{4,5},{5,6},{6,7},{7,8},{8,9},{9,10},{10,1... | collective-permute-start | bytes 393224 | tf_op jit(solution)/shard_map/ppermute | solution.py:26
  46.8 11.4 %collective-permute-start.9 = (bf16[64,1024]{1,0:T(8,128)(2,1)S(1)}, bf16[64,1024]{1,0:T(8,128)(2,1)S(1)}, u32[]{:S(2)}, u32[]{:S(2)}) collective-permute-start(bf16[64,1024]{1,0:T(8,128)(2,1)S(1)} %get-tuple-element.27), channel_id=1, source_target_pairs={{0,15},{1,0},{2,1},{3,2},{4,3},{5,4},{6,5},{7,6},{8,7},{9,8},{10,9... | collective-permute-start | bytes 393224 | tf_op jit(solution)/shard_map/ppermute | solution.py:26
  55.9 10.4 %collective-permute-start.2 = (bf16[64,1024]{1,0:T(8,128)(2,1)S(1)}, bf16[64,1024]{1,0:T(8,128)(2,1)S(1)}, u32[]{:S(2)}, u32[]{:S(2)}) collective-permute-start(bf16[64,1024]{1,0:T(8,128)(2,1)S(1)} %fusion.37), channel_id=1, source_target_pairs={{0,1},{1,2},{2,3},{3,4},{4,5},{5,6},{6,7},{7,8},{8,9},{9,10},{10,1... | collective-permute-start | bytes 393224 | tf_op jit(solution)/shard_map/ppermute | solution.py:26
  66.4 9.4 %collective-permute-start.3 = (bf16[64,1024]{1,0:T(8,128)(2,1)S(1)}, bf16[64,1024]{1,0:T(8,128)(2,1)S(1)}, u32[]{:S(2)}, u32[]{:S(2)}) collective-permute-start(bf16[64,1024]{1,0:T(8,128)(2,1)S(1)} %get-tuple-element.24), channel_id=1, source_target_pairs={{0,1},{1,2},{2,3},{3,4},{4,5},{5,6},{6,7},{7,8},{8,9},{9,10},{10,1... | collective-permute-start | bytes 393224 | tf_op jit(solution)/shard_map/ppermute | solution.py:26
  68.3 8.6 %collective-permute-start.10 = (bf16[64,1024]{1,0:T(8,128)(2,1)S(1)}, bf16[64,1024]{1,0:T(8,128)(2,1)S(1)}, u32[]{:S(2)}, u32[]{:S(2)}) collective-permute-start(bf16[64,1024]{1,0:T(8,128)(2,1)S(1)} %get-tuple-element.25), channel_id=1, source_target_pairs={{0,15},{1,0},{2,1},{3,2},{4,3},{5,4},{6,5},{7,6},{8,7},{9,8},{10,9... | collective-permute-start | bytes 393224 | tf_op jit(solution)/shard_map/ppermute | solution.py:26
  77.0 10.0 %collective-permute-start.4 = (bf16[64,1024]{1,0:T(8,128)(2,1)S(1)}, bf16[64,1024]{1,0:T(8,128)(2,1)S(1)}, u32[]{:S(2)}, u32[]{:S(2)}) collective-permute-start(bf16[64,1024]{1,0:T(8,128)(2,1)S(1)} %get-tuple-element.22), channel_id=1, source_target_pairs={{0,1},{1,2},{2,3},{3,4},{4,5},{5,6},{6,7},{7,8},{8,9},{9,10},{10,1... | collective-permute-start | bytes 393224 | tf_op jit(solution)/shard_map/ppermute | solution.py:26
  78.9 8.5 %collective-permute-start.11 = (bf16[64,1024]{1,0:T(8,128)(2,1)S(1)}, bf16[64,1024]{1,0:T(8,128)(2,1)S(1)}, u32[]{:S(2)}, u32[]{:S(2)}) collective-permute-start(bf16[64,1024]{1,0:T(8,128)(2,1)S(1)} %get-tuple-element.23), channel_id=1, source_target_pairs={{0,15},{1,0},{2,1},{3,2},{4,3},{5,4},{6,5},{7,6},{8,7},{9,8},{10,9... | collective-permute-start | bytes 393224 | tf_op jit(solution)/shard_map/ppermute | solution.py:26
  87.5 10.3 %collective-permute-start.5 = (bf16[64,1024]{1,0:T(8,128)(2,1)S(1)}, bf16[64,1024]{1,0:T(8,128)(2,1)S(1)}, u32[]{:S(2)}, u32[]{:S(2)}) collective-permute-start(bf16[64,1024]{1,0:T(8,128)(2,1)S(1)} %get-tuple-element.20), channel_id=1, source_target_pairs={{0,1},{1,2},{2,3},{3,4},{4,5},{5,6},{6,7},{7,8},{8,9},{9,10},{10,1... | collective-permute-start | bytes 393224 | tf_op jit(solution)/shard_map/ppermute | solution.py:26
  89.7 8.2 %collective-permute-start.12 = (bf16[64,1024]{1,0:T(8,128)(2,1)S(1)}, bf16[64,1024]{1,0:T(8,128)(2,1)S(1)}, u32[]{:S(2)}, u32[]{:S(2)}) collective-permute-start(bf16[64,1024]{1,0:T(8,128)(2,1)S(1)} %get-tuple-element.21), channel_id=1, source_target_pairs={{0,15},{1,0},{2,1},{3,2},{4,3},{5,4},{6,5},{7,6},{8,7},{9,8},{10,9... | collective-permute-start | bytes 393224 | tf_op jit(solution)/shard_map/ppermute | solution.py:26
  97.9 7.4 %collective-permute-start.6 = (bf16[64,1024]{1,0:T(8,128)(2,1)S(1)}, bf16[64,1024]{1,0:T(8,128)(2,1)S(1)}, u32[]{:S(2)}, u32[]{:S(2)}) collective-permute-start(bf16[64,1024]{1,0:T(8,128)(2,1)S(1)} %get-tuple-element.18), channel_id=1, source_target_pairs={{0,1},{1,2},{2,3},{3,4},{4,5},{5,6},{6,7},{7,8},{8,9},{9,10},{10,1... | collective-permute-start | bytes 393224 | tf_op jit(solution)/shard_map/ppermute | solution.py:26
  100.7 8.1 %collective-permute-start.13 = (bf16[64,1024]{1,0:T(8,128)(2,1)S(1)}, bf16[64,1024]{1,0:T(8,128)(2,1)S(1)}, u32[]{:S(2)}, u32[]{:S(2)}) collective-permute-start(bf16[64,1024]{1,0:T(8,128)(2,1)S(1)} %get-tuple-element.19), channel_id=1, source_target_pairs={{0,15},{1,0},{2,1},{3,2},{4,3},{5,4},{6,5},{7,6},{8,7},{9,8},{10,9... | collective-permute-start | bytes 393224 | tf_op jit(solution)/shard_map/ppermute | solution.py:26
  130.5 21.5 %collective-permute-start.16 = (bf16[64,1024]{1,0:T(8,128)(2,1)S(1)}, bf16[64,1024]{1,0:T(8,128)(2,1)S(1)}, u32[]{:S(2)}, u32[]{:S(2)}) collective-permute-start(bf16[64,1024]{1,0:T(8,128)(2,1)S(1)} %get-tuple-element.5), channel_id=1, source_target_pairs={{0,1},{1,2},{2,3},{3,4},{4,5},{5,6},{6,7},{7,8},{8,9},{9,10},{10,1... | collective-permute-start | bytes 393224 | tf_op jit(solution)/shard_map/ppermute | solution.py:26
  132.5 21.5 %collective-permute-start.17 = (bf16[64,1024]{1,0:T(8,128)(2,1)S(1)}, bf16[64,1024]{1,0:T(8,128)(2,1)S(1)}, u32[]{:S(2)}, u32[]{:S(2)}) collective-permute-start(bf16[64,1024]{1,0:T(8,128)(2,1)S(1)} %get-tuple-element.5), channel_id=1, source_target_pairs={{0,15},{1,0},{2,1},{3,2},{4,3},{5,4},{6,5},{7,6},{8,7},{9,8},{10,9... | collective-permute-start | bytes 393224 | tf_op jit(solution)/shard_map/ppermute | solution.py:26
  137.0 70.0 %collective-permute-start.33 = (bf16[512,512]{1,0:T(8,128)(2,1)}, bf16[512,512]{1,0:T(8,128)(2,1)}, u32[]{:S(2)}, u32[]{:S(2)}) collective-permute-start(bf16[512,512]{1,0:T(8,128)(2,1)} %param.11), channel_id=1, source_target_pairs={{0,16},{16,0},{32,48},{48,32},{64,80},{80,64},{96,112},{112,96},{1... | collective-permute-start | bytes 1572872 | tf_op jit(solution)/shard_map/ppermute | solution.py:23
  150.0 60.3 %collective-permute-start.32 = (bf16[512,512]{1,0:T(8,128)(2,1)}, bf16[512,512]{1,0:T(8,128)(2,1)}, u32[]{:S(2)}, u32[]{:S(2)}) collective-permute-start(bf16[512,512]{1,0:T(8,128)(2,1)} %param.10), channel_id=1, source_target_pairs={{0,16},{16,0},{32,48},{48,32},{64,80},{80,64},{96,112},{112,96},{1... | collective-permute-start | bytes 1572872 | tf_op jit(solution)/shard_map/ppermute | solution.py:23
  152.0 7.7 %collective-permute-start.18 = (bf16[64,1024]{1,0:T(8,128)(2,1)S(1)}, bf16[64,1024]{1,0:T(8,128)(2,1)S(1)}, u32[]{:S(2)}, u32[]{:S(2)}) collective-permute-start(bf16[64,1024]{1,0:T(8,128)(2,1)S(1)} %collective-permute-done.16), channel_id=1, source_target_pairs={{0,1},{1,2},{2,3},{3,4},{4,5},{5,6},{6,7},{7,8},{8,9},{9,10},{10,1... | collective-permute-start | bytes 393224 | tf_op jit(solution)/shard_map/ppermute | solution.py:26
  154.0 7.6 %collective-permute-start.19 = (bf16[64,1024]{1,0:T(8,128)(2,1)S(1)}, bf16[64,1024]{1,0:T(8,128)(2,1)S(1)}, u32[]{:S(2)}, u32[]{:S(2)}) collective-permute-start(bf16[64,1024]{1,0:T(8,128)(2,1)S(1)} %collective-permute-done.17), channel_id=1, source_target_pairs={{0,15},{1,0},{2,1},{3,2},{4,3},{5,4},{6,5},{7,6},{8,7},{9,8},{10,9... | collective-permute-start | bytes 393224 | tf_op jit(solution)/shard_map/ppermute | solution.py:26
  194.3 7.8 %collective-permute-start.30 = (bf16[64,1024]{1,0:T(8,128)(2,1)S(1)}, bf16[64,1024]{1,0:T(8,128)(2,1)S(1)}, u32[]{:S(2)}, u32[]{:S(2)}) collective-permute-start(bf16[64,1024]{1,0:T(8,128)(2,1)S(1)} %collective-permute-done.28), channel_id=1, source_target_pairs={{0,1},{1,2},{2,3},{3,4},{4,5},{5,6},{6,7},{7,8},{8,9},{9,10},{10,1... | collective-permute-start | bytes 393224 | tf_op jit(solution)/shard_map/ppermute | solution.py:26
  213.8 27.7 %all-to-all-start.1 = ((bf16[16,64,512]{2,1,0:T(8,128)(2,1)}), bf16[16,64,512]{2,1,0:T(8,128)(2,1)S(1)}, u32[]{:S(2)}, u32[]{:S(2)}) async-start(bf16[16,64,512]{2,1,0:T(8,128)(2,1)} %bitcast.17), calls=%async_computation.1 | async-start | bytes 2097152 | tf_op jit(solution)/shard_map/all_to_all | solution.py:29
  224.5 17.8 %collective-permute-start.34 = (bf16[1024,512]{1,0:T(8,128)(2,1)}, bf16[1024,512]{1,0:T(8,128)(2,1)}, u32[]{:S(2)}, u32[]{:S(2)}) collective-permute-start(bf16[1024,512]{1,0:T(8,128)(2,1)} %pad_maximum_fusion.3), channel_id=1, source_target_pairs={{0,16},{16,0},{32,48},{48,32},{64,80},{80,64},{96,112},{112,96},{1... | collective-permute-start | bytes 3145736 | tf_op jit(solution)/shard_map/ppermute | solution.py:23
  (35 other events, 297.2 us)
Sparse Core Ops, SparseCore 0:
  19.9 77.5 all-gather.2
  152.1 54.2 all-gather.4

commit v2 on v1

v2 whole, which is shorter than its diff:
```python
import jax
import jax.numpy as jnp
from jax import lax
from jax.experimental import pallas as pl
from jax.experimental.pallas import tpu as pltpu
from jax.sharding import PartitionSpec as P

F32 = jnp.float32
BF16 = jnp.bfloat16
NDIMS = (((1,), (1,)), ((), ()))
TDIMS = (((0,), (0,)), ((), ()))


def factors_kernel(acts_ref, gate_ref, up_ref, hidden_ref):
    units = acts_ref.shape[1] // 4
    for i in range(2):
        gate_val = acts_ref[:, 2 * i * units : (2 * i + 1) * units].astype(F32)
        up_val = acts_ref[:, (2 * i + 1) * units : (2 * i + 2) * units].astype(F32)
        sigma = jax.nn.sigmoid(gate_val)
        active = gate_val * sigma
        at = slice(i * units, (i + 1) * units)
        hidden_ref[:, at] = (active * up_val).astype(BF16)
        up_ref[:, at] = active.astype(BF16)
        gate_ref[:, at] = (up_val * sigma * (1.0 + gate_val * (1.0 - sigma))).astype(BF16)


def factors(acts, units):
    rows, block = acts.shape[0], 128
    out = jax.ShapeDtypeStruct((rows, 2 * units), BF16)
    spec = pl.BlockSpec((block, 2 * units), lambda i: (i, 0))
    return pl.pallas_call(
        factors_kernel,
        grid=(rows // block,),
        in_specs=[pl.BlockSpec((block, 4 * units), lambda i: (i, 0))],
        out_specs=[spec] * 3,
        out_shape=[out] * 3,
        compiler_params=pltpu.CompilerParams(vmem_limit_bytes=16 * 1024 * 1024),
        cost_estimate=pl.CostEstimate(
            flops=12 * rows * 2 * units,
            bytes_accessed=10 * rows * 2 * units,
            transcendentals=rows * 2 * units,
        ),
    )(acts)


def local(n_row, n_col, inputs, gate_pre, up_pre, w_gate, w_up, w_down, grad_out):
    chips = n_row // 2
    chip = lax.axis_index("row") // 2
    core = lax.axis_index("row") % 2
    col = lax.axis_index("col")
    siblings = [(i, i ^ 1) for i in range(n_row)]
    groups = [[2 * i + c for i in range(chips)] for c in range(2)]
    tokens = inputs.shape[0]
    units = w_gate.shape[1]

    def swap(array):
        return lax.ppermute(array, "row", siblings)

    def hop(array, step):
        return lax.ppermute(array, "col", [(i, (i + step) % n_col) for i in range(n_col)])

    def exchange(array):
        return lax.all_to_all(array, "row", 0, 0, axis_index_groups=groups, tiled=True)

    aligned = (chip + col) % 2 == 0
    moves = [
        ((2 * r + c) * n_col + z, (2 * (r ^ 1) + c) * n_col + (z - 1) % n_col)
        for r in range(chips)
        for c in range(2)
        for z in range(n_col)
        if (r + z) % 2
    ]
    moved = lax.ppermute(grad_out, ("row", "col"), moves)
    moved = jnp.where(aligned, grad_out, moved)
    spread = jnp.broadcast_to(moved[None], (chips,) + moved.shape).reshape(-1, moved.shape[1])
    acts = jnp.concatenate((gate_pre, up_pre), axis=1)
    spread, acts = lax.optimization_barrier((spread, acts))
    cot = exchange(spread)
    w_next = hop(w_down, -1)
    w_here = jnp.concatenate((w_down, swap(w_down)), axis=0)

    keep = lax.dynamic_slice_in_dim(acts, core * tokens, tokens, 0)
    give = lax.dynamic_slice_in_dim(acts, (1 - core) * tokens, tokens, 0)
    acts = jnp.concatenate((keep, swap(give)), axis=1)
    cot, w_next, acts, w_here = lax.optimization_barrier((cot, w_next, acts, w_here))
    acts_all = lax.all_gather(acts, "col", axis=0, tiled=True)
    w_next = jnp.concatenate((w_next, swap(w_next)), axis=0)
    cot = cot.reshape(n_col // 2, 2, tokens, -1)

    def pick(which):
        return lax.dynamic_index_in_dim(cot, which, 1, False).reshape(n_col // 2 * tokens, -1)

    partial = lax.dot_general(pick(col % 2), w_here, NDIMS, preferred_element_type=F32)
    partial = partial + lax.dot_general(
        pick(1 - col % 2), w_next, NDIMS, preferred_element_type=F32
    )
    partial = partial.astype(BF16)

    w_both = jnp.concatenate((w_gate, w_up), axis=0)
    partial, w_both = lax.optimization_barrier((partial, w_both))
    w_both = jnp.concatenate((w_both, swap(w_both)), axis=1)

    planes = n_col // 2
    half = planes // 2
    rank = col // 2

    def chunk(index):
        start = (index + planes) % planes * tokens
        return lax.dynamic_slice_in_dim(partial, start, tokens, 0).astype(F32)

    up_sum = chunk(rank + half).astype(BF16)
    down_grad = jnp.zeros((n_col * tokens, 2 * units), BF16)
    down_sum = chunk(rank - half + 1).astype(BF16)
    for step in range(1, half + 1):
        up_in = hop(up_sum, 2)
        if step == 2:
            down_sum, w_both, down_grad = lax.optimization_barrier((down_sum, w_both, down_grad))
        if step < half:
            down_in = hop(down_sum, -2)
            up_sum = (up_in.astype(F32) + chunk(rank + half - step)).astype(BF16)
            if step < half - 1:
                down_sum = (down_in.astype(F32) + chunk(rank - half + 1 + step)).astype(BF16)
    w_gate2, w_up2 = w_both[: w_gate.shape[0]], w_both[w_gate.shape[0] :]
    mine = (up_in.astype(F32) + down_in.astype(F32) + chunk(rank)).astype(BF16)

    rows = jnp.concatenate((inputs, grad_out), axis=1)
    rows = lax.all_gather(rows, "row", axis=0, tiled=True, axis_index_groups=groups)
    input_rows, cot_rows = rows[:, : inputs.shape[1]], rows[:, inputs.shape[1] :]

    gate_by, up_by, hidden = factors(acts_all, units)

    half = n_col // 2

    def put(whole, piece, index):
        start = (index + n_col) % n_col * tokens
        return lax.dynamic_update_slice_in_dim(whole, piece, start, 0)

    down_grad = put(down_grad, mine, col)
    above = below = mine
    for step in range(1, half + 1):
        above = hop(above, 1)
        if step == half - 1:
            below, gate_by, up_by, hidden = lax.optimization_barrier(
                (below, gate_by, up_by, hidden)
            )
        if step < half:
            below = hop(below, -1)
        down_grad = put(down_grad, above, col - step)
        if step < half:
            down_grad = put(down_grad, below, col + step)

    grads = down_grad.astype(F32)
    gate_grad = (grads * gate_by.astype(F32)).astype(BF16)
    up_grad = (grads * up_by.astype(F32)).astype(BF16)
    total = lax.dot_general(gate_grad, w_gate2, NDIMS, preferred_element_type=F32)
    total = total + lax.dot_general(up_grad, w_up2, NDIMS, preferred_element_type=F32)
    total, gate_grad, up_grad = lax.optimization_barrier(
        (total.astype(BF16), gate_grad, up_grad)
    )
    sums = exchange(total).reshape(chips, tokens, -1)
    input_grad = jnp.sum(sums.astype(F32), axis=0).astype(BF16)
    wd = lax.dot_general(hidden, cot_rows, TDIMS, preferred_element_type=F32)
    w_down_grad = (wd[:units] + swap(wd[units:].astype(BF16)).astype(F32)).astype(BF16)
    wg = lax.dot_general(input_rows, gate_grad, TDIMS, preferred_element_type=F32)
    wu = lax.dot_general(input_rows, up_grad, TDIMS, preferred_element_type=F32)
    other = swap(jnp.concatenate((wg[:, units:], wu[:, units:]), axis=0).astype(BF16)).astype(F32)
    width = wg.shape[0]
    w_gate_grad = (wg[:, :units] + other[:width]).astype(BF16)
    w_up_grad = (wu[:, :units] + other[width:]).astype(BF16)
    return (input_grad, w_gate_grad, w_up_grad, w_down_grad)


def solution(mesh):
    n_row, n_col = mesh.shape["row"], mesh.shape["col"]

    def step(*arrays):
        return local(n_row, n_col, *arrays)

    return jax.shard_map(
        step,
        mesh=mesh,
        in_specs=(
            P("row", "col"),
            P("col", "row"),
            P("col", "row"),
            P("col", "row"),
            P("col", "row"),
            P("row", "col"),
            P("row", "col"),
        ),
        out_specs=(P("row", "col"), P("col", "row"), P("col", "row"), P("row", "col")),
        check_vma=False,
    )
```

time: 254 us -> 234 us (0.921)
  starting transfers between devices: 147 us -> 132 us
  waiting for transfers between devices: 57 us -> 47.9 us
  other arithmetic: 10.2 us -> 16.7 us
  matrix products: 15.6 us -> 10.9 us
    ppermute x6, starting transfers between devices: 38.7 us -> 22.9 us  [swap(): return lax.ppermute(array, 'row', siblings)]
    all_to_all x2, starting transfers between devices: 8.39 us -> 24 us  [exchange(): lax.all_to_all(array, 'row', 0, 0, axis_index_groups=groups, tiled=True)]
    ppermute x30 -> x23, starting transfers between devices: 99.8 us -> 84.5 us  [hop(): lax.ppermute(array, 'col', [(i, (i + step) % n_col) for i in range(n_col)])]
    all_to_all x2, waiting for transfers between devices: 12.7 us -> 0.01 us  [exchange(): lax.all_to_all(array, 'row', 0, 0, axis_index_groups=groups, tiled=True)]
    concatenate x0 -> x5, other arithmetic: none -> 5.71 us  [the longest x1 1.71 us: local(): w_both = jnp.concatenate((w_both, swap(w_both)), axis=1)]
    unnamed x39 -> x32, local copies, waits for them, and re-layouts: 1.38 us -> 4.96 us
    ppermute x30 -> x23, waiting for transfers between devices: 39.8 us -> 42.7 us  [hop(): lax.ppermute(array, 'col', [(i, (i + step) % n_col) for i in range(n_col)])]
  transfers between devices with their start and end apart: 40 -> 34, of which waited for: 24 -> 19; matrix products, arithmetic and copies ran while one was open for 11% -> 11% of each run, Pallas kernels for 0% -> 1%
where the time goes in v2:
time: 234 us; the launch traced here: 233 us
  starting transfers between devices  132 us (56%)
  waiting for transfers between devices  47.9 us (20%)
  other arithmetic  16.7 us (7%)
  between operations  15.3 us (7%)
  matrix products  10.9 us (5%)
  local copies, waits for them, and re-layouts  7.59 us (3%)
    ppermute x23, starting transfers between devices, hop(): lax.ppermute(array, 'col', [(i, (i + step) % n_col) for i in range(n_col)])  84.5 us
    ppermute x23, waiting for transfers between devices, hop(): lax.ppermute(array, 'col', [(i, (i + step) % n_col) for i in range(n_col)])  42.7 us
    all_to_all x2, starting transfers between devices, exchange(): lax.all_to_all(array, 'row', 0, 0, axis_index_groups=groups, tiled=True)  24 us
    ppermute x6, starting transfers between devices, swap(): return lax.ppermute(array, 'row', siblings)  22.9 us
    unnamed x32, local copies, waits for them, and re-layouts  4.96 us
  transfers between devices with their start and end apart: 34, of which 19 were waited for; matrix products, arithmetic and copies ran while one was open for 11% of the time, Pallas kernels for 1%

profile of v2, /device:TPU:1, one launch (start us, length us, event | category | flops | bytes accessed | tf_op | source)
XLA Modules:
  0.0 233.0 jit_solution(15613442277475611189)
XLA Ops:
  11.0 17.8 %all-to-all-start = ((bf16[16,64,512]{2,1,0:T(8,128)(2,1)}), bf16[16,64,512]{2,1,0:T(8,128)(2,1)S(1)}, u32[]{:S(2)}, u32[]{:S(2)}) async-start(bf16[16,64,512]{2,1,0:T(8,128)(2,1)} %bitcast.1), calls=%async_computation | async-start | bytes 2097152 | tf_op jit(solution)/shard_map/all_to_all | solution.py:63
  28.9 3.7 %collective-permute-start.3 = (bf16[512,512]{1,0:T(8,128)(2,1)S(1)}, bf16[512,512]{1,0:T(8,128)(2,1)S(1)}, u32[]{:S(2)}, u32[]{:S(2)}) collective-permute-start(bf16[512,512]{1,0:T(8,128)(2,1)S(1)} %copy-done.13), channel_id=1, source_target_pairs={{0,16},{16,0},{32,48},{48,32},{64,80},{80,64},{96,112},{112,96},{1... | collective-permute-start | bytes 1572872 | tf_op jit(solution)/shard_map/ppermute | solution.py:57
  32.6 6.0 %collective-permute-start.1 = (bf16[512,512]{1,0:T(8,128)(2,1)S(1)}, bf16[512,512]{1,0:T(8,128)(2,1)S(1)}, u32[]{:S(2)}, u32[]{:S(2)}) collective-permute-start(bf16[512,512]{1,0:T(8,128)(2,1)S(1)} %copy-done.13), channel_id=1, source_target_pairs={{0,15},{1,0},{2,1},{3,2},{4,3},{5,4},{6,5},{7,6},{8,7},{9,8},{10,9... | collective-permute-start | bytes 1572872 | tf_op jit(solution)/shard_map/ppermute | solution.py:60
  43.7 6.2 %collective-permute-done.1 = bf16[512,512]{1,0:T(8,128)(2,1)S(1)} collective-permute-done((bf16[512,512]{1,0:T(8,128)(2,1)S(1)}, bf16[512,512]{1,0:T(8,128)(2,1)S(1)}, u32[]{:S(2)}, u32[]{:S(2)}) %collective-permute-start.1) | collective-permute-done | bytes 524320 | tf_op jit(solution)/shard_map/ppermute | solution.py:60
  60.7 5.5 %collective-permute-start.5 = (bf16[64,1024]{1,0:T(8,128)(2,1)}, bf16[64,1024]{1,0:T(8,128)(2,1)}, u32[]{:S(2)}, u32[]{:S(2)}) collective-permute-start(bf16[64,1024]{1,0:T(8,128)(2,1)} %get-tuple-element.57), channel_id=1, source_target_pairs={{0,14},{1,15},{2,0},{3,1},{4,2},{5,3},{6,4},{7,5},{8,6},{9,7},{10,... | collective-permute-start | bytes 393224 | tf_op jit(solution)/shard_map/ppermute | solution.py:60
  70.2 3.1 %collective-permute-done.5 = bf16[64,1024]{1,0:T(8,128)(2,1)} collective-permute-done((bf16[64,1024]{1,0:T(8,128)(2,1)}, bf16[64,1024]{1,0:T(8,128)(2,1)}, u32[]{:S(2)}, u32[]{:S(2)}) %collective-permute-start.5) | collective-permute-done | bytes 131104 | tf_op jit(solution)/shard_map/ppermute | solution.py:60
  73.3 6.1 %collective-permute-done.8 = bf16[64,1024]{1,0:T(8,128)(2,1)S(1)} collective-permute-done((bf16[64,1024]{1,0:T(8,128)(2,1)S(1)}, bf16[64,1024]{1,0:T(8,128)(2,1)S(1)}, u32[]{:S(2)}, u32[]{:S(2)}) %collective-permute-start.8) | collective-permute-done | bytes 131104 | tf_op jit(solution)/shard_map/ppermute | solution.py:60
  84.6 5.5 %collective-permute-start.11 = (bf16[64,1024]{1,0:T(8,128)(2,1)S(1)}, bf16[64,1024]{1,0:T(8,128)(2,1)S(1)}, u32[]{:S(2)}, u32[]{:S(2)}) collective-permute-start(bf16[64,1024]{1,0:T(8,128)(2,1)S(1)} %get-tuple-element.33), channel_id=1, source_target_pairs={{0,14},{1,15},{2,0},{3,1},{4,2},{5,3},{6,4},{7,5},{8,6},{9,7},{10,... | collective-permute-start | bytes 393224 | tf_op jit(solution)/shard_map/ppermute | solution.py:60
  93.5 5.9 %collective-permute-start.12 = (bf16[64,1024]{1,0:T(8,128)(2,1)S(1)}, bf16[64,1024]{1,0:T(8,128)(2,1)S(1)}, u32[]{:S(2)}, u32[]{:S(2)}) collective-permute-start(bf16[64,1024]{1,0:T(8,128)(2,1)S(1)} %get-tuple-element.53), channel_id=1, source_target_pairs={{0,14},{1,15},{2,0},{3,1},{4,2},{5,3},{6,4},{7,5},{8,6},{9,7},{10,... | collective-permute-start | bytes 393224 | tf_op jit(solution)/shard_map/ppermute | solution.py:60
  101.5 4.8 %collective-permute-done.12 = bf16[64,1024]{1,0:T(8,128)(2,1)S(1)} collective-permute-done((bf16[64,1024]{1,0:T(8,128)(2,1)S(1)}, bf16[64,1024]{1,0:T(8,128)(2,1)S(1)}, u32[]{:S(2)}, u32[]{:S(2)}) %collective-permute-start.12) | collective-permute-done | bytes 131104 | tf_op jit(solution)/shard_map/ppermute | solution.py:60
  106.3 3.2 %collective-permute-done.10 = bf16[64,1024]{1,0:T(8,128)(2,1)S(1)} collective-permute-done((bf16[64,1024]{1,0:T(8,128)(2,1)S(1)}, bf16[64,1024]{1,0:T(8,128)(2,1)S(1)}, u32[]{:S(2)}, u32[]{:S(2)}) %collective-permute-start.10) | collective-permute-done | bytes 131104 | tf_op jit(solution)/shard_map/ppermute | solution.py:60
  109.8 11.0 %collective-permute-start.13 = (bf16[64,1024]{1,0:T(8,128)(2,1)S(1)}, bf16[64,1024]{1,0:T(8,128)(2,1)S(1)}, u32[]{:S(2)}, u32[]{:S(2)}) collective-permute-start(bf16[64,1024]{1,0:T(8,128)(2,1)S(1)} %get-tuple-element.47), channel_id=1, source_target_pairs={{0,1},{1,2},{2,3},{3,4},{4,5},{5,6},{6,7},{7,8},{8,9},{9,10},{10,1... | collective-permute-start | bytes 393224 | tf_op jit(solution)/shard_map/ppermute | solution.py:60
  125.7 3.2 %collective-permute-start.15 = (bf16[64,1024]{1,0:T(8,128)(2,1)S(1)}, bf16[64,1024]{1,0:T(8,128)(2,1)S(1)}, u32[]{:S(2)}, u32[]{:S(2)}) collective-permute-start(bf16[64,1024]{1,0:T(8,128)(2,1)S(1)} %collective-permute-done.13), channel_id=1, source_target_pairs={{0,1},{1,2},{2,3},{3,4},{4,5},{5,6},{6,7},{7,8},{8,9},{9,10},{10,1... | collective-permute-start | bytes 393224 | tf_op jit(solution)/shard_map/ppermute | solution.py:60
  129.0 3.2 %collective-permute-start.16 = (bf16[64,1024]{1,0:T(8,128)(2,1)S(1)}, bf16[64,1024]{1,0:T(8,128)(2,1)S(1)}, u32[]{:S(2)}, u32[]{:S(2)}) collective-permute-start(bf16[64,1024]{1,0:T(8,128)(2,1)S(1)} %collective-permute-done.14), channel_id=1, source_target_pairs={{0,15},{1,0},{2,1},{3,2},{4,3},{5,4},{6,5},{7,6},{8,7},{9,8},{10,9... | collective-permute-start | bytes 393224 | tf_op jit(solution)/shard_map/ppermute | solution.py:60
  132.3 3.4 %collective-permute-done.15 = bf16[64,1024]{1,0:T(8,128)(2,1)S(1)} collective-permute-done((bf16[64,1024]{1,0:T(8,128)(2,1)S(1)}, bf16[64,1024]{1,0:T(8,128)(2,1)S(1)}, u32[]{:S(2)}, u32[]{:S(2)}) %collective-permute-start.15) | collective-permute-done | bytes 131104 | tf_op jit(solution)/shard_map/ppermute | solution.py:60
  138.5 3.7 %collective-permute-start.18 = (bf16[64,1024]{1,0:T(8,128)(2,1)S(1)}, bf16[64,1024]{1,0:T(8,128)(2,1)S(1)}, u32[]{:S(2)}, u32[]{:S(2)}) collective-permute-start(bf16[64,1024]{1,0:T(8,128)(2,1)S(1)} %collective-permute-done.16), channel_id=1, source_target_pairs={{0,15},{1,0},{2,1},{3,2},{4,3},{5,4},{6,5},{7,6},{8,7},{9,8},{10,9... | collective-permute-start | bytes 393224 | tf_op jit(solution)/shard_map/ppermute | solution.py:60
  145.0 4.1 %collective-permute-start.20 = (bf16[64,1024]{1,0:T(8,128)(2,1)S(1)}, bf16[64,1024]{1,0:T(8,128)(2,1)S(1)}, u32[]{:S(2)}, u32[]{:S(2)}) collective-permute-start(bf16[64,1024]{1,0:T(8,128)(2,1)S(1)} %collective-permute-done.18), channel_id=1, source_target_pairs={{0,15},{1,0},{2,1},{3,2},{4,3},{5,4},{6,5},{7,6},{8,7},{9,8},{10,9... | collective-permute-start | bytes 393224 | tf_op jit(solution)/shard_map/ppermute | solution.py:60
  152.4 4.5 %collective-permute-start.22 = (bf16[64,1024]{1,0:T(8,128)(2,1)S(1)}, bf16[64,1024]{1,0:T(8,128)(2,1)S(1)}, u32[]{:S(2)}, u32[]{:S(2)}) collective-permute-start(bf16[64,1024]{1,0:T(8,128)(2,1)S(1)} %collective-permute-done.20), channel_id=1, source_target_pairs={{0,15},{1,0},{2,1},{3,2},{4,3},{5,4},{6,5},{7,6},{8,7},{9,8},{10,9... | collective-permute-start | bytes 393224 | tf_op jit(solution)/shard_map/ppermute | solution.py:60
  160.3 4.6 %collective-permute-start.24 = (bf16[64,1024]{1,0:T(8,128)(2,1)S(1)}, bf16[64,1024]{1,0:T(8,128)(2,1)S(1)}, u32[]{:S(2)}, u32[]{:S(2)}) collective-permute-start(bf16[64,1024]{1,0:T(8,128)(2,1)S(1)} %collective-permute-done.22), channel_id=1, source_target_pairs={{0,15},{1,0},{2,1},{3,2},{4,3},{5,4},{6,5},{7,6},{8,7},{9,8},{10,9... | collective-permute-start | bytes 393224 | tf_op jit(solution)/shard_map/ppermute | solution.py:60
  173.5 4.6 %collective-permute-start.26 = (bf16[64,1024]{1,0:T(8,128)(2,1)S(1)}, bf16[64,1024]{1,0:T(8,128)(2,1)S(1)}, u32[]{:S(2)}, u32[]{:S(2)}) collective-permute-start(bf16[64,1024]{1,0:T(8,128)(2,1)S(1)} %collective-permute-done.24), channel_id=1, source_target_pairs={{0,15},{1,0},{2,1},{3,2},{4,3},{5,4},{6,5},{7,6},{8,7},{9,8},{10,9... | collective-permute-start | bytes 393224 | tf_op jit(solution)/shard_map/ppermute | solution.py:60
  180.1 4.9 %collective-permute-done.27 = bf16[64,1024]{1,0:T(8,128)(2,1)S(1)} collective-permute-done((bf16[64,1024]{1,0:T(8,128)(2,1)S(1)}, bf16[64,1024]{1,0:T(8,128)(2,1)S(1)}, u32[]{:S(2)}, u32[]{:S(2)}) %collective-permute-start.27) | collective-permute-done | bytes 131104 | tf_op jit(solution)/shard_map/ppermute | solution.py:60
  191.1 6.2 %all-to-all-start.1 = ((bf16[16,64,512]{2,1,0:T(8,128)(2,1)}), bf16[16,64,512]{2,1,0:T(8,128)(2,1)S(1)}, u32[]{:S(2)}, u32[]{:S(2)}) async-start(bf16[16,64,512]{2,1,0:T(8,128)(2,1)} %bitcast.18), calls=%async_computation.1 | async-start | bytes 2097152 | tf_op jit(solution)/shard_map/all_to_all | solution.py:63
  199.4 3.3 %fusion.14 = f32[512,1024]{1,0:T(8,128)S(1)} fusion(bf16[1024,1024]{1,0:T(8,128)(2,1)} %copy-done.3, bf16[1024,1024]{1,0:T(8,128)(2,1)} %all-gather.5.cloned.1.call-done), kind=kOutput, calls=%fused_computation.28 | convolution fusion | flops 1073741824 | bytes 5242880 | tf_op jit(solution)/shard_map/dot_general | solution.py:165
  205.4 10.4 %collective-permute-start.28 = (bf16[1024,512]{1,0:T(8,128)(2,1)}, bf16[1024,512]{1,0:T(8,128)(2,1)}, u32[]{:S(2)}, u32[]{:S(2)}) collective-permute-start(bf16[1024,512]{1,0:T(8,128)(2,1)} %pad_maximum_fusion.3), channel_id=1, source_target_pairs={{0,16},{16,0},{32,48},{48,32},{64,80},{80,64},{96,112},{112,96},{1... | collective-permute-start | bytes 3145736 | tf_op jit(solution)/shard_map/ppermute | solution.py:57
  (126 shorter events, 82.8 us)
Async XLA Ops:
  11.0 38.9 %all-to-all-start = ((bf16[16,64,512]{2,1,0:T(8,128)(2,1)}), bf16[16,64,512]{2,1,0:T(8,128)(2,1)S(1)}, u32[]{:S(2)}, u32[]{:S(2)}) async-start(bf16[16,64,512]{2,1,0:T(8,128)(2,1)} %bitcast.1), calls=%async_computation | async-start | bytes 2097152 | tf_op jit(solution)/shard_map/all_to_all | solution.py:63
  28.8 140.2 %all-gather.3.cloned.1.call-start = ((), (), s32[]{:S(2)}) async-start(), calls=%async_computation.2 | async-start | bytes 4456448 | tf_op jit(solution)/shard_map/all_gather | solution.py:86
  28.9 13.7 %collective-permute-start.3 = (bf16[512,512]{1,0:T(8,128)(2,1)S(1)}, bf16[512,512]{1,0:T(8,128)(2,1)S(1)}, u32[]{:S(2)}, u32[]{:S(2)}) collective-permute-start(bf16[512,512]{1,0:T(8,128)(2,1)S(1)} %copy-done.13), channel_id=1, source_target_pairs={{0,16},{16,0},{32,48},{48,32},{64,80},{80,64},{96,112},{112,96},{1... | collective-permute-start | bytes 1572872 | tf_op jit(solution)/shard_map/ppermute | solution.py:57
  32.6 17.3 %collective-permute-start.1 = (bf16[512,512]{1,0:T(8,128)(2,1)S(1)}, bf16[512,512]{1,0:T(8,128)(2,1)S(1)}, u32[]{:S(2)}, u32[]{:S(2)}) collective-permute-start(bf16[512,512]{1,0:T(8,128)(2,1)S(1)} %copy-done.13), channel_id=1, source_target_pairs={{0,15},{1,0},{2,1},{3,2},{4,3},{5,4},{6,5},{7,6},{8,7},{9,8},{10,9... | collective-permute-start | bytes 1572872 | tf_op jit(solution)/shard_map/ppermute | solution.py:60
  49.9 149.4 %all-gather.5.cloned.1.call-start = ((), (), s32[]{:S(2)}) async-start(), calls=%async_computation.3 | async-start | bytes 2228224 | tf_op jit(solution)/shard_map/all_gather | solution.py:127
  56.1 26.9 %collective-permute-start.6 = (bf16[1024,512]{1,0:T(8,128)(2,1)S(1)}, bf16[1024,512]{1,0:T(8,128)(2,1)S(1)}, u32[]{:S(2)}, u32[]{:S(2)}) collective-permute-start(bf16[1024,512]{1,0:T(8,128)(2,1)S(1)} %pad_maximum_fusion.2), channel_id=1, source_target_pairs={{0,16},{16,0},{32,48},{48,32},{64,80},{80,64},{96,112},{112,96},{1... | collective-permute-start | bytes 3145736 | tf_op jit(solution)/shard_map/ppermute | solution.py:57
  58.8 8.7 %collective-permute-start.7 = (bf16[64,1024]{1,0:T(8,128)(2,1)S(1)}, bf16[64,1024]{1,0:T(8,128)(2,1)S(1)}, u32[]{:S(2)}, u32[]{:S(2)}) collective-permute-start(bf16[64,1024]{1,0:T(8,128)(2,1)S(1)} %get-tuple-element.56), channel_id=1, source_target_pairs={{0,2},{1,3},{2,4},{3,5},{4,6},{5,7},{6,8},{7,9},{8,10},{9,11},{10,... | collective-permute-start | bytes 393224 | tf_op jit(solution)/shard_map/ppermute | solution.py:60
  60.7 12.5 %collective-permute-start.5 = (bf16[64,1024]{1,0:T(8,128)(2,1)}, bf16[64,1024]{1,0:T(8,128)(2,1)}, u32[]{:S(2)}, u32[]{:S(2)}) collective-permute-start(bf16[64,1024]{1,0:T(8,128)(2,1)} %get-tuple-element.57), channel_id=1, source_target_pairs={{0,14},{1,15},{2,0},{3,1},{4,2},{5,3},{6,4},{7,5},{8,6},{9,7},{10,... | collective-permute-start | bytes 393224 | tf_op jit(solution)/shard_map/ppermute | solution.py:60
  67.5 11.9 %collective-permute-start.8 = (bf16[64,1024]{1,0:T(8,128)(2,1)S(1)}, bf16[64,1024]{1,0:T(8,128)(2,1)S(1)}, u32[]{:S(2)}, u32[]{:S(2)}) collective-permute-start(bf16[64,1024]{1,0:T(8,128)(2,1)S(1)} %add_convert_fusion.6), channel_id=1, source_target_pairs={{0,2},{1,3},{2,4},{3,5},{4,6},{5,7},{6,8},{7,9},{8,10},{9,11},{10,... | collective-permute-start | bytes 393224 | tf_op jit(solution)/shard_map/ppermute | solution.py:60
  81.0 11.2 %collective-permute-start.9 = (bf16[64,1024]{1,0:T(8,128)(2,1)}, bf16[64,1024]{1,0:T(8,128)(2,1)S(1)}, u32[]{:S(2)}, u32[]{:S(2)}) collective-permute-start(bf16[64,1024]{1,0:T(8,128)(2,1)} %get-tuple-element.54), channel_id=1, source_target_pairs={{0,2},{1,3},{2,4},{3,5},{4,6},{5,7},{6,8},{7,9},{8,10},{9,11},{10,... | collective-permute-start | bytes 393224 | tf_op jit(solution)/shard_map/ppermute | solution.py:60
  84.6 8.8 %collective-permute-start.11 = (bf16[64,1024]{1,0:T(8,128)(2,1)S(1)}, bf16[64,1024]{1,0:T(8,128)(2,1)S(1)}, u32[]{:S(2)}, u32[]{:S(2)}) collective-permute-start(bf16[64,1024]{1,0:T(8,128)(2,1)S(1)} %get-tuple-element.33), channel_id=1, source_target_pairs={{0,14},{1,15},{2,0},{3,1},{4,2},{5,3},{6,4},{7,5},{8,6},{9,7},{10,... | collective-permute-start | bytes 393224 | tf_op jit(solution)/shard_map/ppermute | solution.py:60
  93.5 12.7 %collective-permute-start.12 = (bf16[64,1024]{1,0:T(8,128)(2,1)S(1)}, bf16[64,1024]{1,0:T(8,128)(2,1)S(1)}, u32[]{:S(2)}, u32[]{:S(2)}) collective-permute-start(bf16[64,1024]{1,0:T(8,128)(2,1)S(1)} %get-tuple-element.53), channel_id=1, source_target_pairs={{0,14},{1,15},{2,0},{3,1},{4,2},{5,3},{6,4},{7,5},{8,6},{9,7},{10,... | collective-permute-start | bytes 393224 | tf_op jit(solution)/shard_map/ppermute | solution.py:60
  99.5 10.0 %collective-permute-start.10 = (bf16[64,1024]{1,0:T(8,128)(2,1)S(1)}, bf16[64,1024]{1,0:T(8,128)(2,1)S(1)}, u32[]{:S(2)}, u32[]{:S(2)}) collective-permute-start(bf16[64,1024]{1,0:T(8,128)(2,1)S(1)} %get-tuple-element.52), channel_id=1, source_target_pairs={{0,2},{1,3},{2,4},{3,5},{4,6},{5,7},{6,8},{7,9},{8,10},{9,11},{10,... | collective-permute-start | bytes 393224 | tf_op jit(solution)/shard_map/ppermute | solution.py:60
  109.8 15.9 %collective-permute-start.13 = (bf16[64,1024]{1,0:T(8,128)(2,1)S(1)}, bf16[64,1024]{1,0:T(8,128)(2,1)S(1)}, u32[]{:S(2)}, u32[]{:S(2)}) collective-permute-start(bf16[64,1024]{1,0:T(8,128)(2,1)S(1)} %get-tuple-element.47), channel_id=1, source_target_pairs={{0,1},{1,2},{2,3},{3,4},{4,5},{5,6},{6,7},{7,8},{8,9},{9,10},{10,1... | collective-permute-start | bytes 393224 | tf_op jit(solution)/shard_map/ppermute | solution.py:60
  120.8 8.2 %collective-permute-start.14 = (bf16[64,1024]{1,0:T(8,128)(2,1)S(1)}, bf16[64,1024]{1,0:T(8,128)(2,1)S(1)}, u32[]{:S(2)}, u32[]{:S(2)}) collective-permute-start(bf16[64,1024]{1,0:T(8,128)(2,1)S(1)} %get-tuple-element.47), channel_id=1, source_target_pairs={{0,15},{1,0},{2,1},{3,2},{4,3},{5,4},{6,5},{7,6},{8,7},{9,8},{10,9... | collective-permute-start | bytes 393224 | tf_op jit(solution)/shard_map/ppermute | solution.py:60
  125.7 10.0 %collective-permute-start.15 = (bf16[64,1024]{1,0:T(8,128)(2,1)S(1)}, bf16[64,1024]{1,0:T(8,128)(2,1)S(1)}, u32[]{:S(2)}, u32[]{:S(2)}) collective-permute-start(bf16[64,1024]{1,0:T(8,128)(2,1)S(1)} %collective-permute-done.13), channel_id=1, source_target_pairs={{0,1},{1,2},{2,3},{3,4},{4,5},{5,6},{6,7},{7,8},{8,9},{9,10},{10,1... | collective-permute-start | bytes 393224 | tf_op jit(solution)/shard_map/ppermute | solution.py:60
  129.0 9.5 %collective-permute-start.16 = (bf16[64,1024]{1,0:T(8,128)(2,1)S(1)}, bf16[64,1024]{1,0:T(8,128)(2,1)S(1)}, u32[]{:S(2)}, u32[]{:S(2)}) collective-permute-start(bf16[64,1024]{1,0:T(8,128)(2,1)S(1)} %collective-permute-done.14), channel_id=1, source_target_pairs={{0,15},{1,0},{2,1},{3,2},{4,3},{5,4},{6,5},{7,6},{8,7},{9,8},{10,9... | collective-permute-start | bytes 393224 | tf_op jit(solution)/shard_map/ppermute | solution.py:60
  142.6 7.5 %collective-permute-start.19 = (bf16[64,1024]{1,0:T(8,128)(2,1)S(1)}, bf16[64,1024]{1,0:T(8,128)(2,1)S(1)}, u32[]{:S(2)}, u32[]{:S(2)}) collective-permute-start(bf16[64,1024]{1,0:T(8,128)(2,1)S(1)} %collective-permute-done.17), channel_id=1, source_target_pairs={{0,1},{1,2},{2,3},{3,4},{4,5},{5,6},{6,7},{7,8},{8,9},{9,10},{10,1... | collective-permute-start | bytes 393224 | tf_op jit(solution)/shard_map/ppermute | solution.py:60
  150.1 8.3 %collective-permute-start.21 = (bf16[64,1024]{1,0:T(8,128)(2,1)S(1)}, bf16[64,1024]{1,0:T(8,128)(2,1)S(1)}, u32[]{:S(2)}, u32[]{:S(2)}) collective-permute-start(bf16[64,1024]{1,0:T(8,128)(2,1)S(1)} %collective-permute-done.19), channel_id=1, source_target_pairs={{0,1},{1,2},{2,3},{3,4},{4,5},{5,6},{6,7},{7,8},{8,9},{9,10},{10,1... | collective-permute-start | bytes 393224 | tf_op jit(solution)/shard_map/ppermute | solution.py:60
  152.4 7.9 %collective-permute-start.22 = (bf16[64,1024]{1,0:T(8,128)(2,1)S(1)}, bf16[64,1024]{1,0:T(8,128)(2,1)S(1)}, u32[]{:S(2)}, u32[]{:S(2)}) collective-permute-start(bf16[64,1024]{1,0:T(8,128)(2,1)S(1)} %collective-permute-done.20), channel_id=1, source_target_pairs={{0,15},{1,0},{2,1},{3,2},{4,3},{5,4},{6,5},{7,6},{8,7},{9,8},{10,9... | collective-permute-start | bytes 393224 | tf_op jit(solution)/shard_map/ppermute | solution.py:60
  160.3 13.2 %collective-permute-start.24 = (bf16[64,1024]{1,0:T(8,128)(2,1)S(1)}, bf16[64,1024]{1,0:T(8,128)(2,1)S(1)}, u32[]{:S(2)}, u32[]{:S(2)}) collective-permute-start(bf16[64,1024]{1,0:T(8,128)(2,1)S(1)} %collective-permute-done.22), channel_id=1, source_target_pairs={{0,15},{1,0},{2,1},{3,2},{4,3},{5,4},{6,5},{7,6},{8,7},{9,8},{10,9... | collective-permute-start | bytes 393224 | tf_op jit(solution)/shard_map/ppermute | solution.py:60
  165.8 12.4 %collective-permute-start.25 = (bf16[64,1024]{1,0:T(8,128)(2,1)S(1)}, bf16[64,1024]{1,0:T(8,128)(2,1)S(1)}, u32[]{:S(2)}, u32[]{:S(2)}) collective-permute-start(bf16[64,1024]{1,0:T(8,128)(2,1)S(1)} %collective-permute-done.23), channel_id=1, source_target_pairs={{0,1},{1,2},{2,3},{3,4},{4,5},{5,6},{6,7},{7,8},{8,9},{9,10},{10,1... | collective-permute-start | bytes 393224 | tf_op jit(solution)/shard_map/ppermute | solution.py:60
  191.1 30.9 %all-to-all-start.1 = ((bf16[16,64,512]{2,1,0:T(8,128)(2,1)}), bf16[16,64,512]{2,1,0:T(8,128)(2,1)S(1)}, u32[]{:S(2)}, u32[]{:S(2)}) async-start(bf16[16,64,512]{2,1,0:T(8,128)(2,1)} %bitcast.18), calls=%async_computation.1 | async-start | bytes 2097152 | tf_op jit(solution)/shard_map/all_to_all | solution.py:63
  205.4 17.3 %collective-permute-start.28 = (bf16[1024,512]{1,0:T(8,128)(2,1)}, bf16[1024,512]{1,0:T(8,128)(2,1)}, u32[]{:S(2)}, u32[]{:S(2)}) collective-permute-start(bf16[1024,512]{1,0:T(8,128)(2,1)} %pad_maximum_fusion.3), channel_id=1, source_target_pairs={{0,16},{16,0},{32,48},{48,32},{64,80},{80,64},{96,112},{112,96},{1... | collective-permute-start | bytes 3145736 | tf_op jit(solution)/shard_map/ppermute | solution.py:57
  (26 other events, 147.2 us)
Sparse Core Ops, SparseCore 0:
  50.1 87.0 all-gather.2
  140.8 58.5 all-gather.4

commit v3 on v2

--- a/solution.py
+++ b/solution.py
@@ -64,7 +64,7 @@
 
     aligned = (chip + col) % 2 == 0
     moves = [
-        ((2 * r + c) * n_col + z, (2 * (r ^ 1) + c) * n_col + (z - 1) % n_col)
+        ((2 * r + c) * n_col + z, (2 * (r ^ 1) + c) * n_col + (z + 1) % n_col)
         for r in range(chips)
         for c in range(2)
         for z in range(n_col)
@@ -76,7 +76,7 @@
     acts = jnp.concatenate((gate_pre, up_pre), axis=1)
     spread, acts = lax.optimization_barrier((spread, acts))
     cot = exchange(spread)
-    w_next = hop(w_down, -1)
+    w_next = hop(w_down, 1)
     w_here = jnp.concatenate((w_down, swap(w_down)), axis=0)
 
     keep = lax.dynamic_slice_in_dim(acts, core * tokens, tokens, 0)
@@ -139,9 +139,9 @@
     above = below = mine
     for step in range(1, half + 1):
         above = hop(above, 1)
-        if step == half - 1:
-            below, gate_by, up_by, hidden = lax.optimization_barrier(
-                (below, gate_by, up_by, hidden)
+        if step == half:
+            above, gate_by, up_by, hidden = lax.optimization_barrier(
+                (above, gate_by, up_by, hidden)
             )
         if step < half:
             below = hop(below, -1)
@@ -159,14 +159,26 @@
     )
     sums = exchange(total).reshape(chips, tokens, -1)
     input_grad = jnp.sum(sums.astype(F32), axis=0).astype(BF16)
+    total, gate_grad, up_grad = lax.optimization_barrier(
+        (total.astype(BF16), gate_grad, up_grad)
+    )
+    sums = exchange(total).reshape(chips, tokens, -1)
+    input_grad = jnp.sum(sums.astype(F32), axis=0).astype(BF16)
     wd = lax.dot_general(hidden, cot_rows, TDIMS, preferred_element_type=F32)
     w_down_grad = (wd[:units] + swap(wd[units:].astype(BF16)).astype(F32)).astype(BF16)
-    wg = lax.dot_general(input_rows, gate_grad, TDIMS, preferred_element_type=F32)
-    wu = lax.dot_general(input_rows, up_grad, TDIMS, preferred_element_type=F32)
-    other = swap(jnp.concatenate((wg[:, units:], wu[:, units:]), axis=0).astype(BF16)).astype(F32)
-    width = wg.shape[0]
-    w_gate_grad = (wg[:, :units] + other[:width]).astype(BF16)
-    w_up_grad = (wu[:, :units] + other[width:]).astype(BF16)
+
+    def over_tokens(left, right):
+        return lax.dot_general(left, right, TDIMS, preferred_element_type=F32)
+
+    wd_other = swap(over_tokens(hidden[:, units:], cot_rows).astype(BF16))
+    wg_give = over_tokens(input_rows, gate_grad[:, units:]).astype(BF16)
+    wu_give = over_tokens(input_rows, up_grad[:, units:]).astype(BF16)
+    width = wg_give.shape[0]
+    other = swap(jnp.concatenate((wg_give, wu_give), axis=0))
+    w_down_grad = (over_tokens(hidden[:, :units], cot_rows) + wd_other.astype(F32)).astype(BF16)
+    w_gate_grad = over_tokens(input_rows, gate_grad[:, :units]) + other[:width].astype(F32)
+    w_up_grad = over_tokens(input_rows, up_grad[:, :units]) + other[width:].astype(F32)
+    w_gate_grad, w_up_grad = w_gate_grad.astype(BF16), w_up_grad.astype(BF16)
     return (input_grad, w_gate_grad, w_up_grad, w_down_grad)
 
 

time: 234 us -> 231 us (0.987)
  starting transfers between devices: 132 us -> 119 us
  waiting for transfers between devices: 47.9 us -> 57.4 us
  matrix products: 10.9 us -> 16.1 us
  other arithmetic: 16.7 us -> 12.6 us
    ppermute x23, starting transfers between devices: 84.5 us -> 73.2 us  [hop(): lax.ppermute(array, 'col', [(i, (i + step) % n_col) for i in range(n_col)])]
    ppermute x23, waiting for transfers between devices: 42.7 us -> 50 us  [hop(): lax.ppermute(array, 'col', [(i, (i + step) % n_col) for i in range(n_col)])]
    dot_general x3 -> x6, matrix products: 5.89 us -> 11.1 us  [over_tokens(): return lax.dot_general(left, right, TDIMS, preferred_element_type=F32)]
    ppermute x6, starting transfers between devices: 22.9 us -> 18.7 us  [swap(): return lax.ppermute(array, 'row', siblings)]
    convert_element_type x3 -> x0, other arithmetic: 3.96 us -> none  [the longest x1 1.65 us: local(): swap(jnp.concatenate((wg[:, units:], wu[:, units:]), axis=0).astype(BF16))]
    all_gather x1, waiting for transfers between devices: 2.11 us -> 5.76 us  [local(): lax.all_gather(rows, 'row', axis=0, tiled=True, axis_index_groups=groups)]
    unnamed x32 -> x24, local copies, waits for them, and re-layouts: 4.96 us -> 4.96 us
  transfers between devices with their start and end apart: 34 -> 34, of which waited for: 19 -> 18; matrix products, arithmetic and copies ran while one was open for 11% -> 11% of each run, Pallas kernels for 1% -> 1%
where the time goes in v3:
time: 231 us; the launch traced here: 230 us
  starting transfers between devices  119 us (52%)
  waiting for transfers between devices  57.4 us (25%)
  matrix products  16.1 us (7%)
  between operations  15.2 us (7%)
  other arithmetic  12.6 us (5%)
  local copies, waits for them, and re-layouts  7.37 us (3%)
    ppermute x23, starting transfers between devices, hop(): lax.ppermute(array, 'col', [(i, (i + step) % n_col) for i in range(n_col)])  73.2 us
    ppermute x23, waiting for transfers between devices, hop(): lax.ppermute(array, 'col', [(i, (i + step) % n_col) for i in range(n_col)])  50 us
    all_to_all x2, starting transfers between devices, exchange(): lax.all_to_all(array, 'row', 0, 0, axis_index_groups=groups, tiled=True)  26.1 us
    ppermute x6, starting transfers between devices, swap(): return lax.ppermute(array, 'row', siblings)  18.7 us
    dot_general x6, matrix products, over_tokens(): return lax.dot_general(left, right, TDIMS, preferred_element_type=F32)  11.1 us
    all_gather x1, waiting for transfers between devices, local(): lax.all_gather(rows, 'row', axis=0, tiled=True, axis_index_groups=groups)  5.76 us
    unnamed x24, local copies, waits for them, and re-layouts  4.96 us
  transfers between devices with their start and end apart: 34, of which 18 were waited for; matrix products, arithmetic and copies ran while one was open for 11% of the time, Pallas kernels for 1%

profile of v3, /device:TPU:1, one launch (start us, length us, event | category | flops | bytes accessed | tf_op | source)
XLA Modules:
  0.0 229.9 jit_solution(799528412019722998)
XLA Ops:
  11.0 18.0 %all-to-all-start = ((bf16[16,64,512]{2,1,0:T(8,128)(2,1)}), bf16[16,64,512]{2,1,0:T(8,128)(2,1)S(1)}, u32[]{:S(2)}, u32[]{:S(2)}) async-start(bf16[16,64,512]{2,1,0:T(8,128)(2,1)} %bitcast.1), calls=%async_computation | async-start | bytes 2097152 | tf_op jit(solution)/shard_map/all_to_all | solution.py:63
  29.1 3.7 %collective-permute-start.3 = (bf16[512,512]{1,0:T(8,128)(2,1)S(1)}, bf16[512,512]{1,0:T(8,128)(2,1)S(1)}, u32[]{:S(2)}, u32[]{:S(2)}) collective-permute-start(bf16[512,512]{1,0:T(8,128)(2,1)S(1)} %copy-done.8), channel_id=1, source_target_pairs={{0,16},{16,0},{32,48},{48,32},{64,80},{80,64},{96,112},{112,96},{1... | collective-permute-start | bytes 1572872 | tf_op jit(solution)/shard_map/ppermute | solution.py:57
  39.8 9.6 %collective-permute-done.1 = bf16[512,512]{1,0:T(8,128)(2,1)S(1)} collective-permute-done((bf16[512,512]{1,0:T(8,128)(2,1)S(1)}, bf16[512,512]{1,0:T(8,128)(2,1)S(1)}, u32[]{:S(2)}, u32[]{:S(2)}) %collective-permute-start.1) | collective-permute-done | bytes 524320 | tf_op jit(solution)/shard_map/ppermute | solution.py:60
  60.3 5.5 %collective-permute-start.5 = (bf16[64,1024]{1,0:T(8,128)(2,1)}, bf16[64,1024]{1,0:T(8,128)(2,1)}, u32[]{:S(2)}, u32[]{:S(2)}) collective-permute-start(bf16[64,1024]{1,0:T(8,128)(2,1)} %get-tuple-element.57), channel_id=1, source_target_pairs={{0,14},{1,15},{2,0},{3,1},{4,2},{5,3},{6,4},{7,5},{8,6},{9,7},{10,... | collective-permute-start | bytes 393224 | tf_op jit(solution)/shard_map/ppermute | solution.py:60
  65.8 4.7 %collective-permute-done.7 = bf16[64,1024]{1,0:T(8,128)(2,1)S(1)} collective-permute-done((bf16[64,1024]{1,0:T(8,128)(2,1)S(1)}, bf16[64,1024]{1,0:T(8,128)(2,1)S(1)}, u32[]{:S(2)}, u32[]{:S(2)}) %collective-permute-start.7) | collective-permute-done | bytes 131104 | tf_op jit(solution)/shard_map/ppermute | solution.py:60
  73.2 10.6 %collective-permute-done.8 = bf16[64,1024]{1,0:T(8,128)(2,1)S(1)} collective-permute-done((bf16[64,1024]{1,0:T(8,128)(2,1)S(1)}, bf16[64,1024]{1,0:T(8,128)(2,1)S(1)}, u32[]{:S(2)}, u32[]{:S(2)}) %collective-permute-start.8) | collective-permute-done | bytes 131104 | tf_op jit(solution)/shard_map/ppermute | solution.py:60
  89.1 5.5 %collective-permute-start.11 = (bf16[64,1024]{1,0:T(8,128)(2,1)S(1)}, bf16[64,1024]{1,0:T(8,128)(2,1)S(1)}, u32[]{:S(2)}, u32[]{:S(2)}) collective-permute-start(bf16[64,1024]{1,0:T(8,128)(2,1)S(1)} %get-tuple-element.33), channel_id=1, source_target_pairs={{0,14},{1,15},{2,0},{3,1},{4,2},{5,3},{6,4},{7,5},{8,6},{9,7},{10,... | collective-permute-start | bytes 393224 | tf_op jit(solution)/shard_map/ppermute | solution.py:60
  94.6 3.4 %collective-permute-done.9 = bf16[64,1024]{1,0:T(8,128)(2,1)S(1)} collective-permute-done((bf16[64,1024]{1,0:T(8,128)(2,1)}, bf16[64,1024]{1,0:T(8,128)(2,1)S(1)}, u32[]{:S(2)}, u32[]{:S(2)}) %collective-permute-start.9) | collective-permute-done | bytes 131104 | tf_op jit(solution)/shard_map/ppermute | solution.py:60
  98.0 3.8 %collective-permute-done.11 = bf16[64,1024]{1,0:T(8,128)(2,1)S(1)} collective-permute-done((bf16[64,1024]{1,0:T(8,128)(2,1)S(1)}, bf16[64,1024]{1,0:T(8,128)(2,1)S(1)}, u32[]{:S(2)}, u32[]{:S(2)}) %collective-permute-start.11) | collective-permute-done | bytes 131104 | tf_op jit(solution)/shard_map/ppermute | solution.py:60
  101.9 5.1 %collective-permute-start.12 = (bf16[64,1024]{1,0:T(8,128)(2,1)S(1)}, bf16[64,1024]{1,0:T(8,128)(2,1)S(1)}, u32[]{:S(2)}, u32[]{:S(2)}) collective-permute-start(bf16[64,1024]{1,0:T(8,128)(2,1)S(1)} %get-tuple-element.53), channel_id=1, source_target_pairs={{0,14},{1,15},{2,0},{3,1},{4,2},{5,3},{6,4},{7,5},{8,6},{9,7},{10,... | collective-permute-start | bytes 393224 | tf_op jit(solution)/shard_map/ppermute | solution.py:60
  109.0 4.1 %collective-permute-done.12 = bf16[64,1024]{1,0:T(8,128)(2,1)S(1)} collective-permute-done((bf16[64,1024]{1,0:T(8,128)(2,1)S(1)}, bf16[64,1024]{1,0:T(8,128)(2,1)S(1)}, u32[]{:S(2)}, u32[]{:S(2)}) %collective-permute-start.12) | collective-permute-done | bytes 131104 | tf_op jit(solution)/shard_map/ppermute | solution.py:60
  113.1 4.8 %collective-permute-done.10 = bf16[64,1024]{1,0:T(8,128)(2,1)S(1)} collective-permute-done((bf16[64,1024]{1,0:T(8,128)(2,1)S(1)}, bf16[64,1024]{1,0:T(8,128)(2,1)S(1)}, u32[]{:S(2)}, u32[]{:S(2)}) %collective-permute-start.10) | collective-permute-done | bytes 131104 | tf_op jit(solution)/shard_map/ppermute | solution.py:60
  120.1 4.6 %collective-permute-start.14 = (bf16[64,1024]{1,0:T(8,128)(2,1)S(1)}, bf16[64,1024]{1,0:T(8,128)(2,1)S(1)}, u32[]{:S(2)}, u32[]{:S(2)}) collective-permute-start(bf16[64,1024]{1,0:T(8,128)(2,1)S(1)} %get-tuple-element.47), channel_id=1, source_target_pairs={{0,15},{1,0},{2,1},{3,2},{4,3},{5,4},{6,5},{7,6},{8,7},{9,8},{10,9... | collective-permute-start | bytes 393224 | tf_op jit(solution)/shard_map/ppermute | solution.py:60
  129.2 4.6 %collective-permute-start.16 = (bf16[64,1024]{1,0:T(8,128)(2,1)S(1)}, bf16[64,1024]{1,0:T(8,128)(2,1)S(1)}, u32[]{:S(2)}, u32[]{:S(2)}) collective-permute-start(bf16[64,1024]{1,0:T(8,128)(2,1)S(1)} %collective-permute-done.14), channel_id=1, source_target_pairs={{0,15},{1,0},{2,1},{3,2},{4,3},{5,4},{6,5},{7,6},{8,7},{9,8},{10,9... | collective-permute-start | bytes 393224 | tf_op jit(solution)/shard_map/ppermute | solution.py:60
  133.9 3.1 %collective-permute-done.15 = bf16[64,1024]{1,0:T(8,128)(2,1)S(1)} collective-permute-done((bf16[64,1024]{1,0:T(8,128)(2,1)S(1)}, bf16[64,1024]{1,0:T(8,128)(2,1)S(1)}, u32[]{:S(2)}, u32[]{:S(2)}) %collective-permute-start.15) | collective-permute-done | bytes 131104 | tf_op jit(solution)/shard_map/ppermute | solution.py:60
  138.9 4.6 %collective-permute-start.18 = (bf16[64,1024]{1,0:T(8,128)(2,1)S(1)}, bf16[64,1024]{1,0:T(8,128)(2,1)S(1)}, u32[]{:S(2)}, u32[]{:S(2)}) collective-permute-start(bf16[64,1024]{1,0:T(8,128)(2,1)S(1)} %collective-permute-done.16), channel_id=1, source_target_pairs={{0,15},{1,0},{2,1},{3,2},{4,3},{5,4},{6,5},{7,6},{8,7},{9,8},{10,9... | collective-permute-start | bytes 393224 | tf_op jit(solution)/shard_map/ppermute | solution.py:60
  145.8 4.6 %collective-permute-start.20 = (bf16[64,1024]{1,0:T(8,128)(2,1)S(1)}, bf16[64,1024]{1,0:T(8,128)(2,1)S(1)}, u32[]{:S(2)}, u32[]{:S(2)}) collective-permute-start(bf16[64,1024]{1,0:T(8,128)(2,1)S(1)} %collective-permute-done.18), channel_id=1, source_target_pairs={{0,15},{1,0},{2,1},{3,2},{4,3},{5,4},{6,5},{7,6},{8,7},{9,8},{10,9... | collective-permute-start | bytes 393224 | tf_op jit(solution)/shard_map/ppermute | solution.py:60
  152.7 4.6 %collective-permute-start.22 = (bf16[64,1024]{1,0:T(8,128)(2,1)S(1)}, bf16[64,1024]{1,0:T(8,128)(2,1)S(1)}, u32[]{:S(2)}, u32[]{:S(2)}) collective-permute-start(bf16[64,1024]{1,0:T(8,128)(2,1)S(1)} %collective-permute-done.20), channel_id=1, source_target_pairs={{0,15},{1,0},{2,1},{3,2},{4,3},{5,4},{6,5},{7,6},{8,7},{9,8},{10,9... | collective-permute-start | bytes 393224 | tf_op jit(solution)/shard_map/ppermute | solution.py:60
  160.4 4.9 %collective-permute-start.24 = (bf16[64,1024]{1,0:T(8,128)(2,1)S(1)}, bf16[64,1024]{1,0:T(8,128)(2,1)S(1)}, u32[]{:S(2)}, u32[]{:S(2)}) collective-permute-start(bf16[64,1024]{1,0:T(8,128)(2,1)S(1)} %collective-permute-done.22), channel_id=1, source_target_pairs={{0,15},{1,0},{2,1},{3,2},{4,3},{5,4},{6,5},{7,6},{8,7},{9,8},{10,9... | collective-permute-start | bytes 393224 | tf_op jit(solution)/shard_map/ppermute | solution.py:60
  168.5 4.6 %collective-permute-start.26 = (bf16[64,1024]{1,0:T(8,128)(2,1)S(1)}, bf16[64,1024]{1,0:T(8,128)(2,1)S(1)}, u32[]{:S(2)}, u32[]{:S(2)}) collective-permute-start(bf16[64,1024]{1,0:T(8,128)(2,1)S(1)} %collective-permute-done.24), channel_id=1, source_target_pairs={{0,15},{1,0},{2,1},{3,2},{4,3},{5,4},{6,5},{7,6},{8,7},{9,8},{10,9... | collective-permute-start | bytes 393224 | tf_op jit(solution)/shard_map/ppermute | solution.py:60
  187.2 8.1 %all-to-all-start.1 = ((bf16[16,64,512]{2,1,0:T(8,128)(2,1)}), bf16[16,64,512]{2,1,0:T(8,128)(2,1)S(1)}, u32[]{:S(2)}, u32[]{:S(2)}) async-start(bf16[16,64,512]{2,1,0:T(8,128)(2,1)} %bitcast.15), calls=%async_computation.1 | async-start | bytes 2097152 | tf_op jit(solution)/shard_map/all_to_all | solution.py:63
  195.4 5.8 %all-gather.5.cloned.1.call-done = bf16[1024,1024]{1,0:T(8,128)(2,1)} async-done(((bf16[64,1024]{1,0:T(8,128)(2,1)}), bf16[1024,1024]{1,0:T(8,128)(2,1)}) %all-gather.5.cloned.1.call-update) | async-done | bytes 2097168 | tf_op jit(solution)/shard_map/all_gather | solution.py:127
  205.8 6.4 %collective-permute-start.28 = (bf16[1024,512]{1,0:T(8,128)(2,1)}, bf16[1024,512]{1,0:T(8,128)(2,1)}, u32[]{:S(2)}, u32[]{:S(2)}) collective-permute-start(bf16[1024,512]{1,0:T(8,128)(2,1)} %pad_maximum_fusion.3), channel_id=1, source_target_pairs={{0,16},{16,0},{32,48},{48,32},{64,80},{80,64},{96,112},{112,96},{1... | collective-permute-start | bytes 3145736 | tf_op jit(solution)/shard_map/ppermute | solution.py:57
  219.2 3.9 %add_convert_fusion.2 = (bf16[512,512]{1,0:T(8,128)(2,1)}, bf16[512,512]{1,0:T(8,128)(2,1)}) fusion(bf16[1024,512]{1,0:T(8,128)(2,1)} %collective-permute-done.28, f32[512,512]{1,0:T(8,128)} %fusion.13, bf16[1024,1024]{1,0:T(8,128)(2,1)} %copy-done.4, bf16[1024,1024]{1,0:T(8,128)(2,1)} %all-gather.5.cloned.1.call-done), kind=kOutput, calls=%fused_computation.21 | convolution fusion | flops 538443776 | bytes 5242880 | tf_op jit(solution)/shard_map/dot_general | solution.py:171
  (115 shorter events, 76.2 us)
Async XLA Ops:
  11.0 38.5 %all-to-all-start = ((bf16[16,64,512]{2,1,0:T(8,128)(2,1)}), bf16[16,64,512]{2,1,0:T(8,128)(2,1)S(1)}, u32[]{:S(2)}, u32[]{:S(2)}) async-start(bf16[16,64,512]{2,1,0:T(8,128)(2,1)} %bitcast.1), calls=%async_computation | async-start | bytes 2097152 | tf_op jit(solution)/shard_map/all_to_all | solution.py:63
  29.0 147.7 %all-gather.3.cloned.1.call-start = ((), (), s32[]{:S(2)}) async-start(), calls=%async_computation.2 | async-start | bytes 4456448 | tf_op jit(solution)/shard_map/all_gather | solution.py:86
  29.1 9.7 %collective-permute-start.3 = (bf16[512,512]{1,0:T(8,128)(2,1)S(1)}, bf16[512,512]{1,0:T(8,128)(2,1)S(1)}, u32[]{:S(2)}, u32[]{:S(2)}) collective-permute-start(bf16[512,512]{1,0:T(8,128)(2,1)S(1)} %copy-done.8), channel_id=1, source_target_pairs={{0,16},{16,0},{32,48},{48,32},{64,80},{80,64},{96,112},{112,96},{1... | collective-permute-start | bytes 1572872 | tf_op jit(solution)/shard_map/ppermute | solution.py:57
  32.8 16.6 %collective-permute-start.1 = (bf16[512,512]{1,0:T(8,128)(2,1)S(1)}, bf16[512,512]{1,0:T(8,128)(2,1)S(1)}, u32[]{:S(2)}, u32[]{:S(2)}) collective-permute-start(bf16[512,512]{1,0:T(8,128)(2,1)S(1)} %copy-done.8), channel_id=1, source_target_pairs={{0,1},{1,2},{2,3},{3,4},{4,5},{5,6},{6,7},{7,8},{8,9},{9,10},{10,1... | collective-permute-start | bytes 1572872 | tf_op jit(solution)/shard_map/ppermute | solution.py:60
  49.5 151.6 %all-gather.5.cloned.1.call-start = ((), (), s32[]{:S(2)}) async-start(), calls=%async_computation.3 | async-start | bytes 2228224 | tf_op jit(solution)/shard_map/all_gather | solution.py:127
  55.6 31.7 %collective-permute-start.6 = (bf16[1024,512]{1,0:T(8,128)(2,1)S(1)}, bf16[1024,512]{1,0:T(8,128)(2,1)S(1)}, u32[]{:S(2)}, u32[]{:S(2)}) collective-permute-start(bf16[1024,512]{1,0:T(8,128)(2,1)S(1)} %pad_maximum_fusion.2), channel_id=1, source_target_pairs={{0,16},{16,0},{32,48},{48,32},{64,80},{80,64},{96,112},{112,96},{1... | collective-permute-start | bytes 3145736 | tf_op jit(solution)/shard_map/ppermute | solution.py:57
  58.3 12.2 %collective-permute-start.7 = (bf16[64,1024]{1,0:T(8,128)(2,1)S(1)}, bf16[64,1024]{1,0:T(8,128)(2,1)S(1)}, u32[]{:S(2)}, u32[]{:S(2)}) collective-permute-start(bf16[64,1024]{1,0:T(8,128)(2,1)S(1)} %get-tuple-element.56), channel_id=1, source_target_pairs={{0,2},{1,3},{2,4},{3,5},{4,6},{5,7},{6,8},{7,9},{8,10},{9,11},{10,... | collective-permute-start | bytes 393224 | tf_op jit(solution)/shard_map/ppermute | solution.py:60
  60.3 12.9 %collective-permute-start.5 = (bf16[64,1024]{1,0:T(8,128)(2,1)}, bf16[64,1024]{1,0:T(8,128)(2,1)}, u32[]{:S(2)}, u32[]{:S(2)}) collective-permute-start(bf16[64,1024]{1,0:T(8,128)(2,1)} %get-tuple-element.57), channel_id=1, source_target_pairs={{0,14},{1,15},{2,0},{3,1},{4,2},{5,3},{6,4},{7,5},{8,6},{9,7},{10,... | collective-permute-start | bytes 393224 | tf_op jit(solution)/shard_map/ppermute | solution.py:60
  70.5 13.3 %collective-permute-start.8 = (bf16[64,1024]{1,0:T(8,128)(2,1)S(1)}, bf16[64,1024]{1,0:T(8,128)(2,1)S(1)}, u32[]{:S(2)}, u32[]{:S(2)}) collective-permute-start(bf16[64,1024]{1,0:T(8,128)(2,1)S(1)} %add_convert_fusion.8), channel_id=1, source_target_pairs={{0,2},{1,3},{2,4},{3,5},{4,6},{5,7},{6,8},{7,9},{8,10},{9,11},{10,... | collective-permute-start | bytes 393224 | tf_op jit(solution)/shard_map/ppermute | solution.py:60
  85.4 12.6 %collective-permute-start.9 = (bf16[64,1024]{1,0:T(8,128)(2,1)}, bf16[64,1024]{1,0:T(8,128)(2,1)S(1)}, u32[]{:S(2)}, u32[]{:S(2)}) collective-permute-start(bf16[64,1024]{1,0:T(8,128)(2,1)} %get-tuple-element.54), channel_id=1, source_target_pairs={{0,2},{1,3},{2,4},{3,5},{4,6},{5,7},{6,8},{7,9},{8,10},{9,11},{10,... | collective-permute-start | bytes 393224 | tf_op jit(solution)/shard_map/ppermute | solution.py:60
  89.1 12.8 %collective-permute-start.11 = (bf16[64,1024]{1,0:T(8,128)(2,1)S(1)}, bf16[64,1024]{1,0:T(8,128)(2,1)S(1)}, u32[]{:S(2)}, u32[]{:S(2)}) collective-permute-start(bf16[64,1024]{1,0:T(8,128)(2,1)S(1)} %get-tuple-element.33), channel_id=1, source_target_pairs={{0,14},{1,15},{2,0},{3,1},{4,2},{5,3},{6,4},{7,5},{8,6},{9,7},{10,... | collective-permute-start | bytes 393224 | tf_op jit(solution)/shard_map/ppermute | solution.py:60
  101.9 11.2 %collective-permute-start.12 = (bf16[64,1024]{1,0:T(8,128)(2,1)S(1)}, bf16[64,1024]{1,0:T(8,128)(2,1)S(1)}, u32[]{:S(2)}, u32[]{:S(2)}) collective-permute-start(bf16[64,1024]{1,0:T(8,128)(2,1)S(1)} %get-tuple-element.53), channel_id=1, source_target_pairs={{0,14},{1,15},{2,0},{3,1},{4,2},{5,3},{6,4},{7,5},{8,6},{9,7},{10,... | collective-permute-start | bytes 393224 | tf_op jit(solution)/shard_map/ppermute | solution.py:60
  107.0 10.9 %collective-permute-start.10 = (bf16[64,1024]{1,0:T(8,128)(2,1)S(1)}, bf16[64,1024]{1,0:T(8,128)(2,1)S(1)}, u32[]{:S(2)}, u32[]{:S(2)}) collective-permute-start(bf16[64,1024]{1,0:T(8,128)(2,1)S(1)} %get-tuple-element.52), channel_id=1, source_target_pairs={{0,2},{1,3},{2,4},{3,5},{4,6},{5,7},{6,8},{7,9},{8,10},{9,11},{10,... | collective-permute-start | bytes 393224 | tf_op jit(solution)/shard_map/ppermute | solution.py:60
  118.2 9.1 %collective-permute-start.13 = (bf16[64,1024]{1,0:T(8,128)(2,1)S(1)}, bf16[64,1024]{1,0:T(8,128)(2,1)S(1)}, u32[]{:S(2)}, u32[]{:S(2)}) collective-permute-start(bf16[64,1024]{1,0:T(8,128)(2,1)S(1)} %get-tuple-element.47), channel_id=1, source_target_pairs={{0,1},{1,2},{2,3},{3,4},{4,5},{5,6},{6,7},{7,8},{8,9},{9,10},{10,1... | collective-permute-start | bytes 393224 | tf_op jit(solution)/shard_map/ppermute | solution.py:60
  120.1 9.1 %collective-permute-start.14 = (bf16[64,1024]{1,0:T(8,128)(2,1)S(1)}, bf16[64,1024]{1,0:T(8,128)(2,1)S(1)}, u32[]{:S(2)}, u32[]{:S(2)}) collective-permute-start(bf16[64,1024]{1,0:T(8,128)(2,1)S(1)} %get-tuple-element.47), channel_id=1, source_target_pairs={{0,15},{1,0},{2,1},{3,2},{4,3},{5,4},{6,5},{7,6},{8,7},{9,8},{10,9... | collective-permute-start | bytes 393224 | tf_op jit(solution)/shard_map/ppermute | solution.py:60
  127.3 9.6 %collective-permute-start.15 = (bf16[64,1024]{1,0:T(8,128)(2,1)S(1)}, bf16[64,1024]{1,0:T(8,128)(2,1)S(1)}, u32[]{:S(2)}, u32[]{:S(2)}) collective-permute-start(bf16[64,1024]{1,0:T(8,128)(2,1)S(1)} %collective-permute-done.13), channel_id=1, source_target_pairs={{0,1},{1,2},{2,3},{3,4},{4,5},{5,6},{6,7},{7,8},{8,9},{9,10},{10,1... | collective-permute-start | bytes 393224 | tf_op jit(solution)/shard_map/ppermute | solution.py:60
  129.2 9.6 %collective-permute-start.16 = (bf16[64,1024]{1,0:T(8,128)(2,1)S(1)}, bf16[64,1024]{1,0:T(8,128)(2,1)S(1)}, u32[]{:S(2)}, u32[]{:S(2)}) collective-permute-start(bf16[64,1024]{1,0:T(8,128)(2,1)S(1)} %collective-permute-done.14), channel_id=1, source_target_pairs={{0,15},{1,0},{2,1},{3,2},{4,3},{5,4},{6,5},{7,6},{8,7},{9,8},{10,9... | collective-permute-start | bytes 393224 | tf_op jit(solution)/shard_map/ppermute | solution.py:60
  150.8 7.7 %collective-permute-start.21 = (bf16[64,1024]{1,0:T(8,128)(2,1)S(1)}, bf16[64,1024]{1,0:T(8,128)(2,1)S(1)}, u32[]{:S(2)}, u32[]{:S(2)}) collective-permute-start(bf16[64,1024]{1,0:T(8,128)(2,1)S(1)} %collective-permute-done.19), channel_id=1, source_target_pairs={{0,1},{1,2},{2,3},{3,4},{4,5},{5,6},{6,7},{7,8},{8,9},{9,10},{10,1... | collective-permute-start | bytes 393224 | tf_op jit(solution)/shard_map/ppermute | solution.py:60
  152.7 7.7 %collective-permute-start.22 = (bf16[64,1024]{1,0:T(8,128)(2,1)S(1)}, bf16[64,1024]{1,0:T(8,128)(2,1)S(1)}, u32[]{:S(2)}, u32[]{:S(2)}) collective-permute-start(bf16[64,1024]{1,0:T(8,128)(2,1)S(1)} %collective-permute-done.20), channel_id=1, source_target_pairs={{0,15},{1,0},{2,1},{3,2},{4,3},{5,4},{6,5},{7,6},{8,7},{9,8},{10,9... | collective-permute-start | bytes 393224 | tf_op jit(solution)/shard_map/ppermute | solution.py:60
  158.5 8.1 %collective-permute-start.23 = (bf16[64,1024]{1,0:T(8,128)(2,1)S(1)}, bf16[64,1024]{1,0:T(8,128)(2,1)S(1)}, u32[]{:S(2)}, u32[]{:S(2)}) collective-permute-start(bf16[64,1024]{1,0:T(8,128)(2,1)S(1)} %collective-permute-done.21), channel_id=1, source_target_pairs={{0,1},{1,2},{2,3},{3,4},{4,5},{5,6},{6,7},{7,8},{8,9},{9,10},{10,1... | collective-permute-start | bytes 393224 | tf_op jit(solution)/shard_map/ppermute | solution.py:60
  160.4 8.0 %collective-permute-start.24 = (bf16[64,1024]{1,0:T(8,128)(2,1)S(1)}, bf16[64,1024]{1,0:T(8,128)(2,1)S(1)}, u32[]{:S(2)}, u32[]{:S(2)}) collective-permute-start(bf16[64,1024]{1,0:T(8,128)(2,1)S(1)} %collective-permute-done.22), channel_id=1, source_target_pairs={{0,15},{1,0},{2,1},{3,2},{4,3},{5,4},{6,5},{7,6},{8,7},{9,8},{10,9... | collective-permute-start | bytes 393224 | tf_op jit(solution)/shard_map/ppermute | solution.py:60
  173.4 7.8 %collective-permute-start.27 = (bf16[64,1024]{1,0:T(8,128)(2,1)S(1)}, bf16[64,1024]{1,0:T(8,128)(2,1)S(1)}, u32[]{:S(2)}, u32[]{:S(2)}) collective-permute-start(bf16[64,1024]{1,0:T(8,128)(2,1)S(1)} %collective-permute-done.25), channel_id=1, source_target_pairs={{0,1},{1,2},{2,3},{3,4},{4,5},{5,6},{6,7},{7,8},{8,9},{9,10},{10,1... | collective-permute-start | bytes 393224 | tf_op jit(solution)/shard_map/ppermute | solution.py:60
  187.2 31.2 %all-to-all-start.1 = ((bf16[16,64,512]{2,1,0:T(8,128)(2,1)}), bf16[16,64,512]{2,1,0:T(8,128)(2,1)S(1)}, u32[]{:S(2)}, u32[]{:S(2)}) async-start(bf16[16,64,512]{2,1,0:T(8,128)(2,1)} %bitcast.15), calls=%async_computation.1 | async-start | bytes 2097152 | tf_op jit(solution)/shard_map/all_to_all | solution.py:63
  205.8 13.4 %collective-permute-start.28 = (bf16[1024,512]{1,0:T(8,128)(2,1)}, bf16[1024,512]{1,0:T(8,128)(2,1)}, u32[]{:S(2)}, u32[]{:S(2)}) collective-permute-start(bf16[1024,512]{1,0:T(8,128)(2,1)} %pad_maximum_fusion.3), channel_id=1, source_target_pairs={{0,16},{16,0},{32,48},{48,32},{64,80},{80,64},{96,112},{112,96},{1... | collective-permute-start | bytes 3145736 | tf_op jit(solution)/shard_map/ppermute | solution.py:57
  (22 other events, 129.1 us)
Sparse Core Ops, SparseCore 0:
  49.6 88.1 all-gather.2
  141.4 59.6 all-gather.4

commit v4 on v3

--- a/solution.py
+++ b/solution.py
@@ -8,7 +8,6 @@
 F32 = jnp.float32
 BF16 = jnp.bfloat16
 NDIMS = (((1,), (1,)), ((), ()))
-TDIMS = (((0,), (0,)), ((), ()))
 
 
 def factors_kernel(acts_ref, gate_ref, up_ref, hidden_ref):
@@ -19,7 +18,7 @@
         sigma = jax.nn.sigmoid(gate_val)
         active = gate_val * sigma
         at = slice(i * units, (i + 1) * units)
-        hidden_ref[:, at] = (active * up_val).astype(BF16)
+        hidden_ref[at, :] = (active * up_val).T.astype(BF16)
         up_ref[:, at] = active.astype(BF16)
         gate_ref[:, at] = (up_val * sigma * (1.0 + gate_val * (1.0 - sigma))).astype(BF16)
 
@@ -32,8 +31,8 @@
         factors_kernel,
         grid=(rows // block,),
         in_specs=[pl.BlockSpec((block, 4 * units), lambda i: (i, 0))],
-        out_specs=[spec] * 3,
-        out_shape=[out] * 3,
+        out_specs=[spec, spec, pl.BlockSpec((2 * units, block), lambda i: (0, i))],
+        out_shape=[out, out, jax.ShapeDtypeStruct((2 * units, rows), BF16)],
         compiler_params=pltpu.CompilerParams(vmem_limit_bytes=16 * 1024 * 1024),
         cost_estimate=pl.CostEstimate(
             flops=12 * rows * 2 * units,
@@ -159,23 +158,17 @@
     )
     sums = exchange(total).reshape(chips, tokens, -1)
     input_grad = jnp.sum(sums.astype(F32), axis=0).astype(BF16)
-    total, gate_grad, up_grad = lax.optimization_barrier(
-        (total.astype(BF16), gate_grad, up_grad)
-    )
-    sums = exchange(total).reshape(chips, tokens, -1)
-    input_grad = jnp.sum(sums.astype(F32), axis=0).astype(BF16)
-    wd = lax.dot_general(hidden, cot_rows, TDIMS, preferred_element_type=F32)
-    w_down_grad = (wd[:units] + swap(wd[units:].astype(BF16)).astype(F32)).astype(BF16)
 
     def over_tokens(left, right):
-        return lax.dot_general(left, right, TDIMS, preferred_element_type=F32)
+        return jnp.dot(left, right, preferred_element_type=F32)
 
-    wd_other = swap(over_tokens(hidden[:, units:], cot_rows).astype(BF16))
+    input_rows = lax.optimization_barrier(input_rows.T)
+    wd_other = swap(over_tokens(hidden[units:], cot_rows).astype(BF16))
     wg_give = over_tokens(input_rows, gate_grad[:, units:]).astype(BF16)
     wu_give = over_tokens(input_rows, up_grad[:, units:]).astype(BF16)
     width = wg_give.shape[0]
     other = swap(jnp.concatenate((wg_give, wu_give), axis=0))
-    w_down_grad = (over_tokens(hidden[:, :units], cot_rows) + wd_other.astype(F32)).astype(BF16)
+    w_down_grad = (over_tokens(hidden[:units], cot_rows) + wd_other.astype(F32)).astype(BF16)
     w_gate_grad = over_tokens(input_rows, gate_grad[:, :units]) + other[:width].astype(F32)
     w_up_grad = over_tokens(input_rows, up_grad[:, :units]) + other[width:].astype(F32)
     w_gate_grad, w_up_grad = w_gate_grad.astype(BF16), w_up_grad.astype(BF16)

time: 231 us -> 235 us (1.017)
  starting transfers between devices: 119 us -> 123 us
    ppermute x6, starting transfers between devices: 18.7 us -> 24.5 us  [swap(): return lax.ppermute(array, 'row', siblings)]
    all_gather x1, waiting for transfers between devices: 5.76 us -> 0.02 us  [local(): lax.all_gather(rows, 'row', axis=0, tiled=True, axis_index_groups=groups)]
    ppermute x23, waiting for transfers between devices: 50 us -> 54.2 us  [hop(): lax.ppermute(array, 'col', [(i, (i + step) % n_col) for i in range(n_col)])]
    transpose x0 -> x1, local copies, waits for them, and re-layouts: none -> 2.99 us  [local(): input_rows = lax.optimization_barrier(input_rows.T)]
    unnamed x24 -> x22, local copies, waits for them, and re-layouts: 4.96 us -> 3.27 us
  transfers between devices with their start and end apart: 34 -> 34, of which waited for: 18 -> 17; matrix products, arithmetic and copies ran while one was open for 11% -> 10% of each run, Pallas kernels for 1% -> 1%
where the time goes in v4:
time: 235 us; the launch traced here: 233 us
  starting transfers between devices  123 us (52%)
  waiting for transfers between devices  55.9 us (24%)
  matrix products  16 us (7%)
  between operations  15.2 us (6%)
  other arithmetic  12.8 us (5%)
  local copies, waits for them, and re-layouts  8 us (3%)
  Pallas kernels  2.82 us (1%)
    ppermute x23, starting transfers between devices, hop(): lax.ppermute(array, 'col', [(i, (i + step) % n_col) for i in range(n_col)])  72.9 us
    ppermute x23, waiting for transfers between devices, hop(): lax.ppermute(array, 'col', [(i, (i + step) % n_col) for i in range(n_col)])  54.2 us
    ppermute x6, starting transfers between devices, swap(): return lax.ppermute(array, 'row', siblings)  24.5 us
    all_to_all x2, starting transfers between devices, exchange(): lax.all_to_all(array, 'row', 0, 0, axis_index_groups=groups, tiled=True)  24.2 us
    dot_general x6, matrix products, over_tokens(): return jnp.dot(left, right, preferred_element_type=F32)  11 us
  transfers between devices with their start and end apart: 34, of which 17 were waited for; matrix products, arithmetic and copies ran while one was open for 10% of the time, Pallas kernels for 1%

profile of v4, /device:TPU:1, one launch (start us, length us, event | category | flops | bytes accessed | tf_op | source)
XLA Modules:
  0.0 233.4 jit_solution(7163946095108389464)
XLA Ops:
  12.6 18.0 %all-to-all-start = ((bf16[16,64,512]{2,1,0:T(8,128)(2,1)}), bf16[16,64,512]{2,1,0:T(8,128)(2,1)S(1)}, u32[]{:S(2)}, u32[]{:S(2)}) async-start(bf16[16,64,512]{2,1,0:T(8,128)(2,1)} %bitcast.1), calls=%async_computation | async-start | bytes 2097152 | tf_op jit(solution)/shard_map/all_to_all | solution.py:62
  30.7 3.7 %collective-permute-start.3 = (bf16[512,512]{1,0:T(8,128)(2,1)S(1)}, bf16[512,512]{1,0:T(8,128)(2,1)S(1)}, u32[]{:S(2)}, u32[]{:S(2)}) collective-permute-start(bf16[512,512]{1,0:T(8,128)(2,1)S(1)} %copy-done.10), channel_id=1, source_target_pairs={{0,16},{16,0},{32,48},{48,32},{64,80},{80,64},{96,112},{112,96},{1... | collective-permute-start | bytes 1572872 | tf_op jit(solution)/shard_map/ppermute | solution.py:56
  41.4 9.8 %collective-permute-done.1 = bf16[512,512]{1,0:T(8,128)(2,1)S(1)} collective-permute-done((bf16[512,512]{1,0:T(8,128)(2,1)S(1)}, bf16[512,512]{1,0:T(8,128)(2,1)S(1)}, u32[]{:S(2)}, u32[]{:S(2)}) %collective-permute-start.1) | collective-permute-done | bytes 524320 | tf_op jit(solution)/shard_map/ppermute | solution.py:59
  61.2 5.5 %collective-permute-start.5 = (bf16[64,1024]{1,0:T(8,128)(2,1)S(1)}, bf16[64,1024]{1,0:T(8,128)(2,1)}, u32[]{:S(2)}, u32[]{:S(2)}) collective-permute-start(bf16[64,1024]{1,0:T(8,128)(2,1)S(1)} %get-tuple-element.57), channel_id=1, source_target_pairs={{0,14},{1,15},{2,0},{3,1},{4,2},{5,3},{6,4},{7,5},{8,6},{9,7},{10,... | collective-permute-start | bytes 393224 | tf_op jit(solution)/shard_map/ppermute | solution.py:59
  66.6 4.7 %collective-permute-done.7 = bf16[64,1024]{1,0:T(8,128)(2,1)S(1)} collective-permute-done((bf16[64,1024]{1,0:T(8,128)(2,1)S(1)}, bf16[64,1024]{1,0:T(8,128)(2,1)S(1)}, u32[]{:S(2)}, u32[]{:S(2)}) %collective-permute-start.7) | collective-permute-done | bytes 131104 | tf_op jit(solution)/shard_map/ppermute | solution.py:59
  73.4 6.6 %collective-permute-done.8 = bf16[64,1024]{1,0:T(8,128)(2,1)S(1)} collective-permute-done((bf16[64,1024]{1,0:T(8,128)(2,1)S(1)}, bf16[64,1024]{1,0:T(8,128)(2,1)S(1)}, u32[]{:S(2)}, u32[]{:S(2)}) %collective-permute-start.8) | collective-permute-done | bytes 131104 | tf_op jit(solution)/shard_map/ppermute | solution.py:59
  85.2 4.8 %collective-permute-start.11 = (bf16[64,1024]{1,0:T(8,128)(2,1)S(1)}, bf16[64,1024]{1,0:T(8,128)(2,1)S(1)}, u32[]{:S(2)}, u32[]{:S(2)}) collective-permute-start(bf16[64,1024]{1,0:T(8,128)(2,1)S(1)} %get-tuple-element.33), channel_id=1, source_target_pairs={{0,14},{1,15},{2,0},{3,1},{4,2},{5,3},{6,4},{7,5},{8,6},{9,7},{10,... | collective-permute-start | bytes 393224 | tf_op jit(solution)/shard_map/ppermute | solution.py:59
  90.1 4.6 %collective-permute-done.11 = bf16[64,1024]{1,0:T(8,128)(2,1)S(1)} collective-permute-done((bf16[64,1024]{1,0:T(8,128)(2,1)S(1)}, bf16[64,1024]{1,0:T(8,128)(2,1)S(1)}, u32[]{:S(2)}, u32[]{:S(2)}) %collective-permute-start.11) | collective-permute-done | bytes 131104 | tf_op jit(solution)/shard_map/ppermute | solution.py:59
  94.8 3.2 %collective-permute-start.12 = (bf16[64,1024]{1,0:T(8,128)(2,1)S(1)}, bf16[64,1024]{1,0:T(8,128)(2,1)S(1)}, u32[]{:S(2)}, u32[]{:S(2)}) collective-permute-start(bf16[64,1024]{1,0:T(8,128)(2,1)S(1)} %get-tuple-element.53), channel_id=1, source_target_pairs={{0,14},{1,15},{2,0},{3,1},{4,2},{5,3},{6,4},{7,5},{8,6},{9,7},{10,... | collective-permute-start | bytes 393224 | tf_op jit(solution)/shard_map/ppermute | solution.py:59
  103.7 5.8 %collective-permute-done.10 = bf16[64,1024]{1,0:T(8,128)(2,1)S(1)} collective-permute-done((bf16[64,1024]{1,0:T(8,128)(2,1)S(1)}, bf16[64,1024]{1,0:T(8,128)(2,1)S(1)}, u32[]{:S(2)}, u32[]{:S(2)}) %collective-permute-start.10) | collective-permute-done | bytes 131104 | tf_op jit(solution)/shard_map/ppermute | solution.py:59
  111.7 4.6 %collective-permute-start.14 = (bf16[64,1024]{1,0:T(8,128)(2,1)S(1)}, bf16[64,1024]{1,0:T(8,128)(2,1)S(1)}, u32[]{:S(2)}, u32[]{:S(2)}) collective-permute-start(bf16[64,1024]{1,0:T(8,128)(2,1)S(1)} %get-tuple-element.47), channel_id=1, source_target_pairs={{0,15},{1,0},{2,1},{3,2},{4,3},{5,4},{6,5},{7,6},{8,7},{9,8},{10,9... | collective-permute-start | bytes 393224 | tf_op jit(solution)/shard_map/ppermute | solution.py:59
  120.7 4.6 %collective-permute-start.16 = (bf16[64,1024]{1,0:T(8,128)(2,1)S(1)}, bf16[64,1024]{1,0:T(8,128)(2,1)S(1)}, u32[]{:S(2)}, u32[]{:S(2)}) collective-permute-start(bf16[64,1024]{1,0:T(8,128)(2,1)S(1)} %collective-permute-done.14), channel_id=1, source_target_pairs={{0,15},{1,0},{2,1},{3,2},{4,3},{5,4},{6,5},{7,6},{8,7},{9,8},{10,9... | collective-permute-start | bytes 393224 | tf_op jit(solution)/shard_map/ppermute | solution.py:59
  125.4 3.7 %collective-permute-done.15 = bf16[64,1024]{1,0:T(8,128)(2,1)S(1)} collective-permute-done((bf16[64,1024]{1,0:T(8,128)(2,1)S(1)}, bf16[64,1024]{1,0:T(8,128)(2,1)S(1)}, u32[]{:S(2)}, u32[]{:S(2)}) %collective-permute-start.15) | collective-permute-done | bytes 131104 | tf_op jit(solution)/shard_map/ppermute | solution.py:59
  130.9 4.6 %collective-permute-start.18 = (bf16[64,1024]{1,0:T(8,128)(2,1)S(1)}, bf16[64,1024]{1,0:T(8,128)(2,1)S(1)}, u32[]{:S(2)}, u32[]{:S(2)}) collective-permute-start(bf16[64,1024]{1,0:T(8,128)(2,1)S(1)} %collective-permute-done.16), channel_id=1, source_target_pairs={{0,15},{1,0},{2,1},{3,2},{4,3},{5,4},{6,5},{7,6},{8,7},{9,8},{10,9... | collective-permute-start | bytes 393224 | tf_op jit(solution)/shard_map/ppermute | solution.py:59
  140.2 5.4 %collective-permute-start.20 = (bf16[64,1024]{1,0:T(8,128)(2,1)S(1)}, bf16[64,1024]{1,0:T(8,128)(2,1)S(1)}, u32[]{:S(2)}, u32[]{:S(2)}) collective-permute-start(bf16[64,1024]{1,0:T(8,128)(2,1)S(1)} %collective-permute-done.18), channel_id=1, source_target_pairs={{0,15},{1,0},{2,1},{3,2},{4,3},{5,4},{6,5},{7,6},{8,7},{9,8},{10,9... | collective-permute-start | bytes 393224 | tf_op jit(solution)/shard_map/ppermute | solution.py:59
  145.7 3.3 %collective-permute-done.19 = bf16[64,1024]{1,0:T(8,128)(2,1)S(1)} collective-permute-done((bf16[64,1024]{1,0:T(8,128)(2,1)S(1)}, bf16[64,1024]{1,0:T(8,128)(2,1)S(1)}, u32[]{:S(2)}, u32[]{:S(2)}) %collective-permute-start.19) | collective-permute-done | bytes 131104 | tf_op jit(solution)/shard_map/ppermute | solution.py:59
  150.9 4.6 %collective-permute-start.22 = (bf16[64,1024]{1,0:T(8,128)(2,1)S(1)}, bf16[64,1024]{1,0:T(8,128)(2,1)S(1)}, u32[]{:S(2)}, u32[]{:S(2)}) collective-permute-start(bf16[64,1024]{1,0:T(8,128)(2,1)S(1)} %collective-permute-done.20), channel_id=1, source_target_pairs={{0,15},{1,0},{2,1},{3,2},{4,3},{5,4},{6,5},{7,6},{8,7},{9,8},{10,9... | collective-permute-start | bytes 393224 | tf_op jit(solution)/shard_map/ppermute | solution.py:59
  155.5 4.4 %collective-permute-done.21 = bf16[64,1024]{1,0:T(8,128)(2,1)S(1)} collective-permute-done((bf16[64,1024]{1,0:T(8,128)(2,1)S(1)}, bf16[64,1024]{1,0:T(8,128)(2,1)S(1)}, u32[]{:S(2)}, u32[]{:S(2)}) %collective-permute-start.21) | collective-permute-done | bytes 131104 | tf_op jit(solution)/shard_map/ppermute | solution.py:59
  161.8 4.6 %collective-permute-start.24 = (bf16[64,1024]{1,0:T(8,128)(2,1)S(1)}, bf16[64,1024]{1,0:T(8,128)(2,1)S(1)}, u32[]{:S(2)}, u32[]{:S(2)}) collective-permute-start(bf16[64,1024]{1,0:T(8,128)(2,1)S(1)} %collective-permute-done.22), channel_id=1, source_target_pairs={{0,15},{1,0},{2,1},{3,2},{4,3},{5,4},{6,5},{7,6},{8,7},{9,8},{10,9... | collective-permute-start | bytes 393224 | tf_op jit(solution)/shard_map/ppermute | solution.py:59
  166.5 3.0 %collective-permute-done.23 = bf16[64,1024]{1,0:T(8,128)(2,1)S(1)} collective-permute-done((bf16[64,1024]{1,0:T(8,128)(2,1)S(1)}, bf16[64,1024]{1,0:T(8,128)(2,1)S(1)}, u32[]{:S(2)}, u32[]{:S(2)}) %collective-permute-start.23) | collective-permute-done | bytes 131104 | tf_op jit(solution)/shard_map/ppermute | solution.py:59
  171.4 4.6 %collective-permute-start.26 = (bf16[64,1024]{1,0:T(8,128)(2,1)S(1)}, bf16[64,1024]{1,0:T(8,128)(2,1)S(1)}, u32[]{:S(2)}, u32[]{:S(2)}) collective-permute-start(bf16[64,1024]{1,0:T(8,128)(2,1)S(1)} %collective-permute-done.24), channel_id=1, source_target_pairs={{0,15},{1,0},{2,1},{3,2},{4,3},{5,4},{6,5},{7,6},{8,7},{9,8},{10,9... | collective-permute-start | bytes 393224 | tf_op jit(solution)/shard_map/ppermute | solution.py:59
  192.8 6.2 %all-to-all-start.1 = ((bf16[16,64,512]{2,1,0:T(8,128)(2,1)}), bf16[16,64,512]{2,1,0:T(8,128)(2,1)S(1)}, u32[]{:S(2)}, u32[]{:S(2)}) async-start(bf16[16,64,512]{2,1,0:T(8,128)(2,1)} %bitcast.21), calls=%async_computation.1 | async-start | bytes 2097152 | tf_op jit(solution)/shard_map/all_to_all | solution.py:62
  203.4 12.4 %collective-permute-start.28 = (bf16[1024,512]{1,0:T(8,128)(2,1)}, bf16[1024,512]{1,0:T(8,128)(2,1)}, u32[]{:S(2)}, u32[]{:S(2)}) collective-permute-start(bf16[1024,512]{1,0:T(8,128)(2,1)} %pad_maximum_fusion.3), channel_id=1, source_target_pairs={{0,16},{16,0},{32,48},{48,32},{64,80},{80,64},{96,112},{112,96},{1... | collective-permute-start | bytes 3145736 | tf_op jit(solution)/shard_map/ppermute | solution.py:56
  222.6 3.9 %add_convert_fusion.2 = (bf16[512,512]{1,0:T(8,128)(2,1)}, bf16[512,512]{1,0:T(8,128)(2,1)}) fusion(bf16[1024,512]{1,0:T(8,128)(2,1)} %collective-permute-done.28, f32[512,512]{1,0:T(8,128)} %fusion.13, bf16[512,1024]{0,1:T(8,128)(2,1)} %slice_bitcast_fusion, bf16[1024,1024]{1,0:T(8,128)(2,1)} %copy-done.4), kind=kOutput, calls=%fused_computation.22 | convolution fusion | flops 538443776 | bytes 5242880 | tf_op jit(solution)/shard_map/dot_general | solution.py:163
  (114 shorter events, 81.7 us)
Async XLA Ops:
  7.2 171.6 %all-gather.5.cloned.1.call-start = ((), (), s32[]{:S(2)}) async-start(), calls=%async_computation.3 | async-start | bytes 2228224 | tf_op jit(solution)/shard_map/all_gather | solution.py:126
  12.6 38.6 %all-to-all-start = ((bf16[16,64,512]{2,1,0:T(8,128)(2,1)}), bf16[16,64,512]{2,1,0:T(8,128)(2,1)S(1)}, u32[]{:S(2)}, u32[]{:S(2)}) async-start(bf16[16,64,512]{2,1,0:T(8,128)(2,1)} %bitcast.1), calls=%async_computation | async-start | bytes 2097152 | tf_op jit(solution)/shard_map/all_to_all | solution.py:62
  30.6 151.2 %all-gather.3.cloned.1.call-start = ((), (), s32[]{:S(2)}) async-start(), calls=%async_computation.2 | async-start | bytes 4456448 | tf_op jit(solution)/shard_map/all_gather | solution.py:85
  30.7 9.7 %collective-permute-start.3 = (bf16[512,512]{1,0:T(8,128)(2,1)S(1)}, bf16[512,512]{1,0:T(8,128)(2,1)S(1)}, u32[]{:S(2)}, u32[]{:S(2)}) collective-permute-start(bf16[512,512]{1,0:T(8,128)(2,1)S(1)} %copy-done.10), channel_id=1, source_target_pairs={{0,16},{16,0},{32,48},{48,32},{64,80},{80,64},{96,112},{112,96},{1... | collective-permute-start | bytes 1572872 | tf_op jit(solution)/shard_map/ppermute | solution.py:56
  34.4 16.8 %collective-permute-start.1 = (bf16[512,512]{1,0:T(8,128)(2,1)S(1)}, bf16[512,512]{1,0:T(8,128)(2,1)S(1)}, u32[]{:S(2)}, u32[]{:S(2)}) collective-permute-start(bf16[512,512]{1,0:T(8,128)(2,1)S(1)} %copy-done.10), channel_id=1, source_target_pairs={{0,1},{1,2},{2,3},{3,4},{4,5},{5,6},{6,7},{7,8},{8,9},{9,10},{10,1... | collective-permute-start | bytes 1572872 | tf_op jit(solution)/shard_map/ppermute | solution.py:59
  57.2 26.4 %collective-permute-start.6 = (bf16[1024,512]{1,0:T(8,128)(2,1)S(1)}, bf16[1024,512]{1,0:T(8,128)(2,1)S(1)}, u32[]{:S(2)}, u32[]{:S(2)}) collective-permute-start(bf16[1024,512]{1,0:T(8,128)(2,1)S(1)} %pad_maximum_fusion.2), channel_id=1, source_target_pairs={{0,16},{16,0},{32,48},{48,32},{64,80},{80,64},{96,112},{112,96},{1... | collective-permute-start | bytes 3145736 | tf_op jit(solution)/shard_map/ppermute | solution.py:56
  59.2 12.2 %collective-permute-start.7 = (bf16[64,1024]{1,0:T(8,128)(2,1)S(1)}, bf16[64,1024]{1,0:T(8,128)(2,1)S(1)}, u32[]{:S(2)}, u32[]{:S(2)}) collective-permute-start(bf16[64,1024]{1,0:T(8,128)(2,1)S(1)} %get-tuple-element.56), channel_id=1, source_target_pairs={{0,2},{1,3},{2,4},{3,5},{4,6},{5,7},{6,8},{7,9},{8,10},{9,11},{10,... | collective-permute-start | bytes 393224 | tf_op jit(solution)/shard_map/ppermute | solution.py:59
  61.2 12.2 %collective-permute-start.5 = (bf16[64,1024]{1,0:T(8,128)(2,1)S(1)}, bf16[64,1024]{1,0:T(8,128)(2,1)}, u32[]{:S(2)}, u32[]{:S(2)}) collective-permute-start(bf16[64,1024]{1,0:T(8,128)(2,1)S(1)} %get-tuple-element.57), channel_id=1, source_target_pairs={{0,14},{1,15},{2,0},{3,1},{4,2},{5,3},{6,4},{7,5},{8,6},{9,7},{10,... | collective-permute-start | bytes 393224 | tf_op jit(solution)/shard_map/ppermute | solution.py:59
  81.0 9.1 %collective-permute-start.9 = (bf16[64,1024]{1,0:T(8,128)(2,1)S(1)}, bf16[64,1024]{1,0:T(8,128)(2,1)S(1)}, u32[]{:S(2)}, u32[]{:S(2)}) collective-permute-start(bf16[64,1024]{1,0:T(8,128)(2,1)S(1)} %get-tuple-element.54), channel_id=1, source_target_pairs={{0,2},{1,3},{2,4},{3,5},{4,6},{5,7},{6,8},{7,9},{8,10},{9,11},{10,... | collective-permute-start | bytes 393224 | tf_op jit(solution)/shard_map/ppermute | solution.py:59
  85.2 9.5 %collective-permute-start.11 = (bf16[64,1024]{1,0:T(8,128)(2,1)S(1)}, bf16[64,1024]{1,0:T(8,128)(2,1)S(1)}, u32[]{:S(2)}, u32[]{:S(2)}) collective-permute-start(bf16[64,1024]{1,0:T(8,128)(2,1)S(1)} %get-tuple-element.33), channel_id=1, source_target_pairs={{0,14},{1,15},{2,0},{3,1},{4,2},{5,3},{6,4},{7,5},{8,6},{9,7},{10,... | collective-permute-start | bytes 393224 | tf_op jit(solution)/shard_map/ppermute | solution.py:59
  98.1 11.4 %collective-permute-start.10 = (bf16[64,1024]{1,0:T(8,128)(2,1)S(1)}, bf16[64,1024]{1,0:T(8,128)(2,1)S(1)}, u32[]{:S(2)}, u32[]{:S(2)}) collective-permute-start(bf16[64,1024]{1,0:T(8,128)(2,1)S(1)} %get-tuple-element.52), channel_id=1, source_target_pairs={{0,2},{1,3},{2,4},{3,5},{4,6},{5,7},{6,8},{7,9},{8,10},{9,11},{10,... | collective-permute-start | bytes 393224 | tf_op jit(solution)/shard_map/ppermute | solution.py:59
  118.8 10.2 %collective-permute-start.15 = (bf16[64,1024]{1,0:T(8,128)(2,1)S(1)}, bf16[64,1024]{1,0:T(8,128)(2,1)S(1)}, u32[]{:S(2)}, u32[]{:S(2)}) collective-permute-start(bf16[64,1024]{1,0:T(8,128)(2,1)S(1)} %collective-permute-done.13), channel_id=1, source_target_pairs={{0,1},{1,2},{2,3},{3,4},{4,5},{5,6},{6,7},{7,8},{8,9},{9,10},{10,1... | collective-permute-start | bytes 393224 | tf_op jit(solution)/shard_map/ppermute | solution.py:59
  120.7 10.2 %collective-permute-start.16 = (bf16[64,1024]{1,0:T(8,128)(2,1)S(1)}, bf16[64,1024]{1,0:T(8,128)(2,1)S(1)}, u32[]{:S(2)}, u32[]{:S(2)}) collective-permute-start(bf16[64,1024]{1,0:T(8,128)(2,1)S(1)} %collective-permute-done.14), channel_id=1, source_target_pairs={{0,15},{1,0},{2,1},{3,2},{4,3},{5,4},{6,5},{7,6},{8,7},{9,8},{10,9... | collective-permute-start | bytes 393224 | tf_op jit(solution)/shard_map/ppermute | solution.py:59
  129.0 9.1 %collective-permute-start.17 = (bf16[64,1024]{1,0:T(8,128)(2,1)S(1)}, bf16[64,1024]{1,0:T(8,128)(2,1)S(1)}, u32[]{:S(2)}, u32[]{:S(2)}) collective-permute-start(bf16[64,1024]{1,0:T(8,128)(2,1)S(1)} %collective-permute-done.15), channel_id=1, source_target_pairs={{0,1},{1,2},{2,3},{3,4},{4,5},{5,6},{6,7},{7,8},{8,9},{9,10},{10,1... | collective-permute-start | bytes 393224 | tf_op jit(solution)/shard_map/ppermute | solution.py:59
  130.9 9.3 %collective-permute-start.18 = (bf16[64,1024]{1,0:T(8,128)(2,1)S(1)}, bf16[64,1024]{1,0:T(8,128)(2,1)S(1)}, u32[]{:S(2)}, u32[]{:S(2)}) collective-permute-start(bf16[64,1024]{1,0:T(8,128)(2,1)S(1)} %collective-permute-done.16), channel_id=1, source_target_pairs={{0,15},{1,0},{2,1},{3,2},{4,3},{5,4},{6,5},{7,6},{8,7},{9,8},{10,9... | collective-permute-start | bytes 393224 | tf_op jit(solution)/shard_map/ppermute | solution.py:59
  138.1 10.8 %collective-permute-start.19 = (bf16[64,1024]{1,0:T(8,128)(2,1)S(1)}, bf16[64,1024]{1,0:T(8,128)(2,1)S(1)}, u32[]{:S(2)}, u32[]{:S(2)}) collective-permute-start(bf16[64,1024]{1,0:T(8,128)(2,1)S(1)} %collective-permute-done.17), channel_id=1, source_target_pairs={{0,1},{1,2},{2,3},{3,4},{4,5},{5,6},{6,7},{7,8},{8,9},{9,10},{10,1... | collective-permute-start | bytes 393224 | tf_op jit(solution)/shard_map/ppermute | solution.py:59
  140.2 10.6 %collective-permute-start.20 = (bf16[64,1024]{1,0:T(8,128)(2,1)S(1)}, bf16[64,1024]{1,0:T(8,128)(2,1)S(1)}, u32[]{:S(2)}, u32[]{:S(2)}) collective-permute-start(bf16[64,1024]{1,0:T(8,128)(2,1)S(1)} %collective-permute-done.18), channel_id=1, source_target_pairs={{0,15},{1,0},{2,1},{3,2},{4,3},{5,4},{6,5},{7,6},{8,7},{9,8},{10,9... | collective-permute-start | bytes 393224 | tf_op jit(solution)/shard_map/ppermute | solution.py:59
  148.9 11.0 %collective-permute-start.21 = (bf16[64,1024]{1,0:T(8,128)(2,1)S(1)}, bf16[64,1024]{1,0:T(8,128)(2,1)S(1)}, u32[]{:S(2)}, u32[]{:S(2)}) collective-permute-start(bf16[64,1024]{1,0:T(8,128)(2,1)S(1)} %collective-permute-done.19), channel_id=1, source_target_pairs={{0,1},{1,2},{2,3},{3,4},{4,5},{5,6},{6,7},{7,8},{8,9},{9,10},{10,1... | collective-permute-start | bytes 393224 | tf_op jit(solution)/shard_map/ppermute | solution.py:59
  150.9 11.0 %collective-permute-start.22 = (bf16[64,1024]{1,0:T(8,128)(2,1)S(1)}, bf16[64,1024]{1,0:T(8,128)(2,1)S(1)}, u32[]{:S(2)}, u32[]{:S(2)}) collective-permute-start(bf16[64,1024]{1,0:T(8,128)(2,1)S(1)} %collective-permute-done.20), channel_id=1, source_target_pairs={{0,15},{1,0},{2,1},{3,2},{4,3},{5,4},{6,5},{7,6},{8,7},{9,8},{10,9... | collective-permute-start | bytes 393224 | tf_op jit(solution)/shard_map/ppermute | solution.py:59
  159.9 9.6 %collective-permute-start.23 = (bf16[64,1024]{1,0:T(8,128)(2,1)S(1)}, bf16[64,1024]{1,0:T(8,128)(2,1)S(1)}, u32[]{:S(2)}, u32[]{:S(2)}) collective-permute-start(bf16[64,1024]{1,0:T(8,128)(2,1)S(1)} %collective-permute-done.21), channel_id=1, source_target_pairs={{0,1},{1,2},{2,3},{3,4},{4,5},{5,6},{6,7},{7,8},{8,9},{9,10},{10,1... | collective-permute-start | bytes 393224 | tf_op jit(solution)/shard_map/ppermute | solution.py:59
  161.8 9.5 %collective-permute-start.24 = (bf16[64,1024]{1,0:T(8,128)(2,1)S(1)}, bf16[64,1024]{1,0:T(8,128)(2,1)S(1)}, u32[]{:S(2)}, u32[]{:S(2)}) collective-permute-start(bf16[64,1024]{1,0:T(8,128)(2,1)S(1)} %collective-permute-done.22), channel_id=1, source_target_pairs={{0,15},{1,0},{2,1},{3,2},{4,3},{5,4},{6,5},{7,6},{8,7},{9,8},{10,9... | collective-permute-start | bytes 393224 | tf_op jit(solution)/shard_map/ppermute | solution.py:59
  176.8 10.0 %collective-permute-start.27 = (bf16[64,1024]{1,0:T(8,128)(2,1)S(1)}, bf16[64,1024]{1,0:T(8,128)(2,1)S(1)}, u32[]{:S(2)}, u32[]{:S(2)}) collective-permute-start(bf16[64,1024]{1,0:T(8,128)(2,1)S(1)} %collective-permute-done.25), channel_id=1, source_target_pairs={{0,1},{1,2},{2,3},{3,4},{4,5},{5,6},{6,7},{7,8},{8,9},{9,10},{10,1... | collective-permute-start | bytes 393224 | tf_op jit(solution)/shard_map/ppermute | solution.py:59
  192.8 29.0 %all-to-all-start.1 = ((bf16[16,64,512]{2,1,0:T(8,128)(2,1)}), bf16[16,64,512]{2,1,0:T(8,128)(2,1)S(1)}, u32[]{:S(2)}, u32[]{:S(2)}) async-start(bf16[16,64,512]{2,1,0:T(8,128)(2,1)} %bitcast.21), calls=%async_computation.1 | async-start | bytes 2097152 | tf_op jit(solution)/shard_map/all_to_all | solution.py:62
  203.4 19.3 %collective-permute-start.28 = (bf16[1024,512]{1,0:T(8,128)(2,1)}, bf16[1024,512]{1,0:T(8,128)(2,1)}, u32[]{:S(2)}, u32[]{:S(2)}) collective-permute-start(bf16[1024,512]{1,0:T(8,128)(2,1)} %pad_maximum_fusion.3), channel_id=1, source_target_pairs={{0,16},{16,0},{32,48},{48,32},{64,80},{80,64},{96,112},{112,96},{1... | collective-permute-start | bytes 3145736 | tf_op jit(solution)/shard_map/ppermute | solution.py:56
  (21 other events, 118.5 us)
Sparse Core Ops, SparseCore 0:
  11.6 68.1 all-gather.4
  82.4 84.8 all-gather.2

commit v5 on v3

--- a/solution.py
+++ b/solution.py
@@ -124,8 +124,8 @@
     mine = (up_in.astype(F32) + down_in.astype(F32) + chunk(rank)).astype(BF16)
 
     rows = jnp.concatenate((inputs, grad_out), axis=1)
-    rows = lax.all_gather(rows, "row", axis=0, tiled=True, axis_index_groups=groups)
-    input_rows, cot_rows = rows[:, : inputs.shape[1]], rows[:, inputs.shape[1] :]
+    rows, _ = lax.optimization_barrier((rows, partial))
+    rows = exchange(jnp.broadcast_to(rows[None], (chips,) + rows.shape).reshape(-1, rows.shape[1]))
 
     gate_by, up_by, hidden = factors(acts_all, units)
 
@@ -143,12 +143,15 @@
             above, gate_by, up_by, hidden = lax.optimization_barrier(
                 (above, gate_by, up_by, hidden)
             )
+        if step == 4:
+            below, rows = lax.optimization_barrier((below, rows))
         if step < half:
             below = hop(below, -1)
         down_grad = put(down_grad, above, col - step)
         if step < half:
             down_grad = put(down_grad, below, col + step)
 
+    input_rows, cot_rows = rows[:, : inputs.shape[1]], rows[:, inputs.shape[1] :]
     grads = down_grad.astype(F32)
     gate_grad = (grads * gate_by.astype(F32)).astype(BF16)
     up_grad = (grads * up_by.astype(F32)).astype(BF16)
@@ -159,13 +162,6 @@
     )
     sums = exchange(total).reshape(chips, tokens, -1)
     input_grad = jnp.sum(sums.astype(F32), axis=0).astype(BF16)
-    total, gate_grad, up_grad = lax.optimization_barrier(
-        (total.astype(BF16), gate_grad, up_grad)
-    )
-    sums = exchange(total).reshape(chips, tokens, -1)
-    input_grad = jnp.sum(sums.astype(F32), axis=0).astype(BF16)
-    wd = lax.dot_general(hidden, cot_rows, TDIMS, preferred_element_type=F32)
-    w_down_grad = (wd[:units] + swap(wd[units:].astype(BF16)).astype(F32)).astype(BF16)
 
     def over_tokens(left, right):
         return lax.dot_general(left, right, TDIMS, preferred_element_type=F32)

time: 231 us -> 241 us (1.043)
  starting transfers between devices: 119 us -> 131 us
  waiting for transfers between devices: 57.4 us -> 50 us
  matrix products: 16.1 us -> 20.4 us
    all_to_all x2 -> x3, starting transfers between devices: 26.1 us -> 32.2 us  [exchange(): lax.all_to_all(array, 'row', 0, 0, axis_index_groups=groups, tiled=True)]
    ppermute x6, starting transfers between devices: 18.7 us -> 24.6 us  [swap(): return lax.ppermute(array, 'row', siblings)]
    all_gather x1 -> x0, waiting for transfers between devices: 5.76 us -> none  [local(): lax.all_gather(rows, 'row', axis=0, tiled=True, axis_index_groups=groups)]
    dot_general x6, matrix products: 11.1 us -> 15.3 us  [over_tokens(): return lax.dot_general(left, right, TDIMS, preferred_element_type=F32)]
    ppermute x23, waiting for transfers between devices: 50 us -> 46.6 us  [hop(): lax.ppermute(array, 'col', [(i, (i + step) % n_col) for i in range(n_col)])]
  transfers between devices with their start and end apart: 34 -> 34, of which waited for: 18 -> 18; matrix products, arithmetic and copies ran while one was open for 11% -> 10% of each run, Pallas kernels for 1% -> 1%
where the time goes in v5:
time: 241 us; the launch traced here: 240 us
  starting transfers between devices  131 us (54%)
  waiting for transfers between devices  50 us (21%)
  matrix products  20.4 us (8%)
  between operations  15.2 us (6%)
  other arithmetic  11.9 us (5%)
  local copies, waits for them, and re-layouts  8.6 us (4%)
    ppermute x23, starting transfers between devices, hop(): lax.ppermute(array, 'col', [(i, (i + step) % n_col) for i in range(n_col)])  73.6 us
    ppermute x23, waiting for transfers between devices, hop(): lax.ppermute(array, 'col', [(i, (i + step) % n_col) for i in range(n_col)])  46.6 us
    all_to_all x3, starting transfers between devices, exchange(): lax.all_to_all(array, 'row', 0, 0, axis_index_groups=groups, tiled=True)  32.2 us
    ppermute x6, starting transfers between devices, swap(): return lax.ppermute(array, 'row', siblings)  24.6 us
    dot_general x6, matrix products, over_tokens(): return lax.dot_general(left, right, TDIMS, preferred_element_type=F32)  15.3 us
  transfers between devices with their start and end apart: 34, of which 18 were waited for; matrix products, arithmetic and copies ran while one was open for 10% of the time, Pallas kernels for 1%

profile of v5, /device:TPU:1, one launch (start us, length us, event | category | flops | bytes accessed | tf_op | source)
XLA Modules:
  0.0 239.7 jit_solution(1016478306432482514)
XLA Ops:
  11.0 18.0 %all-to-all-start = ((bf16[16,64,512]{2,1,0:T(8,128)(2,1)}), bf16[16,64,512]{2,1,0:T(8,128)(2,1)S(1)}, u32[]{:S(2)}, u32[]{:S(2)}) async-start(bf16[16,64,512]{2,1,0:T(8,128)(2,1)} %bitcast.1), calls=%async_computation | async-start | bytes 2097152 | tf_op jit(solution)/shard_map/all_to_all | solution.py:63
  29.1 3.7 %collective-permute-start.3 = (bf16[512,512]{1,0:T(8,128)(2,1)S(1)}, bf16[512,512]{1,0:T(8,128)(2,1)S(1)}, u32[]{:S(2)}, u32[]{:S(2)}) collective-permute-start(bf16[512,512]{1,0:T(8,128)(2,1)S(1)} %copy-done.9), channel_id=1, source_target_pairs={{0,16},{16,0},{32,48},{48,32},{64,80},{80,64},{96,112},{112,96},{1... | collective-permute-start | bytes 1572872 | tf_op jit(solution)/shard_map/ppermute | solution.py:57
  39.8 9.6 %collective-permute-done.1 = bf16[512,512]{1,0:T(8,128)(2,1)S(1)} collective-permute-done((bf16[512,512]{1,0:T(8,128)(2,1)S(1)}, bf16[512,512]{1,0:T(8,128)(2,1)S(1)}, u32[]{:S(2)}, u32[]{:S(2)}) %collective-permute-start.1) | collective-permute-done | bytes 524320 | tf_op jit(solution)/shard_map/ppermute | solution.py:60
  60.2 5.5 %collective-permute-start.5 = (bf16[64,1024]{1,0:T(8,128)(2,1)}, bf16[64,1024]{1,0:T(8,128)(2,1)}, u32[]{:S(2)}, u32[]{:S(2)}) collective-permute-start(bf16[64,1024]{1,0:T(8,128)(2,1)} %get-tuple-element.61), channel_id=1, source_target_pairs={{0,14},{1,15},{2,0},{3,1},{4,2},{5,3},{6,4},{7,5},{8,6},{9,7},{10,... | collective-permute-start | bytes 393224 | tf_op jit(solution)/shard_map/ppermute | solution.py:60
  65.7 4.7 %collective-permute-done.7 = bf16[64,1024]{1,0:T(8,128)(2,1)S(1)} collective-permute-done((bf16[64,1024]{1,0:T(8,128)(2,1)S(1)}, bf16[64,1024]{1,0:T(8,128)(2,1)S(1)}, u32[]{:S(2)}, u32[]{:S(2)}) %collective-permute-start.7) | collective-permute-done | bytes 131104 | tf_op jit(solution)/shard_map/ppermute | solution.py:60
  74.0 7.0 %all-to-all-start.1 = ((bf16[16,64,1024]{2,1,0:T(8,128)(2,1)}), bf16[16,64,1024]{2,1,0:T(8,128)(2,1)}, u32[]{:S(2)}, u32[]{:S(2)}) async-start(bf16[16,64,1024]{2,1,0:T(8,128)(2,1)} %broadcast_in_dim.8), calls=%async_computation.1 | async-start | bytes 4194304 | tf_op jit(solution)/shard_map/all_to_all | solution.py:63
  89.0 5.5 %collective-permute-start.11 = (bf16[64,1024]{1,0:T(8,128)(2,1)S(1)}, bf16[64,1024]{1,0:T(8,128)(2,1)S(1)}, u32[]{:S(2)}, u32[]{:S(2)}) collective-permute-start(bf16[64,1024]{1,0:T(8,128)(2,1)S(1)} %get-tuple-element.36), channel_id=1, source_target_pairs={{0,14},{1,15},{2,0},{3,1},{4,2},{5,3},{6,4},{7,5},{8,6},{9,7},{10,... | collective-permute-start | bytes 393224 | tf_op jit(solution)/shard_map/ppermute | solution.py:60
  94.5 3.5 %collective-permute-done.9 = bf16[64,1024]{1,0:T(8,128)(2,1)S(1)} collective-permute-done((bf16[64,1024]{1,0:T(8,128)(2,1)}, bf16[64,1024]{1,0:T(8,128)(2,1)S(1)}, u32[]{:S(2)}, u32[]{:S(2)}) %collective-permute-start.9) | collective-permute-done | bytes 131104 | tf_op jit(solution)/shard_map/ppermute | solution.py:60
  98.0 3.0 %collective-permute-done.11 = bf16[64,1024]{1,0:T(8,128)(2,1)S(1)} collective-permute-done((bf16[64,1024]{1,0:T(8,128)(2,1)S(1)}, bf16[64,1024]{1,0:T(8,128)(2,1)S(1)}, u32[]{:S(2)}, u32[]{:S(2)}) %collective-permute-start.11) | collective-permute-done | bytes 131104 | tf_op jit(solution)/shard_map/ppermute | solution.py:60
  101.2 4.4 %collective-permute-start.10 = (bf16[64,1024]{1,0:T(8,128)(2,1)S(1)}, bf16[64,1024]{1,0:T(8,128)(2,1)S(1)}, u32[]{:S(2)}, u32[]{:S(2)}) collective-permute-start(bf16[64,1024]{1,0:T(8,128)(2,1)S(1)} %get-tuple-element.56), channel_id=1, source_target_pairs={{0,2},{1,3},{2,4},{3,5},{4,6},{5,7},{6,8},{7,9},{8,10},{9,11},{10,... | collective-permute-start | bytes 393224 | tf_op jit(solution)/shard_map/ppermute | solution.py:60
  105.6 3.0 %collective-permute-start.12 = (bf16[64,1024]{1,0:T(8,128)(2,1)S(1)}, bf16[64,1024]{1,0:T(8,128)(2,1)S(1)}, u32[]{:S(2)}, u32[]{:S(2)}) collective-permute-start(bf16[64,1024]{1,0:T(8,128)(2,1)S(1)} %get-tuple-element.57), channel_id=1, source_target_pairs={{0,14},{1,15},{2,0},{3,1},{4,2},{5,3},{6,4},{7,5},{8,6},{9,7},{10,... | collective-permute-start | bytes 393224 | tf_op jit(solution)/shard_map/ppermute | solution.py:60
  108.6 5.4 %collective-permute-done.10 = bf16[64,1024]{1,0:T(8,128)(2,1)S(1)} collective-permute-done((bf16[64,1024]{1,0:T(8,128)(2,1)S(1)}, bf16[64,1024]{1,0:T(8,128)(2,1)S(1)}, u32[]{:S(2)}, u32[]{:S(2)}) %collective-permute-start.10) | collective-permute-done | bytes 131104 | tf_op jit(solution)/shard_map/ppermute | solution.py:60
  119.2 4.6 %collective-permute-start.14 = (bf16[64,1024]{1,0:T(8,128)(2,1)S(1)}, bf16[64,1024]{1,0:T(8,128)(2,1)S(1)}, u32[]{:S(2)}, u32[]{:S(2)}) collective-permute-start(bf16[64,1024]{1,0:T(8,128)(2,1)S(1)} %get-tuple-element.53), channel_id=1, source_target_pairs={{0,15},{1,0},{2,1},{3,2},{4,3},{5,4},{6,5},{7,6},{8,7},{9,8},{10,9... | collective-permute-start | bytes 393224 | tf_op jit(solution)/shard_map/ppermute | solution.py:60
  123.8 3.4 %collective-permute-done.13 = bf16[64,1024]{1,0:T(8,128)(2,1)S(1)} collective-permute-done((bf16[64,1024]{1,0:T(8,128)(2,1)S(1)}, bf16[64,1024]{1,0:T(8,128)(2,1)S(1)}, u32[]{:S(2)}, u32[]{:S(2)}) %collective-permute-start.13) | collective-permute-done | bytes 131104 | tf_op jit(solution)/shard_map/ppermute | solution.py:60
  129.3 4.6 %collective-permute-start.16 = (bf16[64,1024]{1,0:T(8,128)(2,1)S(1)}, bf16[64,1024]{1,0:T(8,128)(2,1)S(1)}, u32[]{:S(2)}, u32[]{:S(2)}) collective-permute-start(bf16[64,1024]{1,0:T(8,128)(2,1)S(1)} %collective-permute-done.14), channel_id=1, source_target_pairs={{0,15},{1,0},{2,1},{3,2},{4,3},{5,4},{6,5},{7,6},{8,7},{9,8},{10,9... | collective-permute-start | bytes 393224 | tf_op jit(solution)/shard_map/ppermute | solution.py:60
  137.8 3.7 %collective-permute-start.18 = (bf16[64,1024]{1,0:T(8,128)(2,1)S(1)}, bf16[64,1024]{1,0:T(8,128)(2,1)S(1)}, u32[]{:S(2)}, u32[]{:S(2)}) collective-permute-start(bf16[64,1024]{1,0:T(8,128)(2,1)S(1)} %collective-permute-done.16), channel_id=1, source_target_pairs={{0,15},{1,0},{2,1},{3,2},{4,3},{5,4},{6,5},{7,6},{8,7},{9,8},{10,9... | collective-permute-start | bytes 393224 | tf_op jit(solution)/shard_map/ppermute | solution.py:60
  144.2 4.9 %collective-permute-done.19 = bf16[64,1024]{1,0:T(8,128)(2,1)S(1)} collective-permute-done((bf16[64,1024]{1,0:T(8,128)(2,1)S(1)}, bf16[64,1024]{1,0:T(8,128)(2,1)S(1)}, u32[]{:S(2)}, u32[]{:S(2)}) %collective-permute-start.19) | collective-permute-done | bytes 131104 | tf_op jit(solution)/shard_map/ppermute | solution.py:60
  151.1 4.6 %collective-permute-start.20 = (bf16[64,1024]{1,0:T(8,128)(2,1)S(1)}, bf16[64,1024]{1,0:T(8,128)(2,1)S(1)}, u32[]{:S(2)}, u32[]{:S(2)}) collective-permute-start(bf16[64,1024]{1,0:T(8,128)(2,1)S(1)} %collective-permute-done.18), channel_id=1, source_target_pairs={{0,15},{1,0},{2,1},{3,2},{4,3},{5,4},{6,5},{7,6},{8,7},{9,8},{10,9... | collective-permute-start | bytes 393224 | tf_op jit(solution)/shard_map/ppermute | solution.py:60
  158.0 4.6 %collective-permute-start.22 = (bf16[64,1024]{1,0:T(8,128)(2,1)S(1)}, bf16[64,1024]{1,0:T(8,128)(2,1)S(1)}, u32[]{:S(2)}, u32[]{:S(2)}) collective-permute-start(bf16[64,1024]{1,0:T(8,128)(2,1)S(1)} %collective-permute-done.20), channel_id=1, source_target_pairs={{0,15},{1,0},{2,1},{3,2},{4,3},{5,4},{6,5},{7,6},{8,7},{9,8},{10,9... | collective-permute-start | bytes 393224 | tf_op jit(solution)/shard_map/ppermute | solution.py:60
  165.6 4.9 %collective-permute-start.24 = (bf16[64,1024]{1,0:T(8,128)(2,1)S(1)}, bf16[64,1024]{1,0:T(8,128)(2,1)S(1)}, u32[]{:S(2)}, u32[]{:S(2)}) collective-permute-start(bf16[64,1024]{1,0:T(8,128)(2,1)S(1)} %collective-permute-done.22), channel_id=1, source_target_pairs={{0,15},{1,0},{2,1},{3,2},{4,3},{5,4},{6,5},{7,6},{8,7},{9,8},{10,9... | collective-permute-start | bytes 393224 | tf_op jit(solution)/shard_map/ppermute | solution.py:60
  173.8 4.6 %collective-permute-start.26 = (bf16[64,1024]{1,0:T(8,128)(2,1)S(1)}, bf16[64,1024]{1,0:T(8,128)(2,1)S(1)}, u32[]{:S(2)}, u32[]{:S(2)}) collective-permute-start(bf16[64,1024]{1,0:T(8,128)(2,1)S(1)} %collective-permute-done.24), channel_id=1, source_target_pairs={{0,15},{1,0},{2,1},{3,2},{4,3},{5,4},{6,5},{7,6},{8,7},{9,8},{10,9... | collective-permute-start | bytes 393224 | tf_op jit(solution)/shard_map/ppermute | solution.py:60
  192.3 7.2 %all-to-all-start.2 = ((bf16[16,64,512]{2,1,0:T(8,128)(2,1)}), bf16[16,64,512]{2,1,0:T(8,128)(2,1)S(1)}, u32[]{:S(2)}, u32[]{:S(2)}) async-start(bf16[16,64,512]{2,1,0:T(8,128)(2,1)} %bitcast.16), calls=%async_computation.2 | async-start | bytes 2097152 | tf_op jit(solution)/shard_map/all_to_all | solution.py:63
  204.9 12.4 %collective-permute-start.28 = (bf16[1024,512]{1,0:T(8,128)(2,1)}, bf16[1024,512]{1,0:T(8,128)(2,1)}, u32[]{:S(2)}, u32[]{:S(2)}) collective-permute-start(bf16[1024,512]{1,0:T(8,128)(2,1)} %pad_maximum_fusion.3), channel_id=1, source_target_pairs={{0,16},{16,0},{32,48},{48,32},{64,80},{80,64},{96,112},{112,96},{1... | collective-permute-start | bytes 3145736 | tf_op jit(solution)/shard_map/ppermute | solution.py:57
  226.6 3.3 %fusion.3 = bf16[512,512]{1,0:T(8,128)(2,1)} fusion(bf16[1024,1024]{1,0:T(8,128)(2,1)} %copy-done.6, bf16[1024,1024]{1,0:T(8,128)(2,1)} %bitcast.6, bf16[1024,512]{1,0:T(8,128)(2,1)} %collective-permute-done.28), kind=kOutput, calls=%fused_computation.11 | convolution fusion | flops 537657344 | bytes 3145728 | tf_op jit(solution)/shard_map/dot_general | solution.py:167
  (115 shorter events, 88.4 us)
Async XLA Ops:
  11.0 38.5 %all-to-all-start = ((bf16[16,64,512]{2,1,0:T(8,128)(2,1)}), bf16[16,64,512]{2,1,0:T(8,128)(2,1)S(1)}, u32[]{:S(2)}, u32[]{:S(2)}) async-start(bf16[16,64,512]{2,1,0:T(8,128)(2,1)} %bitcast.1), calls=%async_computation | async-start | bytes 2097152 | tf_op jit(solution)/shard_map/all_to_all | solution.py:63
  29.0 152.6 %all-gather.2.cloned.1.call-start = ((), (), s32[]{:S(2)}) async-start(), calls=%async_computation.3 | async-start | bytes 4456448 | tf_op jit(solution)/shard_map/all_gather | solution.py:86
  29.1 9.7 %collective-permute-start.3 = (bf16[512,512]{1,0:T(8,128)(2,1)S(1)}, bf16[512,512]{1,0:T(8,128)(2,1)S(1)}, u32[]{:S(2)}, u32[]{:S(2)}) collective-permute-start(bf16[512,512]{1,0:T(8,128)(2,1)S(1)} %copy-done.9), channel_id=1, source_target_pairs={{0,16},{16,0},{32,48},{48,32},{64,80},{80,64},{96,112},{112,96},{1... | collective-permute-start | bytes 1572872 | tf_op jit(solution)/shard_map/ppermute | solution.py:57
  32.8 16.6 %collective-permute-start.1 = (bf16[512,512]{1,0:T(8,128)(2,1)S(1)}, bf16[512,512]{1,0:T(8,128)(2,1)S(1)}, u32[]{:S(2)}, u32[]{:S(2)}) collective-permute-start(bf16[512,512]{1,0:T(8,128)(2,1)S(1)} %copy-done.9), channel_id=1, source_target_pairs={{0,1},{1,2},{2,3},{3,4},{4,5},{5,6},{6,7},{7,8},{8,9},{9,10},{10,1... | collective-permute-start | bytes 1572872 | tf_op jit(solution)/shard_map/ppermute | solution.py:60
  55.5 31.7 %collective-permute-start.6 = (bf16[1024,512]{1,0:T(8,128)(2,1)S(1)}, bf16[1024,512]{1,0:T(8,128)(2,1)S(1)}, u32[]{:S(2)}, u32[]{:S(2)}) collective-permute-start(bf16[1024,512]{1,0:T(8,128)(2,1)S(1)} %pad_maximum_fusion.2), channel_id=1, source_target_pairs={{0,16},{16,0},{32,48},{48,32},{64,80},{80,64},{96,112},{112,96},{1... | collective-permute-start | bytes 3145736 | tf_op jit(solution)/shard_map/ppermute | solution.py:57
  58.3 12.2 %collective-permute-start.7 = (bf16[64,1024]{1,0:T(8,128)(2,1)S(1)}, bf16[64,1024]{1,0:T(8,128)(2,1)S(1)}, u32[]{:S(2)}, u32[]{:S(2)}) collective-permute-start(bf16[64,1024]{1,0:T(8,128)(2,1)S(1)} %get-tuple-element.60), channel_id=1, source_target_pairs={{0,2},{1,3},{2,4},{3,5},{4,6},{5,7},{6,8},{7,9},{8,10},{9,11},{10,... | collective-permute-start | bytes 393224 | tf_op jit(solution)/shard_map/ppermute | solution.py:60
  60.2 20.9 %collective-permute-start.5 = (bf16[64,1024]{1,0:T(8,128)(2,1)}, bf16[64,1024]{1,0:T(8,128)(2,1)}, u32[]{:S(2)}, u32[]{:S(2)}) collective-permute-start(bf16[64,1024]{1,0:T(8,128)(2,1)} %get-tuple-element.61), channel_id=1, source_target_pairs={{0,14},{1,15},{2,0},{3,1},{4,2},{5,3},{6,4},{7,5},{8,6},{9,7},{10,... | collective-permute-start | bytes 393224 | tf_op jit(solution)/shard_map/ppermute | solution.py:60
  70.5 13.3 %collective-permute-start.8 = (bf16[64,1024]{1,0:T(8,128)(2,1)S(1)}, bf16[64,1024]{1,0:T(8,128)(2,1)S(1)}, u32[]{:S(2)}, u32[]{:S(2)}) collective-permute-start(bf16[64,1024]{1,0:T(8,128)(2,1)S(1)} %add_convert_fusion.6), channel_id=1, source_target_pairs={{0,2},{1,3},{2,4},{3,5},{4,6},{5,7},{6,8},{7,9},{8,10},{9,11},{10,... | collective-permute-start | bytes 393224 | tf_op jit(solution)/shard_map/ppermute | solution.py:60
  74.0 77.0 %all-to-all-start.1 = ((bf16[16,64,1024]{2,1,0:T(8,128)(2,1)}), bf16[16,64,1024]{2,1,0:T(8,128)(2,1)}, u32[]{:S(2)}, u32[]{:S(2)}) async-start(bf16[16,64,1024]{2,1,0:T(8,128)(2,1)} %broadcast_in_dim.8), calls=%async_computation.1 | async-start | bytes 4194304 | tf_op jit(solution)/shard_map/all_to_all | solution.py:63
  85.4 12.7 %collective-permute-start.9 = (bf16[64,1024]{1,0:T(8,128)(2,1)}, bf16[64,1024]{1,0:T(8,128)(2,1)S(1)}, u32[]{:S(2)}, u32[]{:S(2)}) collective-permute-start(bf16[64,1024]{1,0:T(8,128)(2,1)} %get-tuple-element.58), channel_id=1, source_target_pairs={{0,2},{1,3},{2,4},{3,5},{4,6},{5,7},{6,8},{7,9},{8,10},{9,11},{10,... | collective-permute-start | bytes 393224 | tf_op jit(solution)/shard_map/ppermute | solution.py:60
  89.0 12.1 %collective-permute-start.11 = (bf16[64,1024]{1,0:T(8,128)(2,1)S(1)}, bf16[64,1024]{1,0:T(8,128)(2,1)S(1)}, u32[]{:S(2)}, u32[]{:S(2)}) collective-permute-start(bf16[64,1024]{1,0:T(8,128)(2,1)S(1)} %get-tuple-element.36), channel_id=1, source_target_pairs={{0,14},{1,15},{2,0},{3,1},{4,2},{5,3},{6,4},{7,5},{8,6},{9,7},{10,... | collective-permute-start | bytes 393224 | tf_op jit(solution)/shard_map/ppermute | solution.py:60
  101.2 12.8 %collective-permute-start.10 = (bf16[64,1024]{1,0:T(8,128)(2,1)S(1)}, bf16[64,1024]{1,0:T(8,128)(2,1)S(1)}, u32[]{:S(2)}, u32[]{:S(2)}) collective-permute-start(bf16[64,1024]{1,0:T(8,128)(2,1)S(1)} %get-tuple-element.56), channel_id=1, source_target_pairs={{0,2},{1,3},{2,4},{3,5},{4,6},{5,7},{6,8},{7,9},{8,10},{9,11},{10,... | collective-permute-start | bytes 393224 | tf_op jit(solution)/shard_map/ppermute | solution.py:60
  105.6 11.4 %collective-permute-start.12 = (bf16[64,1024]{1,0:T(8,128)(2,1)S(1)}, bf16[64,1024]{1,0:T(8,128)(2,1)S(1)}, u32[]{:S(2)}, u32[]{:S(2)}) collective-permute-start(bf16[64,1024]{1,0:T(8,128)(2,1)S(1)} %get-tuple-element.57), channel_id=1, source_target_pairs={{0,14},{1,15},{2,0},{3,1},{4,2},{5,3},{6,4},{7,5},{8,6},{9,7},{10,... | collective-permute-start | bytes 393224 | tf_op jit(solution)/shard_map/ppermute | solution.py:60
  117.3 9.9 %collective-permute-start.13 = (bf16[64,1024]{1,0:T(8,128)(2,1)S(1)}, bf16[64,1024]{1,0:T(8,128)(2,1)S(1)}, u32[]{:S(2)}, u32[]{:S(2)}) collective-permute-start(bf16[64,1024]{1,0:T(8,128)(2,1)S(1)} %get-tuple-element.53), channel_id=1, source_target_pairs={{0,1},{1,2},{2,3},{3,4},{4,5},{5,6},{6,7},{7,8},{8,9},{9,10},{10,1... | collective-permute-start | bytes 393224 | tf_op jit(solution)/shard_map/ppermute | solution.py:60
  119.2 10.1 %collective-permute-start.14 = (bf16[64,1024]{1,0:T(8,128)(2,1)S(1)}, bf16[64,1024]{1,0:T(8,128)(2,1)S(1)}, u32[]{:S(2)}, u32[]{:S(2)}) collective-permute-start(bf16[64,1024]{1,0:T(8,128)(2,1)S(1)} %get-tuple-element.53), channel_id=1, source_target_pairs={{0,15},{1,0},{2,1},{3,2},{4,3},{5,4},{6,5},{7,6},{8,7},{9,8},{10,9... | collective-permute-start | bytes 393224 | tf_op jit(solution)/shard_map/ppermute | solution.py:60
  127.2 7.8 %collective-permute-start.15 = (bf16[64,1024]{1,0:T(8,128)(2,1)S(1)}, bf16[64,1024]{1,0:T(8,128)(2,1)S(1)}, u32[]{:S(2)}, u32[]{:S(2)}) collective-permute-start(bf16[64,1024]{1,0:T(8,128)(2,1)S(1)} %collective-permute-done.13), channel_id=1, source_target_pairs={{0,1},{1,2},{2,3},{3,4},{4,5},{5,6},{6,7},{7,8},{8,9},{9,10},{10,1... | collective-permute-start | bytes 393224 | tf_op jit(solution)/shard_map/ppermute | solution.py:60
  129.3 8.5 %collective-permute-start.16 = (bf16[64,1024]{1,0:T(8,128)(2,1)S(1)}, bf16[64,1024]{1,0:T(8,128)(2,1)S(1)}, u32[]{:S(2)}, u32[]{:S(2)}) collective-permute-start(bf16[64,1024]{1,0:T(8,128)(2,1)S(1)} %collective-permute-done.14), channel_id=1, source_target_pairs={{0,15},{1,0},{2,1},{3,2},{4,3},{5,4},{6,5},{7,6},{8,7},{9,8},{10,9... | collective-permute-start | bytes 393224 | tf_op jit(solution)/shard_map/ppermute | solution.py:60
  137.8 13.2 %collective-permute-start.18 = (bf16[64,1024]{1,0:T(8,128)(2,1)S(1)}, bf16[64,1024]{1,0:T(8,128)(2,1)S(1)}, u32[]{:S(2)}, u32[]{:S(2)}) collective-permute-start(bf16[64,1024]{1,0:T(8,128)(2,1)S(1)} %collective-permute-done.16), channel_id=1, source_target_pairs={{0,15},{1,0},{2,1},{3,2},{4,3},{5,4},{6,5},{7,6},{8,7},{9,8},{10,9... | collective-permute-start | bytes 393224 | tf_op jit(solution)/shard_map/ppermute | solution.py:60
  156.0 7.6 %collective-permute-start.23 = (bf16[64,1024]{1,0:T(8,128)(2,1)S(1)}, bf16[64,1024]{1,0:T(8,128)(2,1)S(1)}, u32[]{:S(2)}, u32[]{:S(2)}) collective-permute-start(bf16[64,1024]{1,0:T(8,128)(2,1)S(1)} %collective-permute-done.21), channel_id=1, source_target_pairs={{0,1},{1,2},{2,3},{3,4},{4,5},{5,6},{6,7},{7,8},{8,9},{9,10},{10,1... | collective-permute-start | bytes 393224 | tf_op jit(solution)/shard_map/ppermute | solution.py:60
  163.6 8.2 %collective-permute-start.25 = (bf16[64,1024]{1,0:T(8,128)(2,1)S(1)}, bf16[64,1024]{1,0:T(8,128)(2,1)S(1)}, u32[]{:S(2)}, u32[]{:S(2)}) collective-permute-start(bf16[64,1024]{1,0:T(8,128)(2,1)S(1)} %collective-permute-done.23), channel_id=1, source_target_pairs={{0,1},{1,2},{2,3},{3,4},{4,5},{5,6},{6,7},{7,8},{8,9},{9,10},{10,1... | collective-permute-start | bytes 393224 | tf_op jit(solution)/shard_map/ppermute | solution.py:60
  165.6 8.2 %collective-permute-start.24 = (bf16[64,1024]{1,0:T(8,128)(2,1)S(1)}, bf16[64,1024]{1,0:T(8,128)(2,1)S(1)}, u32[]{:S(2)}, u32[]{:S(2)}) collective-permute-start(bf16[64,1024]{1,0:T(8,128)(2,1)S(1)} %collective-permute-done.22), channel_id=1, source_target_pairs={{0,15},{1,0},{2,1},{3,2},{4,3},{5,4},{6,5},{7,6},{8,7},{9,8},{10,9... | collective-permute-start | bytes 393224 | tf_op jit(solution)/shard_map/ppermute | solution.py:60
  171.8 14.3 %collective-permute-start.27 = (bf16[64,1024]{1,0:T(8,128)(2,1)S(1)}, bf16[64,1024]{1,0:T(8,128)(2,1)S(1)}, u32[]{:S(2)}, u32[]{:S(2)}) collective-permute-start(bf16[64,1024]{1,0:T(8,128)(2,1)S(1)} %collective-permute-done.25), channel_id=1, source_target_pairs={{0,1},{1,2},{2,3},{3,4},{4,5},{5,6},{6,7},{7,8},{8,9},{9,10},{10,1... | collective-permute-start | bytes 393224 | tf_op jit(solution)/shard_map/ppermute | solution.py:60
  192.3 33.6 %all-to-all-start.2 = ((bf16[16,64,512]{2,1,0:T(8,128)(2,1)}), bf16[16,64,512]{2,1,0:T(8,128)(2,1)S(1)}, u32[]{:S(2)}, u32[]{:S(2)}) async-start(bf16[16,64,512]{2,1,0:T(8,128)(2,1)} %bitcast.16), calls=%async_computation.2 | async-start | bytes 2097152 | tf_op jit(solution)/shard_map/all_to_all | solution.py:63
  204.9 21.7 %collective-permute-start.28 = (bf16[1024,512]{1,0:T(8,128)(2,1)}, bf16[1024,512]{1,0:T(8,128)(2,1)}, u32[]{:S(2)}, u32[]{:S(2)}) collective-permute-start(bf16[1024,512]{1,0:T(8,128)(2,1)} %pad_maximum_fusion.3), channel_id=1, source_target_pairs={{0,16},{16,0},{32,48},{48,32},{64,80},{80,64},{96,112},{112,96},{1... | collective-permute-start | bytes 3145736 | tf_op jit(solution)/shard_map/ppermute | solution.py:57
  (22 other events, 130.3 us)
Sparse Core Ops, SparseCore 0:
  49.6 88.1 all-gather.1

commit v6 on v5

--- a/solution.py
+++ b/solution.py
@@ -82,8 +82,9 @@
     keep = lax.dynamic_slice_in_dim(acts, core * tokens, tokens, 0)
     give = lax.dynamic_slice_in_dim(acts, (1 - core) * tokens, tokens, 0)
     acts = jnp.concatenate((keep, swap(give)), axis=1)
-    cot, w_next, acts, w_here = lax.optimization_barrier((cot, w_next, acts, w_here))
+    cot, acts, w_here = lax.optimization_barrier((cot, acts, w_here))
     acts_all = lax.all_gather(acts, "col", axis=0, tiled=True)
+    cot, w_next = lax.optimization_barrier((cot, w_next))
     w_next = jnp.concatenate((w_next, swap(w_next)), axis=0)
     cot = cot.reshape(n_col // 2, 2, tokens, -1)
 
@@ -124,8 +125,8 @@
     mine = (up_in.astype(F32) + down_in.astype(F32) + chunk(rank)).astype(BF16)
 
     rows = jnp.concatenate((inputs, grad_out), axis=1)
-    rows, _ = lax.optimization_barrier((rows, partial))
-    rows = exchange(jnp.broadcast_to(rows[None], (chips,) + rows.shape).reshape(-1, rows.shape[1]))
+    rows = lax.all_gather(rows, "row", axis=0, tiled=True, axis_index_groups=groups)
+    input_rows, cot_rows = rows[:, : inputs.shape[1]], rows[:, inputs.shape[1] :]
 
     gate_by, up_by, hidden = factors(acts_all, units)
 
@@ -143,15 +144,12 @@
             above, gate_by, up_by, hidden = lax.optimization_barrier(
                 (above, gate_by, up_by, hidden)
             )
-        if step == 4:
-            below, rows = lax.optimization_barrier((below, rows))
         if step < half:
             below = hop(below, -1)
         down_grad = put(down_grad, above, col - step)
         if step < half:
             down_grad = put(down_grad, below, col + step)
 
-    input_rows, cot_rows = rows[:, : inputs.shape[1]], rows[:, inputs.shape[1] :]
     grads = down_grad.astype(F32)
     gate_grad = (grads * gate_by.astype(F32)).astype(BF16)
     up_grad = (grads * up_by.astype(F32)).astype(BF16)

time: 241 us -> 240 us (level)
  waiting for transfers between devices: 50 us -> 56.2 us
  matrix products: 20.4 us -> 17.2 us
  starting transfers between devices: 131 us -> 128 us
    all_to_all x3 -> x2, starting transfers between devices: 32.2 us -> 24.8 us  [exchange(): lax.all_to_all(array, 'row', 0, 0, axis_index_groups=groups, tiled=True)]
    all_to_all x3 -> x2, waiting for transfers between devices: 0.01 us -> 7.11 us  [exchange(): lax.all_to_all(array, 'row', 0, 0, axis_index_groups=groups, tiled=True)]
    dot_general x6, matrix products: 15.3 us -> 11.1 us  [over_tokens(): return lax.dot_general(left, right, TDIMS, preferred_element_type=F32)]
    ppermute x6, starting transfers between devices: 24.6 us -> 28.2 us  [swap(): return lax.ppermute(array, 'row', siblings)]
    unnamed x24 -> x30, local copies, waits for them, and re-layouts: 4.63 us -> 5.47 us
  transfers between devices with their start and end apart: 34 -> 34, of which waited for: 18 -> 17; matrix products, arithmetic and copies ran while one was open for 10% -> 11% of each run, Pallas kernels for 1% -> 1%
where the time goes in v6:
time: 240 us; the launch traced here: 239 us
  starting transfers between devices  128 us (53%)
  waiting for transfers between devices  56.2 us (23%)
  matrix products  17.2 us (7%)
  between operations  15.2 us (6%)
  other arithmetic  12.7 us (5%)
  local copies, waits for them, and re-layouts  7.89 us (3%)
    ppermute x23, starting transfers between devices, hop(): lax.ppermute(array, 'col', [(i, (i + step) % n_col) for i in range(n_col)])  73.8 us
    ppermute x23, waiting for transfers between devices, hop(): lax.ppermute(array, 'col', [(i, (i + step) % n_col) for i in range(n_col)])  47.5 us
    ppermute x6, starting transfers between devices, swap(): return lax.ppermute(array, 'row', siblings)  28.2 us
    all_to_all x2, starting transfers between devices, exchange(): lax.all_to_all(array, 'row', 0, 0, axis_index_groups=groups, tiled=True)  24.8 us
    dot_general x6, matrix products, over_tokens(): return lax.dot_general(left, right, TDIMS, preferred_element_type=F32)  11.1 us
    all_to_all x2, waiting for transfers between devices, exchange(): lax.all_to_all(array, 'row', 0, 0, axis_index_groups=groups, tiled=True)  7.11 us
    unnamed x30, local copies, waits for them, and re-layouts  5.47 us
  transfers between devices with their start and end apart: 34, of which 17 were waited for; matrix products, arithmetic and copies ran while one was open for 11% of the time, Pallas kernels for 1%

profile of v6, /device:TPU:1, one launch (start us, length us, event | category | flops | bytes accessed | tf_op | source)
XLA Modules:
  0.0 239.2 jit_solution(15984628094286353319)
XLA Ops:
  11.0 18.0 %all-to-all-start = ((bf16[16,64,512]{2,1,0:T(8,128)(2,1)}), bf16[16,64,512]{2,1,0:T(8,128)(2,1)S(1)}, u32[]{:S(2)}, u32[]{:S(2)}) async-start(bf16[16,64,512]{2,1,0:T(8,128)(2,1)} %bitcast.1), calls=%async_computation | async-start | bytes 2097152 | tf_op jit(solution)/shard_map/all_to_all | solution.py:63
  29.1 3.7 %collective-permute-start.2 = (bf16[512,512]{1,0:T(8,128)(2,1)S(1)}, bf16[512,512]{1,0:T(8,128)(2,1)S(1)}, u32[]{:S(2)}, u32[]{:S(2)}) collective-permute-start(bf16[512,512]{1,0:T(8,128)(2,1)S(1)} %copy-done.11), channel_id=1, source_target_pairs={{0,16},{16,0},{32,48},{48,32},{64,80},{80,64},{96,112},{112,96},{1... | collective-permute-start | bytes 1572872 | tf_op jit(solution)/shard_map/ppermute | solution.py:57
  36.9 7.1 %all-to-all-done = bf16[16,64,512]{2,1,0:T(8,128)(2,1)S(1)} async-done(((bf16[16,64,512]{2,1,0:T(8,128)(2,1)}), bf16[16,64,512]{2,1,0:T(8,128)(2,1)S(1)}, u32[]{:S(2)}, u32[]{:S(2)}) %all-to-all-start) | async-done | bytes 1048608 | tf_op jit(solution)/shard_map/all_to_all | solution.py:63
  46.0 11.5 %collective-permute-done.3 = bf16[512,512]{1,0:T(8,128)(2,1)S(1)} collective-permute-done((bf16[512,512]{1,0:T(8,128)(2,1)S(1)}, bf16[512,512]{1,0:T(8,128)(2,1)S(1)}, u32[]{:S(2)}, u32[]{:S(2)}) %collective-permute-start.3) | collective-permute-done | bytes 524320 | tf_op jit(solution)/shard_map/ppermute | solution.py:60
  57.5 5.9 %collective-permute-start.4 = (bf16[512,512]{1,0:T(8,128)(2,1)S(1)}, bf16[512,512]{1,0:T(8,128)(2,1)S(1)}, u32[]{:S(2)}, u32[]{:S(2)}) collective-permute-start(bf16[512,512]{1,0:T(8,128)(2,1)S(1)} %collective-permute-done.3), channel_id=1, source_target_pairs={{0,16},{16,0},{32,48},{48,32},{64,80},{80,64},{96,112},{112,96},{1... | collective-permute-start | bytes 1572872 | tf_op jit(solution)/shard_map/ppermute | solution.py:57
  73.9 5.5 %collective-permute-start.5 = (bf16[64,1024]{1,0:T(8,128)(2,1)}, bf16[64,1024]{1,0:T(8,128)(2,1)}, u32[]{:S(2)}, u32[]{:S(2)}) collective-permute-start(bf16[64,1024]{1,0:T(8,128)(2,1)} %get-tuple-element.59), channel_id=1, source_target_pairs={{0,14},{1,15},{2,0},{3,1},{4,2},{5,3},{6,4},{7,5},{8,6},{9,7},{10,... | collective-permute-start | bytes 393224 | tf_op jit(solution)/shard_map/ppermute | solution.py:60
  79.4 6.9 %collective-permute-done.7 = bf16[64,1024]{1,0:T(8,128)(2,1)S(1)} collective-permute-done((bf16[64,1024]{1,0:T(8,128)(2,1)S(1)}, bf16[64,1024]{1,0:T(8,128)(2,1)S(1)}, u32[]{:S(2)}, u32[]{:S(2)}) %collective-permute-start.7) | collective-permute-done | bytes 131104 | tf_op jit(solution)/shard_map/ppermute | solution.py:60
  89.0 11.2 %collective-permute-done.8 = bf16[64,1024]{1,0:T(8,128)(2,1)S(1)} collective-permute-done((bf16[64,1024]{1,0:T(8,128)(2,1)S(1)}, bf16[64,1024]{1,0:T(8,128)(2,1)S(1)}, u32[]{:S(2)}, u32[]{:S(2)}) %collective-permute-start.8) | collective-permute-done | bytes 131104 | tf_op jit(solution)/shard_map/ppermute | solution.py:60
  105.5 5.5 %collective-permute-start.11 = (bf16[64,1024]{1,0:T(8,128)(2,1)S(1)}, bf16[64,1024]{1,0:T(8,128)(2,1)S(1)}, u32[]{:S(2)}, u32[]{:S(2)}) collective-permute-start(bf16[64,1024]{1,0:T(8,128)(2,1)S(1)} %get-tuple-element.35), channel_id=1, source_target_pairs={{0,14},{1,15},{2,0},{3,1},{4,2},{5,3},{6,4},{7,5},{8,6},{9,7},{10,... | collective-permute-start | bytes 393224 | tf_op jit(solution)/shard_map/ppermute | solution.py:60
  111.0 4.0 %collective-permute-done.9 = bf16[64,1024]{1,0:T(8,128)(2,1)S(1)} collective-permute-done((bf16[64,1024]{1,0:T(8,128)(2,1)}, bf16[64,1024]{1,0:T(8,128)(2,1)S(1)}, u32[]{:S(2)}, u32[]{:S(2)}) %collective-permute-start.9) | collective-permute-done | bytes 131104 | tf_op jit(solution)/shard_map/ppermute | solution.py:60
  115.0 2.6 %collective-permute-done.11 = bf16[64,1024]{1,0:T(8,128)(2,1)S(1)} collective-permute-done((bf16[64,1024]{1,0:T(8,128)(2,1)S(1)}, bf16[64,1024]{1,0:T(8,128)(2,1)S(1)}, u32[]{:S(2)}, u32[]{:S(2)}) %collective-permute-start.11) | collective-permute-done | bytes 131104 | tf_op jit(solution)/shard_map/ppermute | solution.py:60
  117.7 5.6 %collective-permute-start.12 = (bf16[64,1024]{1,0:T(8,128)(2,1)S(1)}, bf16[64,1024]{1,0:T(8,128)(2,1)S(1)}, u32[]{:S(2)}, u32[]{:S(2)}) collective-permute-start(bf16[64,1024]{1,0:T(8,128)(2,1)S(1)} %get-tuple-element.55), channel_id=1, source_target_pairs={{0,14},{1,15},{2,0},{3,1},{4,2},{5,3},{6,4},{7,5},{8,6},{9,7},{10,... | collective-permute-start | bytes 393224 | tf_op jit(solution)/shard_map/ppermute | solution.py:60
  125.3 3.6 %collective-permute-done.12 = bf16[64,1024]{1,0:T(8,128)(2,1)S(1)} collective-permute-done((bf16[64,1024]{1,0:T(8,128)(2,1)S(1)}, bf16[64,1024]{1,0:T(8,128)(2,1)S(1)}, u32[]{:S(2)}, u32[]{:S(2)}) %collective-permute-start.12) | collective-permute-done | bytes 131104 | tf_op jit(solution)/shard_map/ppermute | solution.py:60
  128.9 3.2 %collective-permute-done.10 = bf16[64,1024]{1,0:T(8,128)(2,1)S(1)} collective-permute-done((bf16[64,1024]{1,0:T(8,128)(2,1)S(1)}, bf16[64,1024]{1,0:T(8,128)(2,1)S(1)}, u32[]{:S(2)}, u32[]{:S(2)}) %collective-permute-start.10) | collective-permute-done | bytes 131104 | tf_op jit(solution)/shard_map/ppermute | solution.py:60
  134.4 4.6 %collective-permute-start.14 = (bf16[64,1024]{1,0:T(8,128)(2,1)S(1)}, bf16[64,1024]{1,0:T(8,128)(2,1)S(1)}, u32[]{:S(2)}, u32[]{:S(2)}) collective-permute-start(bf16[64,1024]{1,0:T(8,128)(2,1)S(1)} %get-tuple-element.49), channel_id=1, source_target_pairs={{0,15},{1,0},{2,1},{3,2},{4,3},{5,4},{6,5},{7,6},{8,7},{9,8},{10,9... | collective-permute-start | bytes 393224 | tf_op jit(solution)/shard_map/ppermute | solution.py:60
  141.3 4.6 %collective-permute-start.16 = (bf16[64,1024]{1,0:T(8,128)(2,1)S(1)}, bf16[64,1024]{1,0:T(8,128)(2,1)S(1)}, u32[]{:S(2)}, u32[]{:S(2)}) collective-permute-start(bf16[64,1024]{1,0:T(8,128)(2,1)S(1)} %collective-permute-done.14), channel_id=1, source_target_pairs={{0,15},{1,0},{2,1},{3,2},{4,3},{5,4},{6,5},{7,6},{8,7},{9,8},{10,9... | collective-permute-start | bytes 393224 | tf_op jit(solution)/shard_map/ppermute | solution.py:60
  148.2 4.6 %collective-permute-start.18 = (bf16[64,1024]{1,0:T(8,128)(2,1)S(1)}, bf16[64,1024]{1,0:T(8,128)(2,1)S(1)}, u32[]{:S(2)}, u32[]{:S(2)}) collective-permute-start(bf16[64,1024]{1,0:T(8,128)(2,1)S(1)} %collective-permute-done.16), channel_id=1, source_target_pairs={{0,15},{1,0},{2,1},{3,2},{4,3},{5,4},{6,5},{7,6},{8,7},{9,8},{10,9... | collective-permute-start | bytes 393224 | tf_op jit(solution)/shard_map/ppermute | solution.py:60
  155.5 4.9 %collective-permute-start.20 = (bf16[64,1024]{1,0:T(8,128)(2,1)S(1)}, bf16[64,1024]{1,0:T(8,128)(2,1)S(1)}, u32[]{:S(2)}, u32[]{:S(2)}) collective-permute-start(bf16[64,1024]{1,0:T(8,128)(2,1)S(1)} %collective-permute-done.18), channel_id=1, source_target_pairs={{0,15},{1,0},{2,1},{3,2},{4,3},{5,4},{6,5},{7,6},{8,7},{9,8},{10,9... | collective-permute-start | bytes 393224 | tf_op jit(solution)/shard_map/ppermute | solution.py:60
  163.9 4.7 %collective-permute-start.22 = (bf16[64,1024]{1,0:T(8,128)(2,1)S(1)}, bf16[64,1024]{1,0:T(8,128)(2,1)S(1)}, u32[]{:S(2)}, u32[]{:S(2)}) collective-permute-start(bf16[64,1024]{1,0:T(8,128)(2,1)S(1)} %collective-permute-done.20), channel_id=1, source_target_pairs={{0,15},{1,0},{2,1},{3,2},{4,3},{5,4},{6,5},{7,6},{8,7},{9,8},{10,9... | collective-permute-start | bytes 393224 | tf_op jit(solution)/shard_map/ppermute | solution.py:60
  171.5 4.6 %collective-permute-start.24 = (bf16[64,1024]{1,0:T(8,128)(2,1)S(1)}, bf16[64,1024]{1,0:T(8,128)(2,1)S(1)}, u32[]{:S(2)}, u32[]{:S(2)}) collective-permute-start(bf16[64,1024]{1,0:T(8,128)(2,1)S(1)} %collective-permute-done.22), channel_id=1, source_target_pairs={{0,15},{1,0},{2,1},{3,2},{4,3},{5,4},{6,5},{7,6},{8,7},{9,8},{10,9... | collective-permute-start | bytes 393224 | tf_op jit(solution)/shard_map/ppermute | solution.py:60
  178.4 4.6 %collective-permute-start.26 = (bf16[64,1024]{1,0:T(8,128)(2,1)S(1)}, bf16[64,1024]{1,0:T(8,128)(2,1)S(1)}, u32[]{:S(2)}, u32[]{:S(2)}) collective-permute-start(bf16[64,1024]{1,0:T(8,128)(2,1)S(1)} %collective-permute-done.24), channel_id=1, source_target_pairs={{0,15},{1,0},{2,1},{3,2},{4,3},{5,4},{6,5},{7,6},{8,7},{9,8},{10,9... | collective-permute-start | bytes 393224 | tf_op jit(solution)/shard_map/ppermute | solution.py:60
  197.2 6.8 %all-to-all-start.1 = ((bf16[16,64,512]{2,1,0:T(8,128)(2,1)}), bf16[16,64,512]{2,1,0:T(8,128)(2,1)S(1)}, u32[]{:S(2)}, u32[]{:S(2)}) async-start(bf16[16,64,512]{2,1,0:T(8,128)(2,1)} %bitcast.15), calls=%async_computation.1 | async-start | bytes 2097152 | tf_op jit(solution)/shard_map/all_to_all | solution.py:63
  208.8 12.7 %collective-permute-start.28 = (bf16[1024,512]{1,0:T(8,128)(2,1)}, bf16[1024,512]{1,0:T(8,128)(2,1)}, u32[]{:S(2)}, u32[]{:S(2)}) collective-permute-start(bf16[1024,512]{1,0:T(8,128)(2,1)} %pad_maximum_fusion.3), channel_id=1, source_target_pairs={{0,16},{16,0},{32,48},{48,32},{64,80},{80,64},{96,112},{112,96},{1... | collective-permute-start | bytes 3145736 | tf_op jit(solution)/shard_map/ppermute | solution.py:57
  228.4 3.9 %add_convert_fusion.2 = (bf16[512,512]{1,0:T(8,128)(2,1)}, bf16[512,512]{1,0:T(8,128)(2,1)}) fusion(bf16[1024,512]{1,0:T(8,128)(2,1)} %collective-permute-done.28, f32[512,512]{1,0:T(8,128)} %fusion.12, bf16[1024,1024]{1,0:T(8,128)(2,1)} %copy-done.4, bf16[1024,1024]{1,0:T(8,128)(2,1)} %all-gather.5.cloned.1.call-done), kind=kOutput, calls=%fused_computation.20 | convolution fusion | flops 538443776 | bytes 5242880 | tf_op jit(solution)/shard_map/dot_general | solution.py:165
  (121 shorter events, 73.8 us)
Async XLA Ops:
  11.0 33.0 %all-to-all-start = ((bf16[16,64,512]{2,1,0:T(8,128)(2,1)}), bf16[16,64,512]{2,1,0:T(8,128)(2,1)S(1)}, u32[]{:S(2)}, u32[]{:S(2)}) async-start(bf16[16,64,512]{2,1,0:T(8,128)(2,1)} %bitcast.1), calls=%async_computation | async-start | bytes 2097152 | tf_op jit(solution)/shard_map/all_to_all | solution.py:63
  29.0 157.6 %all-gather.3.cloned.1.call-start = ((), (), s32[]{:S(2)}) async-start(), calls=%async_computation.2 | async-start | bytes 4456448 | tf_op jit(solution)/shard_map/all_gather | solution.py:86
  29.1 7.8 %collective-permute-start.2 = (bf16[512,512]{1,0:T(8,128)(2,1)S(1)}, bf16[512,512]{1,0:T(8,128)(2,1)S(1)}, u32[]{:S(2)}, u32[]{:S(2)}) collective-permute-start(bf16[512,512]{1,0:T(8,128)(2,1)S(1)} %copy-done.11), channel_id=1, source_target_pairs={{0,16},{16,0},{32,48},{48,32},{64,80},{80,64},{96,112},{112,96},{1... | collective-permute-start | bytes 1572872 | tf_op jit(solution)/shard_map/ppermute | solution.py:57
  44.1 160.0 %all-gather.5.cloned.1.call-start = ((), (), s32[]{:S(2)}) async-start(), calls=%async_computation.3 | async-start | bytes 2228224 | tf_op jit(solution)/shard_map/all_gather | solution.py:128
  44.1 13.4 %collective-permute-start.3 = (bf16[512,512]{1,0:T(8,128)(2,1)S(1)}, bf16[512,512]{1,0:T(8,128)(2,1)S(1)}, u32[]{:S(2)}, u32[]{:S(2)}) collective-permute-start(bf16[512,512]{1,0:T(8,128)(2,1)S(1)} %copy-done.11), channel_id=1, source_target_pairs={{0,1},{1,2},{2,3},{3,4},{4,5},{5,6},{6,7},{7,8},{8,9},{9,10},{10,1... | collective-permute-start | bytes 1572872 | tf_op jit(solution)/shard_map/ppermute | solution.py:60
  57.5 9.1 %collective-permute-start.4 = (bf16[512,512]{1,0:T(8,128)(2,1)S(1)}, bf16[512,512]{1,0:T(8,128)(2,1)S(1)}, u32[]{:S(2)}, u32[]{:S(2)}) collective-permute-start(bf16[512,512]{1,0:T(8,128)(2,1)S(1)} %collective-permute-done.3), channel_id=1, source_target_pairs={{0,16},{16,0},{32,48},{48,32},{64,80},{80,64},{96,112},{112,96},{1... | collective-permute-start | bytes 1572872 | tf_op jit(solution)/shard_map/ppermute | solution.py:57
  69.3 34.5 %collective-permute-start.6 = (bf16[1024,512]{1,0:T(8,128)(2,1)S(1)}, bf16[1024,512]{1,0:T(8,128)(2,1)S(1)}, u32[]{:S(2)}, u32[]{:S(2)}) collective-permute-start(bf16[1024,512]{1,0:T(8,128)(2,1)S(1)} %copy-done.3), channel_id=1, source_target_pairs={{0,16},{16,0},{32,48},{48,32},{64,80},{80,64},{96,112},{112,96},{1... | collective-permute-start | bytes 3145736 | tf_op jit(solution)/shard_map/ppermute | solution.py:57
  72.0 14.3 %collective-permute-start.7 = (bf16[64,1024]{1,0:T(8,128)(2,1)S(1)}, bf16[64,1024]{1,0:T(8,128)(2,1)S(1)}, u32[]{:S(2)}, u32[]{:S(2)}) collective-permute-start(bf16[64,1024]{1,0:T(8,128)(2,1)S(1)} %get-tuple-element.58), channel_id=1, source_target_pairs={{0,2},{1,3},{2,4},{3,5},{4,6},{5,7},{6,8},{7,9},{8,10},{9,11},{10,... | collective-permute-start | bytes 393224 | tf_op jit(solution)/shard_map/ppermute | solution.py:60
  73.9 15.1 %collective-permute-start.5 = (bf16[64,1024]{1,0:T(8,128)(2,1)}, bf16[64,1024]{1,0:T(8,128)(2,1)}, u32[]{:S(2)}, u32[]{:S(2)}) collective-permute-start(bf16[64,1024]{1,0:T(8,128)(2,1)} %get-tuple-element.59), channel_id=1, source_target_pairs={{0,14},{1,15},{2,0},{3,1},{4,2},{5,3},{6,4},{7,5},{8,6},{9,7},{10,... | collective-permute-start | bytes 393224 | tf_op jit(solution)/shard_map/ppermute | solution.py:60
  86.3 13.9 %collective-permute-start.8 = (bf16[64,1024]{1,0:T(8,128)(2,1)S(1)}, bf16[64,1024]{1,0:T(8,128)(2,1)S(1)}, u32[]{:S(2)}, u32[]{:S(2)}) collective-permute-start(bf16[64,1024]{1,0:T(8,128)(2,1)S(1)} %add_convert_fusion.8), channel_id=1, source_target_pairs={{0,2},{1,3},{2,4},{3,5},{4,6},{5,7},{6,8},{7,9},{8,10},{9,11},{10,... | collective-permute-start | bytes 393224 | tf_op jit(solution)/shard_map/ppermute | solution.py:60
  101.8 13.1 %collective-permute-start.9 = (bf16[64,1024]{1,0:T(8,128)(2,1)}, bf16[64,1024]{1,0:T(8,128)(2,1)S(1)}, u32[]{:S(2)}, u32[]{:S(2)}) collective-permute-start(bf16[64,1024]{1,0:T(8,128)(2,1)} %get-tuple-element.56), channel_id=1, source_target_pairs={{0,2},{1,3},{2,4},{3,5},{4,6},{5,7},{6,8},{7,9},{8,10},{9,11},{10,... | collective-permute-start | bytes 393224 | tf_op jit(solution)/shard_map/ppermute | solution.py:60
  105.5 12.1 %collective-permute-start.11 = (bf16[64,1024]{1,0:T(8,128)(2,1)S(1)}, bf16[64,1024]{1,0:T(8,128)(2,1)S(1)}, u32[]{:S(2)}, u32[]{:S(2)}) collective-permute-start(bf16[64,1024]{1,0:T(8,128)(2,1)S(1)} %get-tuple-element.35), channel_id=1, source_target_pairs={{0,14},{1,15},{2,0},{3,1},{4,2},{5,3},{6,4},{7,5},{8,6},{9,7},{10,... | collective-permute-start | bytes 393224 | tf_op jit(solution)/shard_map/ppermute | solution.py:60
  117.7 11.2 %collective-permute-start.12 = (bf16[64,1024]{1,0:T(8,128)(2,1)S(1)}, bf16[64,1024]{1,0:T(8,128)(2,1)S(1)}, u32[]{:S(2)}, u32[]{:S(2)}) collective-permute-start(bf16[64,1024]{1,0:T(8,128)(2,1)S(1)} %get-tuple-element.55), channel_id=1, source_target_pairs={{0,14},{1,15},{2,0},{3,1},{4,2},{5,3},{6,4},{7,5},{8,6},{9,7},{10,... | collective-permute-start | bytes 393224 | tf_op jit(solution)/shard_map/ppermute | solution.py:60
  123.3 8.8 %collective-permute-start.10 = (bf16[64,1024]{1,0:T(8,128)(2,1)S(1)}, bf16[64,1024]{1,0:T(8,128)(2,1)S(1)}, u32[]{:S(2)}, u32[]{:S(2)}) collective-permute-start(bf16[64,1024]{1,0:T(8,128)(2,1)S(1)} %get-tuple-element.54), channel_id=1, source_target_pairs={{0,2},{1,3},{2,4},{3,5},{4,6},{5,7},{6,8},{7,9},{8,10},{9,11},{10,... | collective-permute-start | bytes 393224 | tf_op jit(solution)/shard_map/ppermute | solution.py:60
  146.3 7.4 %collective-permute-start.17 = (bf16[64,1024]{1,0:T(8,128)(2,1)S(1)}, bf16[64,1024]{1,0:T(8,128)(2,1)S(1)}, u32[]{:S(2)}, u32[]{:S(2)}) collective-permute-start(bf16[64,1024]{1,0:T(8,128)(2,1)S(1)} %collective-permute-done.15), channel_id=1, source_target_pairs={{0,1},{1,2},{2,3},{3,4},{4,5},{5,6},{6,7},{7,8},{8,9},{9,10},{10,1... | collective-permute-start | bytes 393224 | tf_op jit(solution)/shard_map/ppermute | solution.py:60
  148.2 7.4 %collective-permute-start.18 = (bf16[64,1024]{1,0:T(8,128)(2,1)S(1)}, bf16[64,1024]{1,0:T(8,128)(2,1)S(1)}, u32[]{:S(2)}, u32[]{:S(2)}) collective-permute-start(bf16[64,1024]{1,0:T(8,128)(2,1)S(1)} %collective-permute-done.16), channel_id=1, source_target_pairs={{0,15},{1,0},{2,1},{3,2},{4,3},{5,4},{6,5},{7,6},{8,7},{9,8},{10,9... | collective-permute-start | bytes 393224 | tf_op jit(solution)/shard_map/ppermute | solution.py:60
  153.6 8.4 %collective-permute-start.19 = (bf16[64,1024]{1,0:T(8,128)(2,1)S(1)}, bf16[64,1024]{1,0:T(8,128)(2,1)S(1)}, u32[]{:S(2)}, u32[]{:S(2)}) collective-permute-start(bf16[64,1024]{1,0:T(8,128)(2,1)S(1)} %collective-permute-done.17), channel_id=1, source_target_pairs={{0,1},{1,2},{2,3},{3,4},{4,5},{5,6},{6,7},{7,8},{8,9},{9,10},{10,1... | collective-permute-start | bytes 393224 | tf_op jit(solution)/shard_map/ppermute | solution.py:60
  155.5 8.4 %collective-permute-start.20 = (bf16[64,1024]{1,0:T(8,128)(2,1)S(1)}, bf16[64,1024]{1,0:T(8,128)(2,1)S(1)}, u32[]{:S(2)}, u32[]{:S(2)}) collective-permute-start(bf16[64,1024]{1,0:T(8,128)(2,1)S(1)} %collective-permute-done.18), channel_id=1, source_target_pairs={{0,15},{1,0},{2,1},{3,2},{4,3},{5,4},{6,5},{7,6},{8,7},{9,8},{10,9... | collective-permute-start | bytes 393224 | tf_op jit(solution)/shard_map/ppermute | solution.py:60
  162.0 7.5 %collective-permute-start.21 = (bf16[64,1024]{1,0:T(8,128)(2,1)S(1)}, bf16[64,1024]{1,0:T(8,128)(2,1)S(1)}, u32[]{:S(2)}, u32[]{:S(2)}) collective-permute-start(bf16[64,1024]{1,0:T(8,128)(2,1)S(1)} %collective-permute-done.19), channel_id=1, source_target_pairs={{0,1},{1,2},{2,3},{3,4},{4,5},{5,6},{6,7},{7,8},{8,9},{9,10},{10,1... | collective-permute-start | bytes 393224 | tf_op jit(solution)/shard_map/ppermute | solution.py:60
  163.9 7.5 %collective-permute-start.22 = (bf16[64,1024]{1,0:T(8,128)(2,1)S(1)}, bf16[64,1024]{1,0:T(8,128)(2,1)S(1)}, u32[]{:S(2)}, u32[]{:S(2)}) collective-permute-start(bf16[64,1024]{1,0:T(8,128)(2,1)S(1)} %collective-permute-done.20), channel_id=1, source_target_pairs={{0,15},{1,0},{2,1},{3,2},{4,3},{5,4},{6,5},{7,6},{8,7},{9,8},{10,9... | collective-permute-start | bytes 393224 | tf_op jit(solution)/shard_map/ppermute | solution.py:60
  178.4 6.9 %collective-permute-start.26 = (bf16[64,1024]{1,0:T(8,128)(2,1)S(1)}, bf16[64,1024]{1,0:T(8,128)(2,1)S(1)}, u32[]{:S(2)}, u32[]{:S(2)}) collective-permute-start(bf16[64,1024]{1,0:T(8,128)(2,1)S(1)} %collective-permute-done.24), channel_id=1, source_target_pairs={{0,15},{1,0},{2,1},{3,2},{4,3},{5,4},{6,5},{7,6},{8,7},{9,8},{10,9... | collective-permute-start | bytes 393224 | tf_op jit(solution)/shard_map/ppermute | solution.py:60
  183.4 7.8 %collective-permute-start.27 = (bf16[64,1024]{1,0:T(8,128)(2,1)S(1)}, bf16[64,1024]{1,0:T(8,128)(2,1)S(1)}, u32[]{:S(2)}, u32[]{:S(2)}) collective-permute-start(bf16[64,1024]{1,0:T(8,128)(2,1)S(1)} %collective-permute-done.25), channel_id=1, source_target_pairs={{0,1},{1,2},{2,3},{3,4},{4,5},{5,6},{6,7},{7,8},{8,9},{9,10},{10,1... | collective-permute-start | bytes 393224 | tf_op jit(solution)/shard_map/ppermute | solution.py:60
  197.2 30.4 %all-to-all-start.1 = ((bf16[16,64,512]{2,1,0:T(8,128)(2,1)}), bf16[16,64,512]{2,1,0:T(8,128)(2,1)S(1)}, u32[]{:S(2)}, u32[]{:S(2)}) async-start(bf16[16,64,512]{2,1,0:T(8,128)(2,1)} %bitcast.15), calls=%async_computation.1 | async-start | bytes 2097152 | tf_op jit(solution)/shard_map/all_to_all | solution.py:63
  208.8 19.7 %collective-permute-start.28 = (bf16[1024,512]{1,0:T(8,128)(2,1)}, bf16[1024,512]{1,0:T(8,128)(2,1)}, u32[]{:S(2)}, u32[]{:S(2)}) collective-permute-start(bf16[1024,512]{1,0:T(8,128)(2,1)} %pad_maximum_fusion.3), channel_id=1, source_target_pairs={{0,16},{16,0},{32,48},{48,32},{64,80},{80,64},{96,112},{112,96},{1... | collective-permute-start | bytes 3145736 | tf_op jit(solution)/shard_map/ppermute | solution.py:57
  (25 other events, 149.7 us)
Sparse Core Ops, SparseCore 0:
  44.2 87.9 all-gather.2
  135.7 59.4 all-gather.4
